TPU v7x, 256 devices: a whole 4x4x8 slice. The times are simulated.
256 devices in a mesh: lat: 16 (over z, x_hi), lon: 4 (over x_lo, core), rep: 4 (over y).
Axes of the slice: x: 4 (x_hi: 2, x_lo: 2; x = x_hi * 2 + x_lo), y: 4, z: 8, core: 2. Of those that a mesh axis runs over, the one named last changes fastest.
Arguments:
- fields: bfloat16 [4, 2, 96, 48, 192], P('rep', None, 'lat', 'lon'), may hold values from -6 to 6
- upstream: bfloat16 [4, 2, 96, 48, 192], P('rep', None, 'lat', 'lon'), may hold values from -6 to 6
- scales: float32 [2, 2, 192], replicated, may hold values from 0.5 to 1.5
- offsets: float32 [2, 2, 192], replicated, may hold values from -1.5 to 1.5
- inward: float32 [2, 192, 576], replicated, may hold values from -0.4375 to 0.4375
- inbias: float32 [2, 576], replicated, may hold values from -1.5 to 1.5
- outward: float32 [2, 192, 192], replicated, may hold values from -0.4375 to 0.4375
- outbias: float32 [2, 192], replicated, may hold values from -1.5 to 1.5
- expand: float32 [2, 192, 768], replicated, may hold values from -0.4375 to 0.4375
- upbias: float32 [2, 768], replicated, may hold values from -1.5 to 1.5
- narrow: float32 [2, 768, 192], replicated, may hold values from -0.21875 to 0.21875
- downbias: float32 [2, 192], replicated, may hold values from -1.5 to 1.5
- tables: float32 [2, 16, 6, 3312], replicated, may hold values from -6 to 224
- window_type: int32 [2, 1, 16], replicated, may hold values from 0 to 15, as said below
- row_valid: int32 [96], replicated, may hold values from 0 to 1, as said below
Outputs:
- result: bfloat16 [4, 2, 96, 48, 192], P('rep', None, 'lat', 'lon')
- adjoint: bfloat16 [4, 2, 96, 48, 192], P('rep', None, 'lat', 'lon')
- adjoint_scales: float32 [2, 2, 192], replicated
- adjoint_offsets: float32 [2, 2, 192], replicated
- adjoint_inward: float32 [2, 192, 576], replicated
- adjoint_inbias: float32 [2, 576], replicated
- adjoint_outward: float32 [2, 192, 192], replicated
- adjoint_outbias: float32 [2, 192], replicated
- adjoint_expand: float32 [2, 192, 768], replicated
- adjoint_upbias: float32 [2, 768], replicated
- adjoint_narrow: float32 [2, 768, 192], replicated
- adjoint_downbias: float32 [2, 192], replicated
- adjoint_tables: float32 [2, 16, 6, 3312], replicated
Inputs may be any that keep to these rules, and one draw needn't show every extreme that they name: `row_valid`: in every aligned group of three rows at least one row is 1. `window_type`: for each block, every table number is named by exactly one pair of level window and latitude window.
All inputs are finite; a program needn't handle non-finite values.
Results may differ from a plain program's by a relative error of at most 0.025.
Values may be sent and summed in bfloat16 or wider, within the bound.
No kernel may reach another device: no remote copies, remote signals or barrier semaphores. Data moves between devices by JAX's collectives and lax.ppermute only.
A program may use at most 128 MiB of HBM per device.

v0:
```python
import math

import jax
import jax.numpy as jnp
from jax import lax
from jax.sharding import PartitionSpec as P

epsilon = 1e-05
masked = -1000000000.0


def from_behind(block, axis, distance):
    devices = range(lax.axis_size(axis))
    route = [((i - distance) % len(devices), i) for i in devices]
    return lax.ppermute(block, axis, route)


def layer_norm(values, scale_row, offset_row):
    widened = values.astype(jnp.float32)
    average = jnp.mean(widened, axis=-1, keepdims=True)
    centred = widened - average
    variance = jnp.mean(centred * centred, axis=-1, keepdims=True)
    return (centred * lax.rsqrt(variance + epsilon) * scale_row + offset_row).astype(jnp.bfloat16)


def to_windows(sample):
    levels, row_count, col_count, features = sample.shape
    sample = sample.reshape(levels // 2, 2, row_count // 6, 6, col_count // 12, 12, features)
    sample = sample.transpose(0, 2, 4, 1, 3, 5, 6)
    return sample.reshape(levels // 2, row_count // 6, col_count // 12, 144, features)


def from_windows(blocks):
    level_wins, band_wins, col_wins, tokens, features = blocks.shape
    blocks = blocks.reshape(level_wins, band_wins, col_wins, 2, 6, 12, features)
    blocks = blocks.transpose(0, 3, 1, 4, 2, 5, 6)
    return blocks.reshape(level_wins * 2, band_wins * 6, col_wins * 12, features)


def relative_index():
    tokens = jnp.arange(144, dtype=jnp.int32)
    level_of = tokens // 72
    row_of = tokens // 12 % 6
    col_of = tokens % 12
    pair_rows = (
        (level_of[:, None] * 2 + level_of[None, :]) * 36 + row_of[:, None] * 6 + row_of[None, :]
    )
    return pair_rows * 23 + col_of[:, None] - col_of[None, :] + 11


def window_bias(position_table, type_ids, allowed):
    level_wins, band_wins = type_ids.shape
    type_count, head_count, rel_count = position_table.shape
    choose = (type_ids == jnp.arange(type_count, dtype=jnp.int32)[None, :]).astype(jnp.float32)
    chosen = jnp.dot(
        choose, position_table.reshape(type_count, -1), precision=lax.Precision.HIGHEST
    )
    chosen = chosen.reshape(level_wins * band_wins, head_count, rel_count)
    spread = jnp.take(chosen, relative_index().reshape(-1), axis=2)
    spread = spread.reshape(level_wins, band_wins, head_count, 144, 144)
    return jnp.where(allowed[:, :, None], spread, masked)


def allowed_pairs(level_region, row_region, row_flags):
    levels = level_region.shape[0]
    row_count = row_region.shape[0]
    target = (levels // 2, row_count // 6, 2, 6, 12)
    final = (levels // 2, row_count // 6, 144)
    level_tag = jnp.broadcast_to(level_region.reshape(levels // 2, 1, 2, 1, 1), target).reshape(
        final
    )
    region_tag = jnp.broadcast_to(row_region.reshape(1, row_count // 6, 1, 6, 1), target).reshape(
        final
    )
    valid_tag = jnp.broadcast_to(row_flags.reshape(1, row_count // 6, 1, 6, 1), target).reshape(
        final
    )
    same_level = level_tag[..., :, None] == level_tag[..., None, :]
    same_region = region_tag[..., :, None] == region_tag[..., None, :]
    return same_level & same_region & (valid_tag[..., None, :] > 0)


def attend(normed, inward, inbias, outward, outbias, bias):
    levels, row_count, col_count, features = normed.shape
    head_count = bias.shape[2]
    head_size = features // head_count
    blocks = to_windows(normed)
    leading = blocks.shape[:4]
    packed = (
        jnp.dot(
            blocks.reshape(-1, features),
            inward.astype(jnp.bfloat16),
            preferred_element_type=jnp.float32,
        )
        + inbias
    )
    packed = packed.astype(jnp.bfloat16).reshape(leading + (3, head_count, head_size))
    query_block = packed[..., 0, :, :]
    key_block = packed[..., 1, :, :]
    value_block = packed[..., 2, :, :]
    scores = jnp.einsum(
        "plwihd,plwjhd->plwhij", query_block, key_block, preferred_element_type=jnp.float32
    )
    scores = scores * head_size ** (-0.5) + bias[:, :, None]
    row_max = jnp.max(scores, axis=-1, keepdims=True)
    weights = jnp.exp(scores - row_max)
    chances = (weights / jnp.sum(weights, axis=-1, keepdims=True)).astype(jnp.bfloat16)
    mixture = jnp.einsum(
        "plwhij,plwjhd->plwihd", chances, value_block, preferred_element_type=jnp.float32
    )
    mixture = mixture.astype(jnp.bfloat16).reshape(-1, features)
    projected = (
        jnp.dot(mixture, outward.astype(jnp.bfloat16), preferred_element_type=jnp.float32) + outbias
    )
    return from_windows(projected.astype(jnp.bfloat16).reshape(leading + (features,)))


def feed_forward(carried, scale_row, offset_row, expand, upbias, narrow, downbias):
    features = carried.shape[-1]
    normed = layer_norm(carried, scale_row, offset_row).reshape(-1, features)
    hidden = (
        jnp.dot(normed, expand.astype(jnp.bfloat16), preferred_element_type=jnp.float32) + upbias
    )
    hidden = jax.nn.gelu(hidden, approximate=False).astype(jnp.bfloat16)
    output = (
        jnp.dot(hidden, narrow.astype(jnp.bfloat16), preferred_element_type=jnp.float32) + downbias
    )
    return (carried.astype(jnp.float32) + output.reshape(carried.shape)).astype(jnp.bfloat16)


def first_block(sample, params, allowed, type_ids):
    (
        scale_set,
        offset_set,
        inward,
        inbias,
        outward,
        outbias,
        expand,
        upbias,
        narrow,
        downbias,
        position_table,
    ) = params
    bias = window_bias(position_table, type_ids, allowed)
    branch = attend(
        layer_norm(sample, scale_set[0], offset_set[0]), inward, inbias, outward, outbias, bias
    )
    carried = (sample.astype(jnp.float32) + branch.astype(jnp.float32)).astype(jnp.bfloat16)
    return feed_forward(carried, scale_set[1], offset_set[1], expand, upbias, narrow, downbias)


def shifted_attention(rolled, params, allowed, type_ids):
    inward, inbias, outward, outbias, position_table = params
    bias = window_bias(position_table, type_ids, allowed)
    leveled = jnp.roll(rolled, -1, axis=0)
    return jnp.roll(attend(leveled, inward, inbias, outward, outbias, bias), 1, axis=0)


def second_tail(carried, restored, params):
    scale_set, offset_set, expand, upbias, narrow, downbias = params
    merged = (carried.astype(jnp.float32) + restored.astype(jnp.float32)).astype(jnp.bfloat16)
    return feed_forward(merged, scale_set[1], offset_set[1], expand, upbias, narrow, downbias)


def roll_forward(normed):
    upper_rows = from_behind(normed[:, :3], "lat", -1)
    shifted = jnp.concatenate([normed[:, 3:], upper_rows], axis=1)
    leftmost = from_behind(shifted[:, :, :6], "lon", -1)
    return jnp.concatenate([shifted[:, :, 6:], leftmost], axis=2)


def roll_back(branch):
    rightmost = from_behind(branch[:, :, -6:], "lon", 1)
    shifted = jnp.concatenate([rightmost, branch[:, :, :-6]], axis=2)
    lowest = from_behind(shifted[:, -3:], "lat", 1)
    return jnp.concatenate([lowest, shifted[:, :-3]], axis=1)


def flatten(members):
    return jnp.concatenate([member.reshape(-1) for member in members])


def unflatten(vector, members):
    pieces = []
    offset_at = 0
    for member in members:
        pieces.append(vector[offset_at : offset_at + member.size].reshape(member.shape))
        offset_at = offset_at + member.size
    return pieces


def body(
    fields,
    upstream,
    scales,
    offsets,
    inward,
    inbias,
    outward,
    outbias,
    expand,
    upbias,
    narrow,
    downbias,
    tables,
    window_type,
    row_valid,
):
    stacked = (
        scales,
        offsets,
        inward,
        inbias,
        outward,
        outbias,
        expand,
        upbias,
        narrow,
        downbias,
        tables,
    )
    first_params = tuple((member[0] for member in stacked))
    second_params = tuple((member[1] for member in stacked))
    sample = fields[0]
    cotangent = upstream[0]
    levels, row_count, col_count, features = sample.shape
    band_index = lax.axis_index("lat")
    total_rows = row_count * lax.axis_size("lat")
    global_rows = band_index * row_count + jnp.arange(row_count, dtype=jnp.int32)
    own_flags = lax.dynamic_slice_in_dim(row_valid, band_index * row_count, row_count)
    level_order = jnp.arange(levels, dtype=jnp.int32)
    allowed_plain = allowed_pairs(
        jnp.zeros((levels,), jnp.int32), jnp.zeros((row_count,), jnp.int32), own_flags
    )
    allowed_shift = allowed_pairs(
        (level_order == levels - 1).astype(jnp.int32),
        (global_rows >= total_rows - 3).astype(jnp.int32),
        jnp.take(row_valid, (global_rows + 3) % total_rows),
    )
    types_plain = lax.dynamic_slice_in_dim(window_type[0], band_index, 1, 1)
    types_shift = lax.dynamic_slice_in_dim(window_type[1], band_index, 1, 1)

    def block_one(sample_in, *params):
        return first_block(sample_in, params, allowed_plain, types_plain)

    def norm_two(carried, scale_set, offset_set):
        return layer_norm(carried, scale_set[0], offset_set[0])

    def attention_two(rolled_in, *params):
        return shifted_attention(rolled_in, params, allowed_shift, types_shift)

    def tail_two(carried, restored, *params):
        return second_tail(carried, restored, params)

    attention_params = second_params[2:6] + (second_params[10],)
    first_out, pull_first = jax.vjp(block_one, sample, *first_params)
    normed, pull_norm = jax.vjp(norm_two, first_out, second_params[0], second_params[1])
    rolled = roll_forward(normed)
    branch = attention_two(rolled, *attention_params)
    restored = roll_back(branch)
    result, pull_tail = jax.vjp(
        tail_two, first_out, restored, *second_params[:2] + second_params[6:10]
    )
    tail_adjoints = pull_tail(cotangent)
    branch_adjoint = roll_forward(tail_adjoints[1])
    rolled_again = roll_forward(normed)
    attention_adjoints = jax.vjp(attention_two, rolled_again, *attention_params)[1](branch_adjoint)
    second_terms = (
        tail_adjoints[2],
        tail_adjoints[3],
        attention_adjoints[1],
        attention_adjoints[2],
        attention_adjoints[3],
        attention_adjoints[4],
        tail_adjoints[4],
        tail_adjoints[5],
        tail_adjoints[6],
        tail_adjoints[7],
        attention_adjoints[5],
    )
    second_flat = flatten(second_terms)
    normed_adjoint = roll_back(attention_adjoints[0])
    norm_adjoints = pull_norm(normed_adjoint)
    state_adjoint = tail_adjoints[0] + norm_adjoints[0]
    first_adjoints = pull_first(state_adjoint)
    first_terms = tuple(first_adjoints[1:]) + (norm_adjoints[1], norm_adjoints[2])
    first_flat = flatten(first_terms)
    both_summed = lax.psum(jnp.concatenate([second_flat, first_flat]), ("lat", "lon", "rep"))
    second_summed = both_summed[: second_flat.shape[0]]
    first_summed = both_summed[second_flat.shape[0] :]
    second_list = unflatten(second_summed, second_terms)
    first_list = unflatten(first_summed, first_terms)
    second_list[0] = second_list[0] + first_list[11]
    second_list[1] = second_list[1] + first_list[12]
    factor = 1.0 / math.sqrt(
        lax.axis_size("rep") * levels * total_rows * col_count * lax.axis_size("lon")
    )
    joined = [jnp.stack([first_list[i], second_list[i]]) * factor for i in range(11)]
    return (
        result[None],
        first_adjoints[0][None],
        joined[0],
        joined[1],
        joined[2],
        joined[3],
        joined[4],
        joined[5],
        joined[6],
        joined[7],
        joined[8],
        joined[9],
        joined[10],
    )


def solution(mesh):
    placed = (
        P("rep", None, "lat", "lon", None),
        P("rep", None, "lat", "lon", None),
        P(),
        P(),
        P(),
        P(),
        P(),
        P(),
        P(),
        P(),
        P(),
        P(),
        P(),
        P(),
        P(),
    )
    return jax.shard_map(
        body,
        mesh=mesh,
        in_specs=placed,
        out_specs=(
            P("rep", None, "lat", "lon", None),
            P("rep", None, "lat", "lon", None),
            P(),
            P(),
            P(),
            P(),
            P(),
            P(),
            P(),
            P(),
            P(),
            P(),
            P(),
        ),
        check_vma=False,
    )
```

profile of v0, /device:TPU:1, one launch (start us, length us, event | category | flops | bytes accessed | tf_op | source)
XLA Modules:
  0.0 968.4 jit_solution(5922768661940319278)
XLA Ops:
  10.3 1.4 slice_reduce_fusion.1
  11.7 2.1 convert.40
  18.0 1.5 fusion.4
  22.6 2.1 copy.68
  24.7 1.6 reshape_squeeze.7
  26.3 2.2 reshape.1703
  28.4 2.2 fusion.6
  30.6 1.4 copy.106
  32.0 39.1 %gather_fusion.3 = f32[20736,6]{1,0:T(8,128)} fusion(f32[6,3312]{0,1:T(8,128)S(1)} %bitcast.293, s32[21504]{0:T(1024)S(1)} %pad_clamp_fusion.1), kind=kCustom, calls=%fused_computation.1.clone | custom fusion | bytes 1078272 | tf_op jit(solution)/shard_map/jvp(jit(_take))/gather | solution.py:59
  71.1 38.9 %gather_fusion.2 = f32[20736,6]{1,0:T(8,128)} fusion(f32[6,3312]{0,1:T(8,128)S(1)} %bitcast.297, s32[21504]{0:T(1024)S(1)} %pad_clamp_fusion.1), kind=kCustom, calls=%fused_computation.clone | custom fusion | bytes 1078272 | tf_op jit(solution)/shard_map/jvp(jit(_take))/gather | solution.py:59
  110.0 16.1 %bitcast_select_fusion = (f32[1,6,20736]{1,2,0:T(8,128)}, f32[1,6,20736]{1,2,0:T(8,128)}) fusion(f32[20736,6]{1,0:T(8,128)} %gather_fusion.3, pred[20736]{0:T(1024)(128)(4,1)S(1)} %compare_and_fusion.1, f32[20736,6]{1,0:T(8,128)} %gather_fusion.2), kind=kLoop, calls=%fused_computation.7 | loop fusion | flops 248832 | bytes 2011392 | tf_op jit(solution)/shard_map/jvp(jit(_take))/select_n | solution.py:59
  126.1 12.2 %copy.70 = f32[6,144,144]{1,2,0:T(8,128)} copy(f32[6,144,144]{0,2,1:T(8,128)} %bitcast.296) | data formatting | bytes 995328 | tf_op jit(solution)/shard_map/jvp()/reshape | solution.py:60
  140.1 1.3 convert.39
  142.5 1.6 fusion.237
  149.2 3.1 multiply_convert_fusion.1
  157.3 8.9 collective-permute-start
  166.1 1.7 reshape.1789
  167.9 1.5 compare_and_fusion
  171.0 1.7 reshape.1791
  178.1 1.7 broadcast_reduce_fusion
  179.8 1.7 broadcast_reduce_fusion.1
  181.6 1.5 and_and_fusion
  183.0 1.6 convert_reduce_fusion.11
  186.2 1.7 eq.190
  187.8 1.3 eq.177
  189.2 1.7 eq.191
  190.9 1.7 eq.186
  192.5 1.3 eq.173
  193.9 1.7 eq.187
  195.6 1.7 and_and_fusion.1
  198.4 1.5 fusion.161
  203.5 43.0 %gather_fusion.1 = f32[20736,6]{1,0:T(8,128)} fusion(f32[6,3312]{0,1:T(8,128)S(1)} %bitcast.294, s32[21504]{0:T(1024)} %pad_clamp_fusion), kind=kCustom, calls=%fused_computation.3 | custom fusion | bytes 1078272 | tf_op jit(solution)/shard_map/jit(_take)/gather | solution.py:59
  246.6 12.1 %copy.77 = f32[6,144,144]{1,2,0:T(8,128)} copy(f32[6,144,144]{0,2,1:T(8,128)} %bitcast.298) | data formatting | bytes 995328 | tf_op jit(solution)/shard_map/jit(_take)/gather | solution.py:59
  259.0 12.1 %copy.84 = f32[6,144,144]{1,2,0:T(8,128)} copy(f32[6,144,144]{0,2,1:T(8,128)} %bitcast.295) | data formatting | bytes 995328 | tf_op jit(solution)/shard_map/jvp()/reshape | solution.py:60
  272.7 2.6 fusion.210
  275.3 1.7 fusion.238
  277.0 1.9 convolution_convert_fusion.17
  282.1 5.9 collective-permute-done.3
  288.5 2.9 multiply_convert_fusion
  295.7 1.3 fusion.13
  297.1 3.1 collective-permute-done.4
  300.8 4.0 collective-permute-start.5
  308.1 1.4 copy.93
  309.5 1.2 reshape.1773
  311.5 1.4 convert_reduce_fusion.7
  321.2 6.1 copy.95
  327.4 112.8 %scatter_custom_fusion = f32[6,3312]{0,1:T(8,128)S(1)} fusion(s32[20736]{0:T(1024)} %copy-done.90, f32[20736,6]{1,0:T(8,128)} %copy.95, f32[]{:T(128)} %constant.119.clone.1), kind=kCustom, calls=%fused_computation.100 | custom fusion | flops 124416 | bytes 80000 | tf_op jit(solution)/shard_map/transpose(jvp(jit(_take)))/scatter-add | solution.py:59
  442.8 2.1 reshape.1767
  446.4 1.8 reshape.1736
  448.2 1.7 collective-permute-done.7
  451.9 2.3 fusion.240
  467.0 1.7 reshape.1777
  471.7 6.1 copy.99
  477.9 113.1 %scatter_custom_fusion.1 = f32[6,3312]{0,1:T(8,128)S(1)} fusion(s32[20736]{0:T(1024)} %copy-done.90, f32[20736,6]{1,0:T(8,128)} %copy.99, f32[]{:T(128)} %constant.119.clone.1), kind=kCustom, calls=%fused_computation.98 | custom fusion | flops 124416 | bytes 80000 | tf_op jit(solution)/shard_map/transpose(jvp(jit(_take)))/scatter-add | solution.py:59
  593.5 1.8 reshape.1748
  595.6 63.6 %concatenate.82 = f32[1526400]{0:T(1024)} concatenate(f32[384]{0:T(512)S(1)} %copy-done.173, f32[384]{0:T(512)S(1)} %copy-done.174, f32[110592]{0:T(1024)} %reshape.1767, f32[576]{0:T(1024)S(1)} %copy-done.155, f32[36864]{0:T(1024)} %reshape.1769, f32[192]{0:T(256)S(1)} %copy-done.181, f32[147456]{0:T(1024)S(1)} %copy-done.19, f32[768]{0:T(1024)S(1)} %copy-done.178, ...), dimensions={0} | concatenate | bytes 12211200 | tf_op jit(solution)/shard_map/concatenate | solution.py:289
  663.7 265.0 %all-reduce.20.cloned.1.call-done = f32[1526400]{0:T(1024)} async-done(((f32[1526400]{0:T(1024)}), f32[1526400]{0:T(1024)}) %all-reduce.20.cloned.1.call-update) | async-done | bytes 6105616 | tf_op jit(solution)/shard_map/psum | solution.py:289
  929.9 1.3 fusion.222
  936.6 2.8 fusion.218
  942.6 1.5 copy.103
  944.1 3.2 fusion.216
  947.3 1.2 stack_reshape.47
  948.5 2.5 stack_reshape.46
  951.5 2.2 copy.104
  (688 shorter events, 103.6 us)
Async XLA Ops:
  7.2 6.7 copy-start.16
  7.2 921.5 %all-reduce.20.cloned.1.call-start = ((), (), s32[]{:S(2)}) async-start(), calls=%async_computation | async-start | bytes 12214272 | tf_op jit(solution)/shard_map/psum | solution.py:289
  8.2 6.9 copy-start.45
  8.4 14.2 %copy-start.90 = (s32[20736]{0:T(1024)}, s32[20736]{0:T(1024)S(1)}, u32[]{:S(2)}) copy-start(s32[20736]{0:T(1024)S(1)} %compare_select_fusion.2) | copy-start | bytes 248836
  126.1 12.2 %copy-start = (s32[96]{0:T(128)S(1)}, s32[96]{0:T(128)}, u32[]{:S(2)}) copy-start(s32[96]{0:T(128)} %param.31) | copy-start | bytes 1156
  126.1 13.6 %copy-start.2 = (bf16[1,2,6,12,192]{4,1,3,2,0:T(2,128)(2,1)S(1)}, bf16[1,2,6,12,192]{4,1,3,2,0:T(2,128)(2,1)}, u32[]{:S(2)}) copy-start(bf16[1,2,6,12,192]{4,1,3,2,0:T(2,128)(2,1)} %param.17) | copy-start | bytes 165892
  126.1 13.8 %copy-start.142 = (f32[1,1,192]{2,1,0:T(1,128)S(1)}, f32[1,1,192]{2,1,0:T(1,128)}, u32[]{:S(2)}) copy-start(f32[1,1,192]{2,1,0:T(1,128)} %get-tuple-element.138) | copy-start | bytes 2308
  126.1 13.8 %copy-start.198 = (f32[1,1,192]{2,1,0:T(1,128)S(1)}, f32[1,1,192]{2,1,0:T(1,128)}, u32[]{:S(2)}) copy-start(f32[1,1,192]{2,1,0:T(1,128)} %get-tuple-element.142) | copy-start | bytes 2308
  139.7 4.5 copy-start.176
  141.4 130.7 %copy-start.3 = (bf16[2,192,576]{2,1,0:T(8,128)(2,1)}, bf16[2,192,576]{2,1,0:T(8,128)(2,1)S(1)}, u32[]{:S(2)}) copy-start(bf16[2,192,576]{2,1,0:T(8,128)(2,1)S(1)} %convert.39) | copy-start | bytes 1327108
  146.4 5.9 copy-start.48
  146.4 6.0 copy-start.33
  148.1 146.6 %copy-start.17 = (bf16[2,6,12,192]{3,2,1,0:T(8,128)(2,1)}, bf16[2,6,12,192]{3,2,1,0:T(8,128)(2,1)S(1)}, u32[]{:S(2)}) copy-start(bf16[2,6,12,192]{3,2,1,0:T(8,128)(2,1)S(1)} %get-tuple-element.76) | copy-start | bytes 165892
  152.4 18.1 %copy-start.93 = (f32[6,144]{1,0:T(8,128)S(1)}, f32[6,144]{1,0:T(8,128)}, u32[]{:S(2)}) copy-start(f32[6,144]{1,0:T(8,128)} %copy-done.92) | copy-start | bytes 10372
  153.3 134.8 %copy-start.14 = (bf16[144,192]{1,0:T(8,128)(2,1)}, bf16[144,192]{1,0:T(8,128)(2,1)S(1)}, u32[]{:S(2)}) copy-start(bf16[144,192]{1,0:T(8,128)(2,1)S(1)} %get-tuple-element.72) | copy-start | bytes 165892
  153.4 31.2 %copy-start.114 = (f32[2,6,12]{2,1,0:T(8,128)}, f32[2,6,12]{2,1,0:T(8,128)S(1)}, u32[]{:S(2)}) copy-start(f32[2,6,12]{2,1,0:T(8,128)S(1)} %div.233) | copy-start | bytes 1732
  154.8 29.8 %copy-start.116 = (f32[2,6,12]{2,1,0:T(8,128)}, f32[2,6,12]{2,1,0:T(8,128)S(1)}, u32[]{:S(2)}) copy-start(f32[2,6,12]{2,1,0:T(8,128)S(1)} %rsqrt.58) | copy-start | bytes 1732
  155.7 41.5 %copy-start.36 = (f32[2,6,12,192]{3,2,1,0:T(8,128)}, f32[2,6,12,192]{3,2,1,0:T(8,128)S(1)}, u32[]{:S(2)}) copy-start(f32[2,6,12,192]{3,2,1,0:T(8,128)S(1)} %reshape.1707) | copy-start | bytes 331780
  157.3 41.2 %collective-permute-start = (bf16[2,3,12,192]{3,2,1,0:T(8,128)(2,1)}, bf16[2,3,12,192]{3,2,1,0:T(8,128)(2,1)}, u32[]{:S(2)}, u32[]{:S(2)}) collective-permute-start(bf16[2,3,12,192]{3,2,1,0:T(8,128)(2,1)} %get-tuple-element.121), channel_id=1, source_target_pairs={{16,0},{32,16},{48,32},{64,48},{80,64},{96,80},{112,96},{128,112},... | collective-permute-start | bytes 82952 | tf_op jit(solution)/shard_map/ppermute | solution.py:15
  199.9 72.1 %collective-permute-start.1 = (bf16[2,6,6,192]{3,2,1,0:T(8,128)(2,1)}, bf16[2,6,6,192]{3,2,1,0:T(8,128)(2,1)S(1)}, u32[]{:S(2)}, u32[]{:S(2)}) collective-permute-start(bf16[2,6,6,192]{3,2,1,0:T(8,128)(2,1)} %get-tuple-element.119), channel_id=1, source_target_pairs={{4,0},{8,4},{12,8},{0,12},{5,1},{9,5},{13,9},{1,13},{6,2},{10,6},{... | collective-permute-start | bytes 82952 | tf_op jit(solution)/shard_map/ppermute | solution.py:15
  246.6 12.2 %copy-start.98 = (pred[144,144]{1,0:T(8,128)(4,1)S(1)}, pred[144,144]{1,0:T(8,128)(4,1)}, u32[]{:S(2)}) copy-start(pred[144,144]{1,0:T(8,128)(4,1)} %compare_and_fusion) | copy-start | bytes 62212
  246.6 12.3 %copy-start.99 = (pred[144,144]{1,0:T(8,128)(4,1)S(1)}, pred[144,144]{1,0:T(8,128)(4,1)}, u32[]{:S(2)}) copy-start(pred[144,144]{1,0:T(8,128)(4,1)} %and_and_fusion) | copy-start | bytes 62212
  259.0 12.2 %copy-start.177 = (pred[144]{0:T(512)(128)(4,1)S(1)}, pred[144]{0:T(512)(128)(4,1)}, u32[]{:S(2)}) copy-start(pred[144]{0:T(512)(128)(4,1)} %copy-done.176) | copy-start | bytes 436
  259.0 13.1 %copy-start.154 = (f32[576]{0:T(1024)S(1)}, f32[576]{0:T(1024)}, u32[]{:S(2)}) copy-start(f32[576]{0:T(1024)} %get-tuple-element.49) | copy-start | bytes 6916
  271.2 33.6 %copy-start.74 = (bf16[144,192]{1,0:T(8,128)(2,1)}, bf16[144,192]{1,0:T(8,128)(2,1)S(1)}, u32[]{:S(2)}) copy-start(bf16[144,192]{1,0:T(8,128)(2,1)S(1)} %reshape.1715) | copy-start | bytes 165892
  272.7 40.6 %copy-start.12 = (bf16[144,576]{0,1:T(8,128)(2,1)}, bf16[144,576]{0,1:T(8,128)(2,1)S(1)}, u32[]{:S(2)}) copy-start(bf16[144,576]{0,1:T(8,128)(2,1)S(1)} %copy.72) | copy-start | bytes 497668
  278.9 9.6 copy-start.127
  279.0 9.5 copy-start.197
  279.0 9.5 copy-start.199
  279.3 2.0 collective-permute-start.2
  281.4 13.3 %copy-start.50 = (bf16[2,3,12,192]{3,2,1,0:T(8,128)(2,1)}, bf16[2,3,12,192]{3,2,1,0:T(8,128)(2,1)S(1)}, u32[]{:S(2)}) copy-start(bf16[2,3,12,192]{3,2,1,0:T(8,128)(2,1)S(1)} %get-tuple-element.115) | copy-start | bytes 82948
  281.4 6.6 collective-permute-start.3
  288.0 6.7 copy-start.70
  288.2 7.5 copy-start.31
  288.3 5.0 copy-start.137
  288.5 4.8 copy-start.149
  293.1 11.8 %copy-start.59 = (bf16[144,768]{1,0:T(8,128)(2,1)S(1)}, bf16[144,768]{1,0:T(8,128)(2,1)}, u32[]{:S(2)}) copy-start(bf16[144,768]{1,0:T(8,128)(2,1)} %get-tuple-element.67) | copy-start | bytes 663556
  293.2 12.7 %copy-start.104 = (f32[2,6,12]{2,1,0:T(8,128)}, f32[2,6,12]{2,1,0:T(8,128)S(1)}, u32[]{:S(2)}) copy-start(f32[2,6,12]{2,1,0:T(8,128)S(1)} %div.239) | copy-start | bytes 1732
  294.7 11.3 %copy-start.188 = (f32[192]{0:T(256)S(1)}, f32[192]{0:T(256)}, u32[]{:S(2)}) copy-start(f32[192]{0:T(256)} %get-tuple-element.40) | copy-start | bytes 2308
  295.6 11.0 %copy-start.187 = (f32[192]{0:T(256)S(1)}, f32[192]{0:T(256)}, u32[]{:S(2)}) copy-start(f32[192]{0:T(256)} %get-tuple-element.46) | copy-start | bytes 2308
  295.6 4.5 collective-permute-start.4
  300.8 9.9 %collective-permute-start.5 = (bf16[2,6,6,192]{3,2,1,0:T(8,128)(2,1)}, bf16[2,6,6,192]{3,2,1,0:T(8,128)(2,1)}, u32[]{:S(2)}, u32[]{:S(2)}) collective-permute-start(bf16[2,6,6,192]{3,2,1,0:T(8,128)(2,1)} %get-tuple-element.111), channel_id=1, source_target_pairs={{4,0},{8,4},{12,8},{0,12},{5,1},{9,5},{13,9},{1,13},{6,2},{10,6},{... | collective-permute-start | bytes 82952 | tf_op jit(solution)/shard_map/ppermute | solution.py:15
  308.1 4.8 copy-start.40
  308.1 5.1 copy-start.140
  319.7 122.6 %collective-permute-start.6 = (bf16[2,6,6,192]{3,2,1,0:T(8,128)(2,1)}, bf16[2,6,6,192]{3,2,1,0:T(8,128)(2,1)S(1)}, u32[]{:S(2)}, u32[]{:S(2)}) collective-permute-start(bf16[2,6,6,192]{3,2,1,0:T(8,128)(2,1)} %get-tuple-element.108), channel_id=1, source_target_pairs={{12,0},{0,4},{4,8},{8,12},{13,1},{1,5},{5,9},{9,13},{14,2},{2,6},{... | collective-permute-start | bytes 82952 | tf_op jit(solution)/shard_map/ppermute | solution.py:15
  327.4 113.5 %copy-start.207 = (f32[16]{0:T(128)S(1)}, f32[16]{0:T(128)}, u32[]{:S(2)}) copy-start(f32[16]{0:T(128)} %bitcast_convert_fusion) | copy-start | bytes 196
  442.3 7.5 copy-start.67
  442.4 7.5 collective-permute-start.7
  445.5 4.4 copy-start.133
  445.6 4.4 copy-start.136
  446.4 4.6 copy-start.25
  446.4 4.6 copy-start.32
  446.4 4.6 copy-start.75
  446.4 4.6 copy-start.128
  446.4 4.6 copy-start.138
  446.4 4.6 copy-start.150
  446.4 4.6 copy-start.157
  446.4 4.6 copy-start.161
  451.9 4.9 copy-start.41
  460.1 4.8 copy-start.27
  464.8 4.8 copy-start.23
  477.9 114.3 %copy-start.206 = (f32[16]{0:T(128)S(1)}, f32[16]{0:T(128)}, u32[]{:S(2)}) copy-start(f32[16]{0:T(128)} %bitcast_convert_fusion.1) | copy-start | bytes 196
  953.8 5.0 copy-start.21
  953.8 5.0 copy-start.22
  (153 other events, 350.2 us)
Sparse Core Ops, SparseCore 0:
  659.3 269.3 all-reduce.19
where the time goes:
time: 981 us; the launch traced here: 968 us
  local copies, waits for them, and re-layouts  333 us (34%)
  other arithmetic  291 us (30%)
  waiting for transfers between devices  277 us (28%)
  matrix products  33.8 us (3%)
  between operations  17.6 us (2%)
  starting transfers between devices  16 us (2%)
    psum x1, waiting for transfers between devices, body(): lax.psum(jnp.concatenate([second_flat, first_flat]), ('lat', 'lon', 'rep'))  265 us
    scatter-add x2, other arithmetic, window_bias(): spread = jnp.take(chosen, relative_index().reshape(-1), axis=2)  226 us
    gather x4, local copies, waits for them, and re-layouts, window_bias(): spread = jnp.take(chosen, relative_index().reshape(-1), axis=2)  133 us
    concatenate x1, local copies, waits for them, and re-layouts, body(): jnp.concatenate([second_flat, first_flat])  63.6 us
    reshape x2, local copies, waits for them, and re-layouts, window_bias(): spread = spread.reshape(level_wins, band_wins, head_count, 144, 144)  24.3 us
  transfers between devices with their start and end apart: 9, of which 5 were waited for; matrix products, arithmetic and copies ran while one was open for 25% of the time, Pallas kernels for 0%

commit v1 on v0

v1 whole, which is shorter than its diff:
```python
import math

import jax
import jax.numpy as jnp
import numpy as np
from jax import lax
from jax.experimental import pallas as pl
from jax.experimental.pallas import tpu as pltpu
from jax.sharding import PartitionSpec as P

C = 192
HEADS = 6
FFN = 768
TOK = 144
KEYS = 256
QUAD = 48
REL = 3312
ROWS = 144
CHUNK = ROWS + 16
epsilon = 1e-05
masked = -1000000000.0
f32 = jnp.float32
bf16 = jnp.bfloat16
VMEM = 48 * 1024 * 1024


def constants():
    tok = np.arange(TOK)
    a, r, c = tok // 72, tok // 12 % 6, tok % 12
    turn = np.zeros((TOK, TOK), np.float32)
    turn[tok, (r * 12 + c) * 2 + a] = 1
    quad = np.where(r >= 3, 0, 1) + np.where(c >= 6, 0, 2)
    cut = np.zeros((4 * QUAD, TOK), np.float32)
    cut[quad * QUAD + a * 18 + r % 3 * 6 + c % 6, tok] = 1
    quad = np.where(r < 3, 0, 1) + np.where(c < 6, 0, 2)
    join = np.zeros((TOK, 4 * QUAD), np.float32)
    join[tok, quad * QUAD + (1 - a) * 18 + r % 3 * 6 + c % 6] = 1
    spread = np.zeros((256, 12 * 128), np.float32)
    for ci in range(12):
        for rj in range(6):
            for cj in range(12):
                spread[rj * 23 + ci - cj + 11, ci * 128 + rj * 12 + cj] = 1
    place = np.zeros((TOK, 192), np.float32)
    place[tok, c * 16 + a * 6 + r] = 1
    sort = np.zeros((192, 192), np.float32)
    for ai in range(2):
        for aj in range(2):
            for ri in range(6):
                for h in range(HEADS):
                    sort[(h * 2 + aj) * 16 + ai * 6 + ri, ((ai * 2 + aj) * 6 + ri) * 8 + h] = 1
    made = {"turn": turn, "cut": cut, "join": join, "place": place, "sort": sort}
    made = {name: jnp.asarray(m, f32) for name, m in made.items()}
    made["spread"] = jnp.asarray(spread, bf16)
    return made


def low(ref):
    return ref[...].astype(bf16)


def dot(x, y, dims=((1,), (0,))):
    return lax.dot_general(x, y, (dims, ((), ())), preferred_element_type=f32)


def dot_nt(x, y):
    return dot(x, y, ((1,), (1,)))


def dot_tn(x, y):
    return dot(x, y, ((0,), (0,)))


def norm_parts(values):
    centred = values - jnp.mean(values, axis=-1, keepdims=True)
    rstd = lax.rsqrt(jnp.mean(centred * centred, axis=-1, keepdims=True) + epsilon)
    return centred * rstd, rstd


def norm_fwd(values, gain, shift):
    return (norm_parts(values)[0] * gain + shift).astype(bf16)


def norm_bwd(values, gain, dy):
    hat, rstd = norm_parts(values)
    dhat = dy * gain
    first = jnp.mean(dhat, axis=-1, keepdims=True)
    second = jnp.mean(dhat * hat, axis=-1, keepdims=True)
    return rstd * (dhat - first - hat * second), colsum(dy * hat), colsum(dy)


def colsum(x):
    return jnp.sum(x, axis=0, keepdims=True)


def erf(x):
    return lax.erf(x)


def gelu_parts(z):
    cdf = 0.5 * (1.0 + erf(z * (2.0 ** -0.5)))
    return cdf, z * cdf


def pad_keys(x):
    blank = jnp.zeros((56, x.shape[1]), f32)
    return jnp.concatenate([x[:72], blank, x[72:], blank], axis=0)


def unpad_keys(x):
    return jnp.concatenate([x[:72], x[128:200]], axis=0)


def head_only(x, h):
    lane = lax.broadcasted_iota(jnp.int32, x.shape, 1)
    return jnp.where((lane >= 32 * h) & (lane < 32 * h + 32), x.astype(f32), 0.0).astype(bf16)


def join_rows(refs):
    return jnp.concatenate([ref[...] for ref in refs], axis=0)


def write_pieces(pieces, refs):
    for i, ref in enumerate(refs):
        ref[...] = pieces[i * QUAD : (i + 1) * QUAD].astype(bf16)


def key_mask(valid, band, shift):
    lane = lax.broadcasted_iota(jnp.int32, (1, KEYS), 1)
    column = lane & 127
    total_rows = valid.shape[0]
    last = jnp.where(band == total_rows // 6 - 1, 1, 0)
    allowed = jnp.zeros((1, KEYS), jnp.int32)
    for r in range(6):
        at = band * 6 + r + shift
        at = jnp.where(at >= total_rows, at - total_rows, at)
        hit = (column >= 12 * r) & (column < 12 * r + 12)
        allowed = allowed + jnp.where(hit, valid[at], 0)
    if shift:
        row = lax.broadcasted_iota(jnp.int32, (TOK, KEYS), 0)
        wide = lax.broadcasted_iota(jnp.int32, (TOK, KEYS), 1)
        row_level = jnp.where(row >= 72, 1, 0)
        key_level = wide >> 7
        row_part = jnp.where(row - 72 * row_level >= 36, 1, 0)
        key_part = jnp.where((wide & 127) >= 36, 1, 0)
        apart = (row_level ^ key_level) | ((row_part ^ key_part) & last)
        allowed = jnp.where(apart == 0, jnp.broadcast_to(allowed, (TOK, KEYS)), 0)
        column = wide & 127
    mask = jnp.where(allowed > 0, 0.0, masked)
    return jnp.where(column < 72, mask, 2 * masked)


def make_bias(k, where, types, valid, tables, spread, place, sort, bias_ref, turn_ref, row_ref):
    row_ref[...] = jnp.zeros(row_ref.shape, f32)
    kind = types[k, where[0]]
    for h in range(HEADS):
        row_ref[h : h + 1, :REL] = tables[0, h, pl.ds(kind, 1), :]
    wide_rows = row_ref[...]
    rest = jnp.concatenate([wide_rows[:, 138 * i : 138 * i + 256] for i in range(24)], axis=0)
    total = None
    for _ in range(3):
        part = rest.astype(bf16)
        rest = rest - part.astype(f32)
        wide = dot(dot(sort, part).astype(bf16), spread)
        for g in range(12):
            for ci in range(12):
                turn_ref[ci * 16 : ci * 16 + 16, g * 128 : g * 128 + 128] = wide[
                    g * 16 : g * 16 + 16, ci * 128 : ci * 128 + 128
                ].astype(bf16)
        here = dot(place, turn_ref[...])
        total = here if total is None else total + here
    mask = key_mask(valid, where[0], 3 * k)
    for h in range(HEADS):
        bias_ref[:, h * KEYS : (h + 1) * KEYS] = total[:, h * KEYS : (h + 1) * KEYS] + mask


def table_adjoint(dbias, spread, place, sort, turn_ref):
    rows = dot_tn(place, dbias)
    for g in range(12):
        for ci in range(12):
            turn_ref[g * 16 : g * 16 + 16, ci * 128 : ci * 128 + 128] = rows[
                ci * 16 : ci * 16 + 16, g * 128 : g * 128 + 128
            ].astype(bf16)
    narrow = dot_nt(turn_ref[...], spread).astype(bf16)
    rows = dot_tn(sort, narrow)
    pieces = [rows[8 * i : 8 * i + 8, :138] for i in range(24)]
    return jnp.concatenate(pieces + [jnp.zeros((8, 16), f32)], axis=1)


def put(pack, at, value):
    done = 0
    while done < value.shape[0]:
        chunk, row = divmod(at + done, ROWS)
        size = min(ROWS - row, value.shape[0] - done)
        pack[chunk, row : row + size] = value[done : done + size].astype(bf16)
        done += size


def put_rest(pack, table, small):
    row = lax.broadcasted_iota(jnp.int32, (8, 2 * C), 0)
    for chunk in range(8):
        own = table[:, 384 * chunk : 384 * chunk + 384]
        if chunk < 2:
            left = table[:, 3072 + 128 * chunk : 3200 + 128 * chunk]
            moved = [pltpu.roll(left, 6 - 2 * i, 0) if i < 3 else left for i in range(3)]
            own = jnp.where(row >= 6, jnp.concatenate(moved, axis=1), own)
        short = jnp.where(row == 0, small[chunk], 0.0) if chunk < len(small) else jnp.zeros((8, 2 * C), f32)
        pack[chunk, ROWS : ROWS + 16] = jnp.concatenate([own, short], axis=0).astype(bf16)


def attend_fwd(k, u, inward, inbias, outward, outbias, bias_ref, q_ref, k_ref, v_ref, p_ref, mix_ref):
    weight = inward[0].astype(bf16)
    shift = inbias[k : k + 1]
    keyed = pad_keys(u.astype(f32)).astype(bf16)
    q = (dot(u, weight[:, :C]) + shift[:, :C]).astype(bf16)
    key = (dot(keyed, weight[:, C : 2 * C]) + shift[:, C : 2 * C]).astype(bf16)
    v = (dot(keyed, weight[:, 2 * C :]) + shift[:, 2 * C :]).astype(bf16)
    q_ref[...] = q
    k_ref[...] = key
    v_ref[...] = v
    mix = jnp.zeros((TOK, C), f32)
    for h in range(HEADS):
        scores = dot_nt(head_only(q, h), key) * 32 ** (-0.5) + bias_ref[:, h * KEYS : (h + 1) * KEYS]
        weights = jnp.exp(scores - jnp.max(scores, axis=-1, keepdims=True))
        chances = (weights / jnp.sum(weights, axis=-1, keepdims=True)).astype(bf16)
        p_ref[h] = chances
        mix = mix + dot(chances, head_only(v, h))
    mix = mix.astype(bf16)
    mix_ref[...] = mix
    return (dot(mix, outward[0].astype(bf16)) + outbias[k : k + 1]).astype(bf16)


def attend_bwd(dout, u, inward, outward, spread, place, sort, q_ref, k_ref, v_ref, p_ref, mix_ref, pack, dbias_ref, turn_ref):
    q, key, v, mix = q_ref[...], k_ref[...], v_ref[...], mix_ref[...]
    weight = inward[0].astype(bf16)
    dmix = dot_nt(dout, outward[0].astype(bf16)).astype(bf16)
    dq = jnp.zeros((TOK, C), f32)
    dk = jnp.zeros((KEYS, C), f32)
    dv = jnp.zeros((KEYS, C), f32)
    for h in range(HEADS):
        chances = p_ref[h]
        wide = chances.astype(f32)
        dmix_h = head_only(dmix, h)
        dchances = dot_nt(dmix_h, v)
        dscores = wide * (dchances - jnp.sum(wide * dchances, axis=-1, keepdims=True))
        narrow = dscores.astype(bf16)
        dbias_ref[:, h * KEYS : (h + 1) * KEYS] = narrow
        dv = dv + dot_tn(chances, dmix_h)
        dq = dq + dot(narrow, head_only(key, h))
        dk = dk + dot_tn(narrow, head_only(q, h))
    dq = (dq * 32 ** (-0.5)).astype(bf16)
    dk = (dk * 32 ** (-0.5)).astype(bf16)
    dv = dv.astype(bf16)
    keyed = pad_keys(u.astype(f32)).astype(bf16)
    du = dot_nt(dq, weight[:, :C]) + unpad_keys(
        dot_nt(dk, weight[:, C : 2 * C]) + dot_nt(dv, weight[:, 2 * C :])
    )
    pair = lambda x, y: jnp.concatenate([x, y], axis=1)
    put(pack, 4 * C, pair(dot_tn(u, dq), dot_tn(keyed, dk)))
    put(pack, 5 * C, pair(dot_tn(keyed, dv), dot_tn(mix, dout)))
    small = [
        pair(colsum(dq.astype(f32)), colsum(dk.astype(f32))),
        pair(colsum(dv.astype(f32)), colsum(dout.astype(f32))),
    ]
    return du, table_adjoint(dbias_ref[...], spread, place, sort, turn_ref), small


def mlp_fwd(h, gain, shift, expand, upbias, narrow_t, downbias):
    z = dot(norm_fwd(h, gain, shift), expand) + upbias
    hidden = gelu_parts(z)[1].astype(bf16)
    return (h + dot_nt(hidden, narrow_t) + downbias).astype(bf16)


def mlp_both(h, gain, shift, expand, upbias, narrow_t, downbias, dout, want):
    normed = norm_fwd(h, gain, shift)
    z = dot(normed, expand) + upbias
    cdf, wide = gelu_parts(z)
    hidden = wide.astype(bf16)
    result = None
    if want:
        result = (h + dot_nt(hidden, narrow_t) + downbias).astype(bf16)
    slope = cdf + z * jnp.exp(-0.5 * z * z) * (1.0 / math.sqrt(2.0 * math.pi))
    dz32 = dot(dout, narrow_t) * slope
    dz = dz32.astype(bf16)
    dnormed = dot_nt(dz, expand).astype(bf16).astype(f32)
    dx, dgain, dshift = norm_bwd(h, gain, dnormed)
    dwide = dout.astype(f32)
    dh = (dwide + dx).astype(bf16)
    dexpand = dot_tn(normed, dz)
    dnarrow = dot_tn(dout, hidden)
    dense = [dexpand[:, : 2 * C], dexpand[:, 2 * C :], dnarrow[:, : 2 * C], dnarrow[:, 2 * C :]]
    dup = colsum(dz32)
    small = [
        dup[:, : 2 * C],
        dup[:, 2 * C :],
        jnp.concatenate([colsum(dwide), dgain], axis=1),
        jnp.concatenate([dshift, jnp.zeros((1, C), f32)], axis=1),
    ]
    return result, dh, dense, small


def bias_kernel(where, types, valid, tables, spread, place, sort, bias_ref, turned, rows):
    make_bias(1, where, types, valid, tables, spread[...], low(place), low(sort), bias_ref, turned, rows)


def first_kernel(
    where, types, valid, fields, scales, offsets, inward, inbias, outward, outbias, expand, upbias, narrow, downbias,
    tables, turn, cut, spread, place, sort,
    q, k, v, p, mix, h1, y1, pa, pb, pc, pd, bias, turned, rows,
):
    make_bias(0, where, types, valid, tables, spread[...], low(place), low(sort), bias, turned, rows)
    x = dot(low(turn), fields[...])
    u = norm_fwd(x, scales[0, 0:1], offsets[0, 0:1])
    branch = attend_fwd(0, u, inward, inbias, outward, outbias, bias, q, k, v, p, mix)
    carried = (x + branch.astype(f32)).astype(bf16)
    h1[...] = carried
    out = mlp_fwd(
        carried.astype(f32), scales[0, 1:2], offsets[0, 1:2], expand[0].astype(bf16), upbias[0:1],
        narrow[0].astype(bf16), downbias[0:1],
    )
    y1[...] = out
    normed = norm_fwd(out.astype(f32), scales[1, 0:1], offsets[1, 0:1])
    write_pieces(dot(low(cut), normed), (pa, pb, pc, pd))


def second_kernel(
    qa, qb, qc, qd, inward, inbias, outward, outbias, bias, join,
    u_ref, q, k, v, p, mix, pa, pb, pc, pd,
):
    route = low(join)
    u = dot(route, join_rows((qa, qb, qc, qd))).astype(bf16)
    u_ref[...] = u
    branch = attend_fwd(1, u, inward, inbias, outward, outbias, bias, q, k, v, p, mix)
    write_pieces(dot_tn(route, branch), (pa, pb, pc, pd))


def tail_kernel(
    qa, qb, qc, qd, y1, upstream, scales, offsets, expand, upbias, narrow, downbias, turn, cut,
    result, dh_ref, dense_ref, small_ref, pa, pb, pc, pd,
):
    route = low(cut)
    order = low(turn)
    restored = dot_tn(route, join_rows((qa, qb, qc, qd)))
    h2 = (y1[...].astype(f32) + restored).astype(bf16).astype(f32)
    out, dh, dense, small = mlp_both(
        h2, scales[1, 1:2], offsets[1, 1:2], expand[0].astype(bf16), upbias[1:2],
        narrow[0].astype(bf16), downbias[1:2], dot(order, upstream[...]).astype(bf16), True,
    )
    result[...] = dot_tn(order, out).astype(bf16)
    dh_ref[...] = dh
    for i, part in enumerate(dense):
        dense_ref[i * C : (i + 1) * C] = part.astype(bf16)
    for i, row in enumerate(small):
        small_ref[i : i + 1] = row
    write_pieces(dot(route, dh), (pa, pb, pc, pd))


def second_back_kernel(
    qa, qb, qc, qd, dense, short, u, inward, outward, q, k, v, p, mix, join, spread, place, sort,
    pack, pa, pb, pc, pd, dbias, turned,
):
    route = low(join)
    dout = dot(route, join_rows((qa, qb, qc, qd))).astype(bf16)
    du, table, small = attend_bwd(
        dout, u[...], inward, outward, spread[...], low(place), low(sort), q, k, v, p, mix, pack, dbias, turned
    )
    put(pack, 0, dense[...])
    put_rest(pack, table, [short[i : i + 1] for i in range(4)] + small)
    write_pieces(dot_tn(route, du.astype(bf16)), (pa, pb, pc, pd))


def first_back_kernel(
    qa, qb, qc, qd, fields, dh2, y1, h1, scales, offsets, inward, outward, expand, upbias, narrow, downbias,
    q, k, v, p, mix, turn, cut, spread, place, sort,
    adjoint, pack, dbias, turned,
):
    order = low(turn)
    dn = dot_tn(low(cut), join_rows((qa, qb, qc, qd)))
    dx, dgain, dshift = norm_bwd(y1[...].astype(f32), scales[1, 0:1], dn)
    dy1 = (dh2[...].astype(f32) + dx.astype(bf16).astype(f32)).astype(bf16)
    _, dh1, dense, short = mlp_both(
        h1[...].astype(f32), scales[0, 1:2], offsets[0, 1:2], expand[0].astype(bf16), upbias[0:1],
        narrow[0].astype(bf16), downbias[0:1], dy1, False,
    )
    for i, part in enumerate(dense):
        put(pack, i * C, part)
    x = dot(order, fields[...])
    u = norm_fwd(x, scales[0, 0:1], offsets[0, 0:1])
    du, table, small = attend_bwd(
        dh1, u, inward, outward, spread[...], low(place), low(sort), q, k, v, p, mix, pack, dbias, turned
    )
    dx0, dgain0, dshift0 = norm_bwd(x, scales[0, 0:1], du.astype(bf16).astype(f32))
    adjoint[...] = dot_tn(order, (dh1.astype(f32) + dx0).astype(bf16)).astype(bf16)
    pair = lambda x, y: jnp.concatenate([x, y], axis=1)
    put_rest(pack, table, short + small + [pair(dgain0, dshift0), pair(dgain, dshift)])


def core_kernel(where, first, second, got_first, got_second, *outs):
    def deal(own, got):
        for d, out in enumerate(outs):
            at = (where[3] ^ d) * 2
            out[...] = (own[pl.ds(at, 2)].astype(f32) + got[pl.ds(at, 2)].astype(f32)).astype(bf16)

    @pl.when(where[1] == 0)
    def _():
        deal(first, got_first)

    @pl.when(where[1] != 0)
    def _():
        deal(second, got_second)


def samples_kernel(where, a, b, c, d, keep, send):
    for out, at in ((keep, where[2]), (send, where[2] ^ 1)):
        total = a[at].astype(f32) + b[at].astype(f32) + c[at].astype(f32) + d[at].astype(f32)
        out[...] = total.astype(bf16)


def pair_kernel(a, b, out):
    out[...] = (a[...].astype(f32) + b[...].astype(f32)).astype(bf16)


def band_kernel(a, b, c, d, out):
    four = [ref[...].astype(f32) for ref in (a, b, c, d)]
    total = four[0] + four[1] + four[2] + four[3]
    out[:ROWS] = total[:ROWS].astype(bf16)
    if a.shape[0] == CHUNK:
        aside = jnp.concatenate([total[ROWS + 8 :], jnp.zeros((8, 2 * C), f32)], axis=0)
        out[ROWS:CHUNK] = aside.astype(bf16)
        out[CHUNK:] = jnp.concatenate([m[ROWS : ROWS + 8] for m in four], axis=0).astype(bf16)
    else:
        out[ROWS:CHUNK] = total[ROWS:CHUNK].astype(bf16)
        for i, ref in enumerate((a, b, c, d)):
            out[CHUNK + 32 * i : CHUNK + 32 * i + 32] = ref[CHUNK:]


def final_kernel(
    where, types, own, got,
    scales, offsets, inward, inbias, outward, outbias, expand, upbias, narrow, downbias, tables, dense, *, factor
):
    def routes(k):
        lane = lax.broadcasted_iota(jnp.int32, (1, 128), 1)
        kind = jnp.zeros((1, 128), jnp.int32)
        for e in range(16):
            kind = kind + jnp.where((lane >> 3) == e, types[k, where[0] ^ e], 0)
        row = lax.broadcasted_iota(jnp.int32, (96, 128), 0)
        part = lax.broadcasted_iota(jnp.int32, (96, 128), 1) & 7
        head, match = row >> 4, (row & 15) == kind
        made = [match & (part == head)]
        for i in range(3):
            made.append(match & ((head >> 1) == i) & (part == 6 + (head & 1)))
        return [jnp.where(m, 1.0, 0.0).astype(bf16) for m in made]

    def unpack(k, ref):
        route = routes(k)
        left = None
        small = []
        for chunk in range(8):
            at = (where[3] ^ (chunk // 2), where[2] ^ (chunk % 2))
            dense[chunk * ROWS : (chunk + 1) * ROWS] = ref[at[0], at[1], :ROWS]
            small.append(ref[at[0], at[1], ROWS:CHUNK].astype(f32)[0:1] * factor)
            here = ref[at[0], at[1], CHUNK:]
            rows = dot(route[0], here) * factor
            for h in range(HEADS):
                tables[k, h, :, 384 * chunk : 384 * chunk + 384] = rows[16 * h : 16 * h + 16]
            if chunk < 2:
                left = sum(dot(route[1 + i], here[:, 128 * i : 128 * i + 128]) for i in range(3)) * factor
                start = 3072 + 128 * chunk
                size = min(128, REL - start)
                for h in range(HEADS):
                    tables[k, h, :, start : start + size] = left[16 * h : 16 * h + 16, :size]
        load = lambda i: dense[i * C : (i + 1) * C].astype(f32) * factor
        expand[k, :, : 2 * C] = load(0)
        expand[k, :, 2 * C :] = load(1)
        narrow[k, :, : 2 * C] = load(2)
        narrow[k, :, 2 * C :] = load(3)
        inward[k, :, : 2 * C] = load(4)
        both = load(5)
        inward[k, :, 2 * C :] = both[:, :C]
        outward[k] = both[:, C:]
        upbias[k : k + 1, : 2 * C] = small[0]
        upbias[k : k + 1, 2 * C :] = small[1]
        downbias[k : k + 1] = small[2][:, :C]
        scales[k, 1:2] = small[2][:, C:]
        offsets[k, 1:2] = small[3][:, :C]
        inbias[k : k + 1, : 2 * C] = small[4]
        inbias[k : k + 1, 2 * C :] = small[5][:, :C]
        outbias[k : k + 1] = small[5][:, C:]
        if k == 0:
            for i in range(2):
                scales[i, 0:1] = small[6 + i][:, :C]
                offsets[i, 0:1] = small[6 + i][:, C:]

    @pl.when(where[1] == 0)
    def _():
        unpack(0, own)
        unpack(1, got)

    @pl.when(where[1] != 0)
    def _():
        unpack(0, got)
        unpack(1, own)


def call(kernel, ins, outs, scratch=(), flops=0):
    specs = []
    for array, block in ins:
        dims = array.ndim
        if block == "smem":
            specs.append(pl.BlockSpec(memory_space=pltpu.SMEM))
        elif block is None:
            specs.append(pl.BlockSpec(array.shape, lambda i, dims=dims: (0,) * dims))
        else:
            specs.append(
                pl.BlockSpec((1,) + array.shape[1:], lambda i, dims=dims, block=block: (block,) + (0,) * (dims - 1))
            )
    size = lambda s: math.prod(s.shape) * jnp.dtype(s.dtype).itemsize
    moved = sum(size(o) for o in outs) + sum(size(a) // (1 if b in (None, "smem") else a.shape[0]) for a, b in ins)
    return pl.pallas_call(
        kernel,
        grid=(1,),
        in_specs=specs,
        out_specs=[pl.BlockSpec(o.shape, lambda i, dims=len(o.shape): (0,) * dims) for o in outs],
        out_shape=outs,
        scratch_shapes=list(scratch),
        compiler_params=pltpu.CompilerParams(vmem_limit_bytes=VMEM),
        cost_estimate=pl.CostEstimate(flops=flops, bytes_accessed=moved, transcendentals=0),
    )(*[array for array, _ in ins])


def send_pieces(pieces, step):
    lat, lon = lax.axis_size("lat"), lax.axis_size("lon")
    rows = [(i, (i + step) % lat) for i in range(lat)]
    cols = [(i, (i + step) % lon) for i in range(lon)]
    both = [(i * lon + j, (i + step) % lat * lon + (j + step) % lon) for i in range(lat) for j in range(lon)]
    return (
        pieces[0],
        lax.ppermute(pieces[1], "lat", rows),
        lax.ppermute(pieces[2], "lon", cols),
        lax.ppermute(pieces[3], ("lat", "lon"), both),
    )


def swap(array, axis, distance, only=None):
    devices = range(lax.axis_size(axis))
    return lax.ppermute(array, axis, [(i, i ^ distance) for i in devices if only is None or i % 2 == only])


def body(
    fields, upstream, scales, offsets, inward, inbias, outward, outbias, expand, upbias, narrow, downbias,
    tables, window_type, row_valid,
):
    lon = lax.axis_index("lon")
    where = jnp.stack([lax.axis_index("lat"), lon % 2, lon // 2, lax.axis_index("rep")]).astype(jnp.int32)
    const = constants()
    types = window_type[:, 0, :]
    levels, row_count, col_count = fields.shape[1:4]
    total_rows = row_valid.shape[0]
    x = fields[0].transpose(1, 2, 0, 3).reshape(TOK, C)
    cotangent = upstream[0].transpose(1, 2, 0, 3).reshape(TOK, C)
    narrow = jnp.swapaxes(narrow, 1, 2)
    tables = jnp.swapaxes(tables, 1, 2)
    of = jax.ShapeDtypeStruct
    piece = [of((QUAD, C), bf16)] * 4
    token = of((TOK, C), bf16)
    state = [token, of((KEYS, C), bf16), of((KEYS, C), bf16), of((HEADS, TOK, KEYS), bf16), token]
    pack = of((8, CHUNK, 2 * C), bf16)
    turned = pltpu.VMEM((192, 1536), bf16)
    dbias = pltpu.VMEM((TOK, 1536), bf16)
    rows = pltpu.VMEM((8, 3456), f32)
    whole = lambda *arrays: [(m, None) for m in arrays]
    fixed = lambda *names: [(const[name], None) for name in names]
    scalars = [(where, "smem"), (types, "smem"), (row_valid, "smem")]

    *state0, h1, y1, pa, pb, pc, pd = call(
        first_kernel,
        scalars
        + whole(x, scales, offsets)
        + [(inward, 0)] + whole(inbias) + [(outward, 0)] + whole(outbias)
        + [(expand, 0)] + whole(upbias) + [(narrow, 0)] + whole(downbias)
        + [(tables, 0)]
        + fixed("turn", "cut", "spread", "place", "sort"),
        state + [token, token] + piece,
        (pltpu.VMEM((TOK, 1536), f32), turned, rows),
        10**9,
    )
    pieces = send_pieces((pa, pb, pc, pd), -1)
    (bias1,) = call(
        bias_kernel,
        scalars + [(tables, 1)] + fixed("spread", "place", "sort"),
        [of((TOK, 1536), f32)],
        (turned, rows),
        10**9,
    )
    u1, *rest = call(
        second_kernel,
        whole(*pieces) + [(inward, 1)] + whole(inbias) + [(outward, 1)] + whole(outbias, bias1) + fixed("join"),
        [token] + state + piece,
        (),
        10**9,
    )
    state1, pieces = rest[:5], send_pieces(rest[5:], 1)
    result, dh2, dense1, small1, *pieces = call(
        tail_kernel,
        whole(*pieces, y1, cotangent, scales, offsets)
        + [(expand, 1)] + whole(upbias) + [(narrow, 1)] + whole(downbias)
        + fixed("turn", "cut"),
        [token, token, of((4 * C, 2 * C), bf16), of((8, 2 * C), f32)] + piece,
        (),
        10**9,
    )
    pieces = send_pieces(pieces, -1)
    pack1, *pieces = call(
        second_back_kernel,
        whole(*pieces, dense1, small1, u1) + [(inward, 1), (outward, 1)] + whole(*state1)
        + fixed("join", "spread", "place", "sort"),
        [pack] + piece,
        (dbias, turned),
        10**9,
    )
    pieces = send_pieces(pieces, 1)
    got1 = swap(pack1, "lon", 1, 0)
    adjoint, pack0 = call(
        first_back_kernel,
        whole(*pieces, x, dh2, y1, h1, scales, offsets) + [(inward, 0), (outward, 0), (expand, 0)] + whole(upbias)
        + [(narrow, 0)] + whole(downbias, *state0) + fixed("turn", "cut", "spread", "place", "sort"),
        [token, pack],
        (dbias, turned),
        10**9,
    )
    got0 = swap(pack0, "lon", 1, 1)

    part = of((2, CHUNK, 2 * C), bf16)
    a, b, c, d = call(core_kernel, scalars[:1] + whole(pack0, pack1, got0, got1), [part] * 4)
    b, c, d = (swap(m, "rep", i + 1) for i, m in enumerate((b, c, d)))
    chunk = of((CHUNK, 2 * C), bf16)
    keep, give = call(samples_kernel, scalars[:1] + whole(a, b, c, d), [chunk, chunk])
    (a,) = call(pair_kernel, whole(keep, swap(give, "lon", 2)), [chunk])
    for step, height in ((1, CHUNK + 32), (4, CHUNK + 128)):
        others = [swap(a, "lat", step * i) for i in (1, 2, 3)]
        (a,) = call(band_kernel, whole(a, *others), [of((height, 2 * C), bf16)])
    a = jnp.stack([a, swap(a, "lon", 2)])
    a = jnp.stack([a] + [swap(a, "rep", i) for i in (1, 2, 3)])
    got = swap(a, "lon", 1)

    factor = 1.0 / math.sqrt(lax.axis_size("rep") * levels * total_rows * col_count * lax.axis_size("lon"))

    def finish(*refs):
        final_kernel(*refs, factor=factor)

    outs = [
        (2, 2, C), (2, 2, C), (2, C, 3 * C), (2, 3 * C), (2, C, C), (2, C), (2, C, FFN), (2, FFN), (2, C, FFN),
        (2, C), tables.shape,
    ]
    joined = list(
        call(
            finish,
            scalars[:2] + whole(a, got),
            [of(s, f32) for s in outs],
            (pltpu.VMEM((8 * ROWS, 2 * C), bf16),),
        )
    )
    joined[8] = jnp.swapaxes(joined[8], 1, 2)
    joined[10] = jnp.swapaxes(joined[10], 1, 2)
    back = lambda m: m.reshape(row_count, col_count, levels, C).transpose(2, 0, 1, 3)[None]
    return (back(result), back(adjoint), *joined)


def solution(mesh):
    grid = P("rep", None, "lat", "lon", None)
    return jax.shard_map(
        body, mesh=mesh, in_specs=(grid, grid) + (P(),) * 13, out_specs=(grid, grid) + (P(),) * 11, check_vma=False
    )
```

time: 981 us -> 181 us (0.18); the launches traced: 968 us -> 180 us
  local copies, waits for them, and re-layouts: 333 us -> 32.4 us
  other arithmetic: 291 us -> 0.43 us
  waiting for transfers between devices: 277 us -> 73.5 us
  matrix products: 33.8 us -> 0 us
  starting transfers between devices: 16 us -> 44.8 us
  Pallas kernels: 0 us -> 27.7 us
  between operations: 17.6 us -> 1.35 us
    psum x1 -> x0, waiting for transfers between devices: 265 us -> none  [body(): lax.psum(jnp.concatenate([second_flat, first_flat]), ('lat', 'lon', 'rep'))]
    scatter-add x2 -> x0, other arithmetic: 226 us -> none  [window_bias(): spread = jnp.take(chosen, relative_index().reshape(-1), axis=2)]
    gather x5 -> x0, local copies, waits for them, and re-layouts: 134 us -> none  [the longest x4 133 us: window_bias(): spread = jnp.take(chosen, relative_index().reshape(-1), axis=2)]
    concatenate x2 -> x0, local copies, waits for them, and re-layouts: 63.6 us -> none  [the longest x1 63.6 us: body(): jnp.concatenate([second_flat, first_flat])]
    ppermute x8 -> x29, waiting for transfers between devices: 11.8 us -> 73.5 us  [the longest x17 60.6 us: swap(): lax.ppermute(array, axis, [(i, i ^ distance) for i in devices if only is...]
    reshape x25 -> x4, local copies, waits for them, and re-layouts: 41.9 us -> 5.66 us  [the longest x2 3.12 us: body(): m.reshape(row_count, col_count, levels, C).transpose(2, 0, 1, 3)[None]]
    dot_general x39 -> x0, matrix products: 32.1 us -> none  [the longest x6 8.27 us: feed_forward(): jnp.dot(normed, expand.astype(jnp.bfloat16), preferred_element_type=jnp.f...]
    ppermute x8 -> x29, starting transfers between devices: 16 us -> 44.8 us  [the longest x17 22.6 us: swap(): lax.ppermute(array, axis, [(i, i ^ distance) for i in devices if only is...]
  transfers between devices with their start and end apart: 9 -> 29, of which waited for: 5 -> 21; matrix products, arithmetic and copies ran while one was open for 25% -> 3% of each run, Pallas kernels for 0% -> 4%
where the time goes in v1:
time: 181 us; the launch traced here: 180 us
  waiting for transfers between devices  73.5 us (41%)
  starting transfers between devices  44.8 us (25%)
  local copies, waits for them, and re-layouts  32.4 us (18%)
  Pallas kernels  27.7 us (15%)
    ppermute x17, waiting for transfers between devices, swap(): lax.ppermute(array, axis, [(i, i ^ distance) for i in devices if only is...  60.6 us
    pallas_call x12, Pallas kernels, call(): pl.pallas_call(kernel, grid=(1,), in_specs=specs, out_specs=[pl.BlockSpec...  27.7 us
    unnamed x146, local copies, waits for them, and re-layouts  26.7 us
    ppermute x17, starting transfers between devices, swap(): lax.ppermute(array, axis, [(i, i ^ distance) for i in devices if only is...  22.6 us
    ppermute x4, starting transfers between devices, send_pieces(): lax.ppermute(pieces[1], 'lat', rows)  13.1 us
    ppermute x4, waiting for transfers between devices, send_pieces(): lax.ppermute(pieces[3], ('lat', 'lon'), both)  6.96 us
    ppermute x4, waiting for transfers between devices, send_pieces(): lax.ppermute(pieces[1], 'lat', rows)  5.72 us
    ppermute x4, starting transfers between devices, send_pieces(): lax.ppermute(pieces[3], ('lat', 'lon'), both)  4.83 us
  transfers between devices with their start and end apart: 29, of which 21 were waited for; matrix products, arithmetic and copies ran while one was open for 3% of the time, Pallas kernels for 4%

profile of v1, /device:TPU:1, one launch (start us, length us, event | category | flops | bytes accessed | tf_op | source)
XLA Modules:
  0.0 180.1 jit_solution(14112572605576976764)
XLA Ops:
  0.7 1.0 reshape.38.fields
  1.7 1.1 copy-done
  2.9 1.2 copy-done.3
  4.1 1.3 copy-done.5
  5.3 1.0 copy-done.8
  6.3 0.9 copy-done.10
  7.3 0.9 copy-done.12
  8.2 0.9 copy-done.15
  9.1 0.9 copy-done.20
  10.0 0.7 copy-done.55
  15.5 6.7 %shard_map.300 = (bf16[144,192]{1,0:T(8,128)(2,1)S(1)}, bf16[256,192]{1,0:T(8,128)(2,1)S(1)}, bf16[256,192]{1,0:T(8,128)(2,1)S(1)}, bf16[6,144,256]{2,1,0:T(8,12...) custom-call(s32[4]{0:T(128)S(1)} %pad_add_fusion.where.refs_0_, ...), custom_call_target="tpu_custom_call" | custom-call | flops 1000000000 | bytes 5288976 | tf_op jit(solution)/shard_map/pallas_call | solution.py:518
  22.2 8.9 %collective-permute-start = (bf16[48,192]{1,0:T(8,128)(2,1)S(1)}, bf16[48,192]{1,0:T(8,128)(2,1)S(1)}, u32[]{:S(2)}, u32[]{:S(2)}) collective-permute-start(bf16[48,192]{1,0:T(8,128)(2,1)S(1)} %get-tuple-element.67), channel_id=1, source_target_pairs={{0,240},{16,0},{32,16},{48,32},{64,48},{80,64},{96,80},{112,96},{1... | collective-permute-start | bytes 55304 | tf_op jit(solution)/shard_map/ppermute | solution.py:537
  31.2 0.9 collective-permute-start.1
  32.1 1.4 collective-permute-start.2
  33.5 2.4 %shard_map.301.bias = f32[144,1536]{1,0:T(8,128)S(1)} custom-call(s32[4]{0:T(128)S(1)} %pad_add_fusion.where.refs_0_, s32[2,16]{1,0:T(2,128)S(1)} %bitcast.35, s32[96]{0:T(128)S(1)} %copy-done.69, f32[2,6,16,3312]{3,2,1,0:T(8,128)S(1)} %bitcast.29, bf16[256,1536]{1,0:T(8,128)(2,1)S(1)} %copy-done.1, f32[144,192]{1,0:T(8,128)S(1)} %copy-done.13, ...), custom_call_target="tpu_custom_call" | custom-call | flops 1000000000 | bytes 3201552 | tf_op jit(solution)/shard_map/pallas_call | solution.py:518
  36.6 3.3 %shard_map.302 = (bf16[144,192]{1,0:T(8,128)(2,1)S(1)}, bf16[144,192]{1,0:T(8,128)(2,1)S(1)}, bf16[256,192]{1,0:T(8,128)(2,1)S(1)}, bf16[256,192]{1,0:T(8,128)(2...) custom-call(bf16[48,192]{1,0:T(8,128)(2,1)S(1)} %get-tuple-element.6, ...), custom_call_target="tpu_custom_call" | custom-call | flops 1000000000 | bytes 2543616 | tf_op jit(solution)/shard_map/pallas_call | solution.py:518
  39.9 0.8 copy-done.25
  44.5 1.0 collective-permute-start.3
  45.4 0.9 collective-permute-start.4
  46.3 1.6 reshape.39.upstream
  47.9 3.2 %collective-permute-done.3.qb = bf16[48,192]{1,0:T(8,128)(2,1)} collective-permute-done((bf16[48,192]{1,0:T(8,128)(2,1)}, bf16[48,192]{1,0:T(8,128)(2,1)}, u32[]{:S(2)}, u32[]{:S(2)}) %collective-permute-start.3) | collective-permute-done | bytes 18464 | tf_op jit(solution)/shard_map/ppermute | solution.py:537
  51.1 2.4 %collective-permute-done.5.qd = bf16[48,192]{1,0:T(8,128)(2,1)} collective-permute-done((bf16[48,192]{1,0:T(8,128)(2,1)}, bf16[48,192]{1,0:T(8,128)(2,1)}, u32[]{:S(2)}, u32[]{:S(2)}) %collective-permute-start.5) | collective-permute-done | bytes 18464 | tf_op jit(solution)/shard_map/ppermute | solution.py:539
  53.5 1.3 copy-done.7
  54.8 0.9 copy-done.16
  55.7 0.9 copy-done.21
  56.6 0.9 copy-done.39
  57.5 0.9 copy-done.47
  59.8 0.7 copy-done.72
  60.6 2.0 %shard_map.303 = (bf16[144,192]{1,0:T(8,128)(2,1)S(1)}, bf16[144,192]{1,0:T(8,128)(2,1)S(1)}, bf16[768,384]{1,0:T(8,128)(2,1)S(1)}, f32[8,384]{1,0:T(8,128)S(1)}...) custom-call(bf16[48,192]{1,0:T(8,128)(2,1)S(1)} %copy-done.72, ...), custom_call_target="tpu_custom_call" | custom-call | flops 1000000000 | bytes 2357760 | tf_op jit(solution)/shard_map/pallas_call | solution.py:518
  63.2 3.1 %collective-permute-start.6 = (bf16[48,192]{1,0:T(8,128)(2,1)S(1)}, bf16[48,192]{1,0:T(8,128)(2,1)S(1)}, u32[]{:S(2)}, u32[]{:S(2)}) collective-permute-start(bf16[48,192]{1,0:T(8,128)(2,1)S(1)} %get-tuple-element.77), channel_id=1, source_target_pairs={{0,240},{16,0},{32,16},{48,32},{64,48},{80,64},{96,80},{112,96},{1... | collective-permute-start | bytes 55304 | tf_op jit(solution)/shard_map/ppermute | solution.py:537
  66.3 3.4 %collective-permute-start.8 = (bf16[48,192]{1,0:T(8,128)(2,1)S(1)}, bf16[48,192]{1,0:T(8,128)(2,1)S(1)}, u32[]{:S(2)}, u32[]{:S(2)}) collective-permute-start(bf16[48,192]{1,0:T(8,128)(2,1)S(1)} %get-tuple-element.79), channel_id=1, source_target_pairs={{0,252},{4,240},{8,244},{12,248},{16,12},{20,0},{24,4},{28,8},{32,... | collective-permute-start | bytes 55304 | tf_op jit(solution)/shard_map/ppermute | solution.py:539
  70.0 0.8 collective-permute-done.8.qd
  71.0 2.6 %shard_map.304 = (bf16[8,160,384]{2,1,0:T(8,128)(2,1)S(1)}, bf16[48,192]{1,0:T(8,128)(2,1)S(1)}, bf16[48,192]{1,0:T(8,128)(2,1)S(1)}, bf16[48,192]{1,0:T(8,128)(2,1)S(1)}, bf16[48,192]{1,0:T(8,128)(2,1)S(1)}) custom-call(bf16[48,192]{1,0:T(8,128)(2,1)S(1)} %get-tuple-element.76.qa, bf16[48,192]{1,0:T(8,128)(2,1)S(1)} %collective-permute-done.6.qb, ...), custom_call_target="tpu_custom_call" | custom-call | flops 1000000000 | bytes 4282368 | tf_op jit(solution)/shard_map/pallas_call | solution.py:518
  73.7 2.5 %collective-permute-start.10 = (bf16[48,192]{1,0:T(8,128)(2,1)S(1)}, bf16[48,192]{1,0:T(8,128)(2,1)S(1)}, u32[]{:S(2)}, u32[]{:S(2)}) collective-permute-start(bf16[48,192]{1,0:T(8,128)(2,1)S(1)} %get-tuple-element.90), channel_id=1, source_target_pairs={{0,4},{4,8},{8,12},{12,0},{1,5},{5,9},{9,13},{13,1},{2,6},{6,10},{... | collective-permute-start | bytes 55304 | tf_op jit(solution)/shard_map/ppermute | solution.py:538
  76.2 1.3 collective-permute-start.13
  77.5 2.5 %collective-permute-done.9.qb = bf16[48,192]{1,0:T(8,128)(2,1)S(1)} collective-permute-done((bf16[48,192]{1,0:T(8,128)(2,1)S(1)}, bf16[48,192]{1,0:T(8,128)(2,1)S(1)}, u32[]{:S(2)}, u32[]{:S(2)}) %collective-permute-start.9) | collective-permute-done | bytes 18464 | tf_op jit(solution)/shard_map/ppermute | solution.py:537
  80.0 3.2 %collective-permute-done.11.qd = bf16[48,192]{1,0:T(8,128)(2,1)S(1)} collective-permute-done((bf16[48,192]{1,0:T(8,128)(2,1)S(1)}, bf16[48,192]{1,0:T(8,128)(2,1)S(1)}, u32[]{:S(2)}, u32[]{:S(2)}) %collective-permute-start.11) | collective-permute-done | bytes 18464 | tf_op jit(solution)/shard_map/ppermute | solution.py:539
  83.3 4.8 %shard_map.305 = (bf16[144,192]{1,0:T(8,128)(2,1)S(1)}, bf16[8,160,384]{2,1,0:T(8,128)(2,1)S(1)}) custom-call(bf16[48,192]{1,0:T(8,128)(2,1)S(1)} %get-tuple-element.88.qa, bf16[48,192]{1,0:T(8,128)(2,1)S(1)} %collective-permute-done.9.qb, bf16[48,192]{1,0:T(8,128)(2,1)S(1)} %collective-permute-done.10.qc, bf16[48,192]{1,0:T(8,128)(2,1)S(1)} %collective-permute-done.11.qd, ...), custom_call_target="tpu_custom_call" | custom-call | flops 1000000000 | bytes 5104128 | tf_op jit(solution)/shard_map/pallas_call | solution.py:518
  88.7 1.8 collective-permute-start.12
  90.5 2.1 %collective-permute-done.12.got_first = bf16[8,160,384]{2,1,0:T(8,128)(2,1)S(1)} collective-permute-done((bf16[8,160,384]{2,1,0:T(8,128)(2,1)S(1)}, bf16[8,160,384]{2,1,0:T(8,128)(2,1)S(1)}, u32[]{:S(2)}, u32[]{:S(2)}) %collective-permute-start.12) | collective-permute-done | bytes 983072 | tf_op jit(solution)/shard_map/ppermute | solution.py:545
  92.6 0.8 shard_map.306
  93.4 1.4 collective-permute-start.14
  94.8 2.6 %collective-permute-start.15 = (bf16[2,160,384]{2,1,0:T(8,128)(2,1)S(1)}, bf16[2,160,384]{2,1,0:T(8,128)(2,1)S(1)}, u32[]{:S(2)}, u32[]{:S(2)}) collective-permute-start(bf16[2,160,384]{2,1,0:T(8,128)(2,1)S(1)} %get-tuple-element.104), channel_id=1, source_target_pairs={{0,2},{1,3},{2,0},{3,1},{4,6},{5,7},{6,4},{7,5},{8,10},{9,11},{10,... | collective-permute-start | bytes 737288 | tf_op jit(solution)/shard_map/ppermute | solution.py:545
  97.4 3.2 %collective-permute-done.14.b = bf16[2,160,384]{2,1,0:T(8,128)(2,1)S(1)} collective-permute-done((bf16[2,160,384]{2,1,0:T(8,128)(2,1)S(1)}, bf16[2,160,384]{2,1,0:T(8,128)(2,1)S(1)}, u32[]{:S(2)}, u32[]{:S(2)}) %collective-permute-start.14) | collective-permute-done | bytes 245792 | tf_op jit(solution)/shard_map/ppermute | solution.py:545
  100.7 7.8 %collective-permute-done.15.c = bf16[2,160,384]{2,1,0:T(8,128)(2,1)S(1)} collective-permute-done((bf16[2,160,384]{2,1,0:T(8,128)(2,1)S(1)}, bf16[2,160,384]{2,1,0:T(8,128)(2,1)S(1)}, u32[]{:S(2)}, u32[]{:S(2)}) %collective-permute-start.15) | collective-permute-done | bytes 245792 | tf_op jit(solution)/shard_map/ppermute | solution.py:545
  108.5 2.0 %collective-permute-done.16.d = bf16[2,160,384]{2,1,0:T(8,128)(2,1)S(1)} collective-permute-done((bf16[2,160,384]{2,1,0:T(8,128)(2,1)S(1)}, bf16[2,160,384]{2,1,0:T(8,128)(2,1)S(1)}, u32[]{:S(2)}, u32[]{:S(2)}) %collective-permute-start.16) | collective-permute-done | bytes 245792 | tf_op jit(solution)/shard_map/ppermute | solution.py:545
  111.1 1.3 collective-permute-start.17
  112.4 2.7 %collective-permute-done.17.b = bf16[160,384]{1,0:T(8,128)(2,1)S(1)} collective-permute-done((bf16[160,384]{1,0:T(8,128)(2,1)S(1)}, bf16[160,384]{1,0:T(8,128)(2,1)S(1)}, u32[]{:S(2)}, u32[]{:S(2)}) %collective-permute-start.17) | collective-permute-done | bytes 122912 | tf_op jit(solution)/shard_map/ppermute | solution.py:545
  115.4 4.0 %collective-permute-start.18 = (bf16[160,384]{1,0:T(8,128)(2,1)S(1)}, bf16[160,384]{1,0:T(8,128)(2,1)S(1)}, u32[]{:S(2)}, u32[]{:S(2)}) collective-permute-start(bf16[160,384]{1,0:T(8,128)(2,1)S(1)} %shard_map.308.a), channel_id=1, source_target_pairs={{0,16},{16,0},{32,48},{48,32},{64,80},{80,64},{96,112},{112,96},{1... | collective-permute-start | bytes 368648 | tf_op jit(solution)/shard_map/ppermute | solution.py:545
  119.4 2.1 %collective-permute-done.20.d = bf16[160,384]{1,0:T(8,128)(2,1)S(1)} collective-permute-done((bf16[160,384]{1,0:T(8,128)(2,1)S(1)}, bf16[160,384]{1,0:T(8,128)(2,1)S(1)}, u32[]{:S(2)}, u32[]{:S(2)}) %collective-permute-start.20) | collective-permute-done | bytes 122912 | tf_op jit(solution)/shard_map/ppermute | solution.py:545
  121.5 1.2 collective-permute-done.18.b
  122.8 3.8 %collective-permute-start.23 = (bf16[192,384]{1,0:T(8,128)(2,1)S(1)}, bf16[192,384]{1,0:T(8,128)(2,1)S(1)}, u32[]{:S(2)}, u32[]{:S(2)}) collective-permute-start(bf16[192,384]{1,0:T(8,128)(2,1)S(1)} %shard_map.309.a), channel_id=1, source_target_pairs={{0,192},{16,208},{32,224},{48,240},{64,128},{80,144},{96,160},{112... | collective-permute-start | bytes 442376 | tf_op jit(solution)/shard_map/ppermute | solution.py:545
  126.6 1.5 collective-permute-start.22
  128.8 10.5 %collective-permute-done.23.d = bf16[192,384]{1,0:T(8,128)(2,1)S(1)} collective-permute-done((bf16[192,384]{1,0:T(8,128)(2,1)S(1)}, bf16[192,384]{1,0:T(8,128)(2,1)S(1)}, u32[]{:S(2)}, u32[]{:S(2)}) %collective-permute-start.23) | collective-permute-done | bytes 147488 | tf_op jit(solution)/shard_map/ppermute | solution.py:545
  139.3 3.3 %collective-permute-done.21.b = bf16[192,384]{1,0:T(8,128)(2,1)S(1)} collective-permute-done((bf16[192,384]{1,0:T(8,128)(2,1)S(1)}, bf16[192,384]{1,0:T(8,128)(2,1)S(1)}, u32[]{:S(2)}, u32[]{:S(2)}) %collective-permute-start.21) | collective-permute-done | bytes 147488 | tf_op jit(solution)/shard_map/ppermute | solution.py:545
  142.7 5.7 %collective-permute-done.24 = bf16[288,384]{1,0:T(8,128)(2,1)S(1)} collective-permute-done((bf16[288,384]{1,0:T(8,128)(2,1)S(1)}, bf16[288,384]{1,0:T(8,128)(2,1)S(1)}, u32[]{:S(2)}, u32[]{:S(2)}) %collective-permute-start.24) | collective-permute-done | bytes 221216 | tf_op jit(solution)/shard_map/ppermute | solution.py:545
  148.6 0.7 collective-permute-start.25
  149.3 2.6 %collective-permute-start.27 = (bf16[2,288,384]{2,1,0:T(8,128)(2,1)S(1)}, bf16[2,288,384]{2,1,0:T(8,128)(2,1)S(1)}, u32[]{:S(2)}, u32[]{:S(2)}) collective-permute-start(bf16[2,288,384]{2,1,0:T(8,128)(2,1)S(1)} %get-tuple-element.120), channel_id=1, source_target_pairs={{0,3},{1,2},{2,1},{3,0},{4,7},{5,6},{6,5},{7,4},{8,11},{9,10},{10,... | collective-permute-start | bytes 1327112 | tf_op jit(solution)/shard_map/ppermute | solution.py:545
  151.9 7.9 %collective-permute-done.26 = bf16[2,288,384]{2,1,0:T(8,128)(2,1)S(1)} collective-permute-done((bf16[2,288,384]{2,1,0:T(8,128)(2,1)S(1)}, bf16[2,288,384]{2,1,0:T(8,128)(2,1)S(1)}, u32[]{:S(2)}, u32[]{:S(2)}) %collective-permute-start.26) | collective-permute-done | bytes 442400 | tf_op jit(solution)/shard_map/ppermute | solution.py:545
  159.7 7.2 %collective-permute-done.25 = bf16[2,288,384]{2,1,0:T(8,128)(2,1)S(1)} collective-permute-done((bf16[2,288,384]{2,1,0:T(8,128)(2,1)S(1)}, bf16[2,288,384]{2,1,0:T(8,128)(2,1)S(1)}, u32[]{:S(2)}, u32[]{:S(2)}) %collective-permute-start.25) | collective-permute-done | bytes 442400 | tf_op jit(solution)/shard_map/ppermute | solution.py:545
  166.9 4.8 %collective-permute-done.27 = bf16[2,288,384]{2,1,0:T(8,128)(2,1)S(1)} collective-permute-done((bf16[2,288,384]{2,1,0:T(8,128)(2,1)S(1)}, bf16[2,288,384]{2,1,0:T(8,128)(2,1)S(1)}, u32[]{:S(2)}, u32[]{:S(2)}) %collective-permute-start.27) | collective-permute-done | bytes 442400 | tf_op jit(solution)/shard_map/ppermute | solution.py:545
  172.5 1.6 reshape.40
  174.1 1.6 reshape.41
  175.9 4.3 %shard_map.311 = (f32[2,2,192]{2,1,0:T(2,128)}, f32[2,2,192]{2,1,0:T(2,128)}, f32[2,192,576]{2,1,0:T(8,128)}, f32[2,576]{1,0:T(2,128)}, f32[2,192,192]{2,1,0:T(8...) custom-call(s32[4]{0:T(128)S(1)} %pad_add_fusion.where.refs_0_, ...), custom_call_target="tpu_custom_call" | custom-call | bytes 9641616 | tf_op jit(solution)/shard_map/pallas_call | solution.py:518
  (159 shorter events, 15.4 us)
Async XLA Ops:
  1.6 20.5 %copy-start.18 = (bf16[144,192]{1,0:T(8,128)(2,1)}, bf16[144,192]{1,0:T(8,128)(2,1)S(1)}, u32[]{:S(2)}) copy-start(bf16[144,192]{1,0:T(8,128)(2,1)S(1)} %reshape.38.fields) | copy-start | bytes 165892
  15.5 18.0 %copy-start.1 = (bf16[256,1536]{1,0:T(8,128)(2,1)S(1)}, bf16[256,1536]{1,0:T(8,128)(2,1)}, u32[]{:S(2)}) copy-start(bf16[256,1536]{1,0:T(8,128)(2,1)} %constant.53.clone.spread) | copy-start | bytes 2359300
  15.5 18.0 %copy-start.2 = (f32[2,16,6,3312]{3,1,2,0:T(8,128)S(1)}, f32[2,16,6,3312]{3,1,2,0:T(8,128)}, u32[]{:S(2)}) copy-start(f32[2,16,6,3312]{3,1,2,0:T(8,128)} %param.33) | copy-start | bytes 7630852
  15.5 18.0 %copy-start.11 = (f32[192,192]{1,0:T(8,128)S(1)}, f32[192,192]{1,0:T(8,128)}, u32[]{:S(2)}) copy-start(f32[192,192]{1,0:T(8,128)} %constant.52.clone.sort) | copy-start | bytes 442372
  15.5 18.0 %copy-start.13 = (f32[144,192]{1,0:T(8,128)S(1)}, f32[144,192]{1,0:T(8,128)}, u32[]{:S(2)}) copy-start(f32[144,192]{1,0:T(8,128)} %constant.51.clone.place) | copy-start | bytes 331780
  15.5 18.0 %copy-start.69 = (s32[96]{0:T(128)S(1)}, s32[96]{0:T(128)}, u32[]{:S(2)}) copy-start(s32[96]{0:T(128)} %valid.3) | copy-start | bytes 1156
  22.2 13.7 %copy-start.23 = (bf16[6,144,256]{2,1,0:T(8,128)(2,1)}, bf16[6,144,256]{2,1,0:T(8,128)(2,1)S(1)}, u32[]{:S(2)}) copy-start(bf16[6,144,256]{2,1,0:T(8,128)(2,1)S(1)} %get-tuple-element.97.p) | copy-start | bytes 1327108
  22.2 13.7 %copy-start.29 = (bf16[256,192]{1,0:T(8,128)(2,1)}, bf16[256,192]{1,0:T(8,128)(2,1)S(1)}, u32[]{:S(2)}) copy-start(bf16[256,192]{1,0:T(8,128)(2,1)S(1)} %get-tuple-element.95.k) | copy-start | bytes 294916
  22.2 13.7 %copy-start.31 = (bf16[256,192]{1,0:T(8,128)(2,1)}, bf16[256,192]{1,0:T(8,128)(2,1)S(1)}, u32[]{:S(2)}) copy-start(bf16[256,192]{1,0:T(8,128)(2,1)S(1)} %get-tuple-element.96.v) | copy-start | bytes 294916
  22.2 13.7 %copy-start.40 = (bf16[144,192]{1,0:T(8,128)(2,1)}, bf16[144,192]{1,0:T(8,128)(2,1)S(1)}, u32[]{:S(2)}) copy-start(bf16[144,192]{1,0:T(8,128)(2,1)S(1)} %get-tuple-element.94.q) | copy-start | bytes 165892
  22.2 13.7 %copy-start.42 = (bf16[144,192]{1,0:T(8,128)(2,1)}, bf16[144,192]{1,0:T(8,128)(2,1)S(1)}, u32[]{:S(2)}) copy-start(bf16[144,192]{1,0:T(8,128)(2,1)S(1)} %get-tuple-element.98.mix) | copy-start | bytes 165892
  22.2 13.7 %copy-start.44 = (bf16[144,192]{1,0:T(8,128)(2,1)}, bf16[144,192]{1,0:T(8,128)(2,1)S(1)}, u32[]{:S(2)}) copy-start(bf16[144,192]{1,0:T(8,128)(2,1)S(1)} %get-tuple-element.93.h1) | copy-start | bytes 165892
  22.2 13.7 %copy-start.46 = (bf16[144,192]{1,0:T(8,128)(2,1)}, bf16[144,192]{1,0:T(8,128)(2,1)S(1)}, u32[]{:S(2)}) copy-start(bf16[144,192]{1,0:T(8,128)(2,1)S(1)} %get-tuple-element.74.y1) | copy-start | bytes 165892
  22.2 13.7 %collective-permute-start = (bf16[48,192]{1,0:T(8,128)(2,1)S(1)}, bf16[48,192]{1,0:T(8,128)(2,1)S(1)}, u32[]{:S(2)}, u32[]{:S(2)}) collective-permute-start(bf16[48,192]{1,0:T(8,128)(2,1)S(1)} %get-tuple-element.67), channel_id=1, source_target_pairs={{0,240},{16,0},{32,16},{48,32},{64,48},{80,64},{96,80},{112,96},{1... | collective-permute-start | bytes 55304 | tf_op jit(solution)/shard_map/ppermute | solution.py:537
  31.2 4.8 %collective-permute-start.1 = (bf16[48,192]{1,0:T(8,128)(2,1)S(1)}, bf16[48,192]{1,0:T(8,128)(2,1)S(1)}, u32[]{:S(2)}, u32[]{:S(2)}) collective-permute-start(bf16[48,192]{1,0:T(8,128)(2,1)S(1)} %get-tuple-element.68), channel_id=1, source_target_pairs={{0,12},{4,0},{8,4},{12,8},{1,13},{5,1},{9,5},{13,9},{2,14},{6,2},{... | collective-permute-start | bytes 55304 | tf_op jit(solution)/shard_map/ppermute | solution.py:538
  32.1 4.5 %collective-permute-start.2 = (bf16[48,192]{1,0:T(8,128)(2,1)S(1)}, bf16[48,192]{1,0:T(8,128)(2,1)S(1)}, u32[]{:S(2)}, u32[]{:S(2)}) collective-permute-start(bf16[48,192]{1,0:T(8,128)(2,1)S(1)} %get-tuple-element.69), channel_id=1, source_target_pairs={{0,252},{4,240},{8,244},{12,248},{16,12},{20,0},{24,4},{28,8},{32,... | collective-permute-start | bytes 55304 | tf_op jit(solution)/shard_map/ppermute | solution.py:539
  36.6 16.9 %copy-start.6 = (f32[2,192,768]{2,1,0:T(8,128)S(1)}, f32[2,192,768]{2,1,0:T(8,128)}, u32[]{:S(2)}) copy-start(f32[2,192,768]{2,1,0:T(8,128)} %expand.5) | copy-start | bytes 3538948
  36.6 16.9 %copy-start.56 = (f32[2,768]{1,0:T(2,128)S(1)}, f32[2,768]{1,0:T(2,128)}, u32[]{:S(2)}) copy-start(f32[2,768]{1,0:T(2,128)} %upbias.5) | copy-start | bytes 18436
  36.6 16.9 %copy-start.58 = (f32[2,2,192]{2,1,0:T(2,128)S(1)}, f32[2,2,192]{2,1,0:T(2,128)}, u32[]{:S(2)}) copy-start(f32[2,2,192]{2,1,0:T(2,128)} %scales.5) | copy-start | bytes 9220
  44.5 6.6 %collective-permute-start.3 = (bf16[48,192]{1,0:T(8,128)(2,1)}, bf16[48,192]{1,0:T(8,128)(2,1)}, u32[]{:S(2)}, u32[]{:S(2)}) collective-permute-start(bf16[48,192]{1,0:T(8,128)(2,1)} %get-tuple-element.71), channel_id=1, source_target_pairs={{0,16},{16,32},{32,48},{48,64},{64,80},{80,96},{96,112},{112,128},... | collective-permute-start | bytes 55304 | tf_op jit(solution)/shard_map/ppermute | solution.py:537
  45.4 5.6 %collective-permute-start.4 = (bf16[48,192]{1,0:T(8,128)(2,1)}, bf16[48,192]{1,0:T(8,128)(2,1)}, u32[]{:S(2)}, u32[]{:S(2)}) collective-permute-start(bf16[48,192]{1,0:T(8,128)(2,1)} %get-tuple-element.72), channel_id=1, source_target_pairs={{0,4},{4,8},{8,12},{12,0},{1,5},{5,9},{9,13},{13,1},{2,6},{6,10},{... | collective-permute-start | bytes 55304 | tf_op jit(solution)/shard_map/ppermute | solution.py:538
  46.3 7.2 %collective-permute-start.5 = (bf16[48,192]{1,0:T(8,128)(2,1)}, bf16[48,192]{1,0:T(8,128)(2,1)}, u32[]{:S(2)}, u32[]{:S(2)}) collective-permute-start(bf16[48,192]{1,0:T(8,128)(2,1)} %get-tuple-element.73), channel_id=1, source_target_pairs={{0,20},{4,24},{8,28},{12,16},{16,36},{20,40},{24,44},{28,32},{32,5... | collective-permute-start | bytes 55304 | tf_op jit(solution)/shard_map/ppermute | solution.py:539
  60.5 10.3 %copy-start.26 = (bf16[6,144,256]{2,1,0:T(8,128)(2,1)S(1)}, bf16[6,144,256]{2,1,0:T(8,128)(2,1)}, u32[]{:S(2)}) copy-start(bf16[6,144,256]{2,1,0:T(8,128)(2,1)} %copy-done.25) | copy-start | bytes 1327108
  60.5 10.3 %copy-start.28 = (f32[144,192]{1,0:T(8,128)S(1)}, f32[144,192]{1,0:T(8,128)}, u32[]{:S(2)}) copy-start(f32[144,192]{1,0:T(8,128)} %constant.50.clone.join) | copy-start | bytes 331780
  60.5 10.3 %copy-start.34 = (bf16[256,192]{1,0:T(8,128)(2,1)S(1)}, bf16[256,192]{1,0:T(8,128)(2,1)}, u32[]{:S(2)}) copy-start(bf16[256,192]{1,0:T(8,128)(2,1)} %copy-done.33) | copy-start | bytes 294916
  60.5 10.3 %copy-start.36 = (bf16[256,192]{1,0:T(8,128)(2,1)S(1)}, bf16[256,192]{1,0:T(8,128)(2,1)}, u32[]{:S(2)}) copy-start(bf16[256,192]{1,0:T(8,128)(2,1)} %copy-done.35) | copy-start | bytes 294916
  60.5 10.3 %copy-start.50 = (bf16[144,192]{1,0:T(8,128)(2,1)S(1)}, bf16[144,192]{1,0:T(8,128)(2,1)}, u32[]{:S(2)}) copy-start(bf16[144,192]{1,0:T(8,128)(2,1)} %copy-done.49) | copy-start | bytes 165892
  60.5 10.3 %copy-start.52 = (bf16[144,192]{1,0:T(8,128)(2,1)S(1)}, bf16[144,192]{1,0:T(8,128)(2,1)}, u32[]{:S(2)}) copy-start(bf16[144,192]{1,0:T(8,128)(2,1)} %copy-done.51) | copy-start | bytes 165892
  60.5 10.3 %copy-start.54 = (bf16[144,192]{1,0:T(8,128)(2,1)S(1)}, bf16[144,192]{1,0:T(8,128)(2,1)}, u32[]{:S(2)}) copy-start(bf16[144,192]{1,0:T(8,128)(2,1)} %copy-done.53) | copy-start | bytes 165892
  63.2 6.5 %collective-permute-start.6 = (bf16[48,192]{1,0:T(8,128)(2,1)S(1)}, bf16[48,192]{1,0:T(8,128)(2,1)S(1)}, u32[]{:S(2)}, u32[]{:S(2)}) collective-permute-start(bf16[48,192]{1,0:T(8,128)(2,1)S(1)} %get-tuple-element.77), channel_id=1, source_target_pairs={{0,240},{16,0},{32,16},{48,32},{64,48},{80,64},{96,80},{112,96},{1... | collective-permute-start | bytes 55304 | tf_op jit(solution)/shard_map/ppermute | solution.py:537
  66.3 3.7 %collective-permute-start.7 = (bf16[48,192]{1,0:T(8,128)(2,1)S(1)}, bf16[48,192]{1,0:T(8,128)(2,1)S(1)}, u32[]{:S(2)}, u32[]{:S(2)}) collective-permute-start(bf16[48,192]{1,0:T(8,128)(2,1)S(1)} %get-tuple-element.78), channel_id=1, source_target_pairs={{0,12},{4,0},{8,4},{12,8},{1,13},{5,1},{9,5},{13,9},{2,14},{6,2},{... | collective-permute-start | bytes 55304 | tf_op jit(solution)/shard_map/ppermute | solution.py:538
  66.3 4.5 %collective-permute-start.8 = (bf16[48,192]{1,0:T(8,128)(2,1)S(1)}, bf16[48,192]{1,0:T(8,128)(2,1)S(1)}, u32[]{:S(2)}, u32[]{:S(2)}) collective-permute-start(bf16[48,192]{1,0:T(8,128)(2,1)S(1)} %get-tuple-element.79), channel_id=1, source_target_pairs={{0,252},{4,240},{8,244},{12,248},{16,12},{20,0},{24,4},{28,8},{32,... | collective-permute-start | bytes 55304 | tf_op jit(solution)/shard_map/ppermute | solution.py:539
  70.8 12.3 %copy-start.17 = (f32[192,144]{1,0:T(8,128)S(1)}, f32[192,144]{1,0:T(8,128)}, u32[]{:S(2)}) copy-start(f32[192,144]{1,0:T(8,128)} %constant.49.clone.cut) | copy-start | bytes 331780
  70.8 12.3 %copy-start.19 = (bf16[144,192]{1,0:T(8,128)(2,1)S(1)}, bf16[144,192]{1,0:T(8,128)(2,1)}, u32[]{:S(2)}) copy-start(bf16[144,192]{1,0:T(8,128)(2,1)} %copy-done.18) | copy-start | bytes 165892
  70.9 12.3 %copy-start.22 = (f32[144,144]{1,0:T(8,128)S(1)}, f32[144,144]{1,0:T(8,128)}, u32[]{:S(2)}) copy-start(f32[144,144]{1,0:T(8,128)} %constant.48.clone.turn) | copy-start | bytes 248836
  70.9 12.3 %copy-start.24 = (bf16[6,144,256]{2,1,0:T(8,128)(2,1)S(1)}, bf16[6,144,256]{2,1,0:T(8,128)(2,1)}, u32[]{:S(2)}) copy-start(bf16[6,144,256]{2,1,0:T(8,128)(2,1)} %copy-done.23) | copy-start | bytes 1327108
  70.9 12.3 %copy-start.30 = (bf16[256,192]{1,0:T(8,128)(2,1)S(1)}, bf16[256,192]{1,0:T(8,128)(2,1)}, u32[]{:S(2)}) copy-start(bf16[256,192]{1,0:T(8,128)(2,1)} %copy-done.29) | copy-start | bytes 294916
  70.9 12.3 %copy-start.32 = (bf16[256,192]{1,0:T(8,128)(2,1)S(1)}, bf16[256,192]{1,0:T(8,128)(2,1)}, u32[]{:S(2)}) copy-start(bf16[256,192]{1,0:T(8,128)(2,1)} %copy-done.31) | copy-start | bytes 294916
  70.9 12.3 %copy-start.41 = (bf16[144,192]{1,0:T(8,128)(2,1)S(1)}, bf16[144,192]{1,0:T(8,128)(2,1)}, u32[]{:S(2)}) copy-start(bf16[144,192]{1,0:T(8,128)(2,1)} %copy-done.40) | copy-start | bytes 165892
  70.9 12.3 %copy-start.43 = (bf16[144,192]{1,0:T(8,128)(2,1)S(1)}, bf16[144,192]{1,0:T(8,128)(2,1)}, u32[]{:S(2)}) copy-start(bf16[144,192]{1,0:T(8,128)(2,1)} %copy-done.42) | copy-start | bytes 165892
  70.9 12.3 %copy-start.45 = (bf16[144,192]{1,0:T(8,128)(2,1)S(1)}, bf16[144,192]{1,0:T(8,128)(2,1)}, u32[]{:S(2)}) copy-start(bf16[144,192]{1,0:T(8,128)(2,1)} %copy-done.44) | copy-start | bytes 165892
  70.9 12.3 %copy-start.48 = (bf16[144,192]{1,0:T(8,128)(2,1)S(1)}, bf16[144,192]{1,0:T(8,128)(2,1)}, u32[]{:S(2)}) copy-start(bf16[144,192]{1,0:T(8,128)(2,1)} %copy-done.46) | copy-start | bytes 165892
  70.9 12.3 %copy-start.61 = (f32[2,2,192]{2,1,0:T(2,128)S(1)}, f32[2,2,192]{2,1,0:T(2,128)}, u32[]{:S(2)}) copy-start(f32[2,2,192]{2,1,0:T(2,128)} %offsets.5) | copy-start | bytes 9220
  71.0 12.3 %copy-start.66 = (f32[2,192]{1,0:T(2,128)S(1)}, f32[2,192]{1,0:T(2,128)}, u32[]{:S(2)}) copy-start(f32[2,192]{1,0:T(2,128)} %downbias.5) | copy-start | bytes 4612
  73.6 6.4 %collective-permute-start.9 = (bf16[48,192]{1,0:T(8,128)(2,1)S(1)}, bf16[48,192]{1,0:T(8,128)(2,1)S(1)}, u32[]{:S(2)}, u32[]{:S(2)}) collective-permute-start(bf16[48,192]{1,0:T(8,128)(2,1)S(1)} %get-tuple-element.89), channel_id=1, source_target_pairs={{0,16},{16,32},{32,48},{48,64},{64,80},{80,96},{96,112},{112,128},... | collective-permute-start | bytes 55304 | tf_op jit(solution)/shard_map/ppermute | solution.py:537
  73.7 6.3 %collective-permute-start.10 = (bf16[48,192]{1,0:T(8,128)(2,1)S(1)}, bf16[48,192]{1,0:T(8,128)(2,1)S(1)}, u32[]{:S(2)}, u32[]{:S(2)}) collective-permute-start(bf16[48,192]{1,0:T(8,128)(2,1)S(1)} %get-tuple-element.90), channel_id=1, source_target_pairs={{0,4},{4,8},{8,12},{12,0},{1,5},{5,9},{9,13},{13,1},{2,6},{6,10},{... | collective-permute-start | bytes 55304 | tf_op jit(solution)/shard_map/ppermute | solution.py:538
  76.2 7.0 %collective-permute-start.11 = (bf16[48,192]{1,0:T(8,128)(2,1)S(1)}, bf16[48,192]{1,0:T(8,128)(2,1)S(1)}, u32[]{:S(2)}, u32[]{:S(2)}) collective-permute-start(bf16[48,192]{1,0:T(8,128)(2,1)S(1)} %get-tuple-element.91), channel_id=1, source_target_pairs={{0,20},{4,24},{8,28},{12,16},{16,36},{20,40},{24,44},{28,32},{32,5... | collective-permute-start | bytes 55304 | tf_op jit(solution)/shard_map/ppermute | solution.py:539
  76.2 14.3 %collective-permute-start.13 = (bf16[8,160,384]{2,1,0:T(8,128)(2,1)S(1)}, bf16[8,160,384]{2,1,0:T(8,128)(2,1)S(1)}, u32[]{:S(2)}, u32[]{:S(2)}) collective-permute-start(bf16[8,160,384]{2,1,0:T(8,128)(2,1)S(1)} %get-tuple-element.101.second), channel_id=1, source_target_pairs={{0,4},{8,12},{1,5},{9,13},{2,6},{10,14},{3,7},{11,15},{16,20},{24,... | collective-permute-start | bytes 2949128 | tf_op jit(solution)/shard_map/ppermute | solution.py:545
  88.7 3.9 %collective-permute-start.12 = (bf16[8,160,384]{2,1,0:T(8,128)(2,1)S(1)}, bf16[8,160,384]{2,1,0:T(8,128)(2,1)S(1)}, u32[]{:S(2)}, u32[]{:S(2)}) collective-permute-start(bf16[8,160,384]{2,1,0:T(8,128)(2,1)S(1)} %get-tuple-element.100.first), channel_id=1, source_target_pairs={{4,0},{12,8},{5,1},{13,9},{6,2},{14,10},{7,3},{15,11},{20,16},{28,... | collective-permute-start | bytes 2949128 | tf_op jit(solution)/shard_map/ppermute | solution.py:545
  93.4 7.3 %collective-permute-start.14 = (bf16[2,160,384]{2,1,0:T(8,128)(2,1)S(1)}, bf16[2,160,384]{2,1,0:T(8,128)(2,1)S(1)}, u32[]{:S(2)}, u32[]{:S(2)}) collective-permute-start(bf16[2,160,384]{2,1,0:T(8,128)(2,1)S(1)} %get-tuple-element.103), channel_id=1, source_target_pairs={{0,1},{1,0},{2,3},{3,2},{4,5},{5,4},{6,7},{7,6},{8,9},{9,8},{10,11... | collective-permute-start | bytes 737288 | tf_op jit(solution)/shard_map/ppermute | solution.py:545
  94.8 13.7 %collective-permute-start.15 = (bf16[2,160,384]{2,1,0:T(8,128)(2,1)S(1)}, bf16[2,160,384]{2,1,0:T(8,128)(2,1)S(1)}, u32[]{:S(2)}, u32[]{:S(2)}) collective-permute-start(bf16[2,160,384]{2,1,0:T(8,128)(2,1)S(1)} %get-tuple-element.104), channel_id=1, source_target_pairs={{0,2},{1,3},{2,0},{3,1},{4,6},{5,7},{6,4},{7,5},{8,10},{9,11},{10,... | collective-permute-start | bytes 737288 | tf_op jit(solution)/shard_map/ppermute | solution.py:545
  97.4 13.0 %collective-permute-start.16 = (bf16[2,160,384]{2,1,0:T(8,128)(2,1)S(1)}, bf16[2,160,384]{2,1,0:T(8,128)(2,1)S(1)}, u32[]{:S(2)}, u32[]{:S(2)}) collective-permute-start(bf16[2,160,384]{2,1,0:T(8,128)(2,1)S(1)} %get-tuple-element.105), channel_id=1, source_target_pairs={{0,3},{1,2},{2,1},{3,0},{4,7},{5,6},{6,5},{7,4},{8,11},{9,10},{10,... | collective-permute-start | bytes 737288 | tf_op jit(solution)/shard_map/ppermute | solution.py:545
  111.1 4.0 %collective-permute-start.17 = (bf16[160,384]{1,0:T(8,128)(2,1)S(1)}, bf16[160,384]{1,0:T(8,128)(2,1)S(1)}, u32[]{:S(2)}, u32[]{:S(2)}) collective-permute-start(bf16[160,384]{1,0:T(8,128)(2,1)S(1)} %get-tuple-element.107), channel_id=1, source_target_pairs={{0,8},{4,12},{8,0},{12,4},{1,9},{5,13},{9,1},{13,5},{2,10},{6,14},... | collective-permute-start | bytes 368648 | tf_op jit(solution)/shard_map/ppermute | solution.py:545
  115.2 6.3 %collective-permute-start.20 = (bf16[160,384]{1,0:T(8,128)(2,1)S(1)}, bf16[160,384]{1,0:T(8,128)(2,1)S(1)}, u32[]{:S(2)}, u32[]{:S(2)}) collective-permute-start(bf16[160,384]{1,0:T(8,128)(2,1)S(1)} %shard_map.308.a), channel_id=1, source_target_pairs={{0,48},{16,32},{32,16},{48,0},{64,112},{80,96},{96,80},{112,64},{1... | collective-permute-start | bytes 368648 | tf_op jit(solution)/shard_map/ppermute | solution.py:545
  115.3 6.2 %collective-permute-start.19 = (bf16[160,384]{1,0:T(8,128)(2,1)S(1)}, bf16[160,384]{1,0:T(8,128)(2,1)S(1)}, u32[]{:S(2)}, u32[]{:S(2)}) collective-permute-start(bf16[160,384]{1,0:T(8,128)(2,1)S(1)} %shard_map.308.a), channel_id=1, source_target_pairs={{0,32},{16,48},{32,0},{48,16},{64,96},{80,112},{96,64},{112,80},{1... | collective-permute-start | bytes 368648 | tf_op jit(solution)/shard_map/ppermute | solution.py:545
  115.4 7.3 %collective-permute-start.18 = (bf16[160,384]{1,0:T(8,128)(2,1)S(1)}, bf16[160,384]{1,0:T(8,128)(2,1)S(1)}, u32[]{:S(2)}, u32[]{:S(2)}) collective-permute-start(bf16[160,384]{1,0:T(8,128)(2,1)S(1)} %shard_map.308.a), channel_id=1, source_target_pairs={{0,16},{16,0},{32,48},{48,32},{64,80},{80,64},{96,112},{112,96},{1... | collective-permute-start | bytes 368648 | tf_op jit(solution)/shard_map/ppermute | solution.py:545
  122.8 16.5 %collective-permute-start.23 = (bf16[192,384]{1,0:T(8,128)(2,1)S(1)}, bf16[192,384]{1,0:T(8,128)(2,1)S(1)}, u32[]{:S(2)}, u32[]{:S(2)}) collective-permute-start(bf16[192,384]{1,0:T(8,128)(2,1)S(1)} %shard_map.309.a), channel_id=1, source_target_pairs={{0,192},{16,208},{32,224},{48,240},{64,128},{80,144},{96,160},{112... | collective-permute-start | bytes 442376 | tf_op jit(solution)/shard_map/ppermute | solution.py:545
  126.6 12.7 %collective-permute-start.22 = (bf16[192,384]{1,0:T(8,128)(2,1)S(1)}, bf16[192,384]{1,0:T(8,128)(2,1)S(1)}, u32[]{:S(2)}, u32[]{:S(2)}) collective-permute-start(bf16[192,384]{1,0:T(8,128)(2,1)S(1)} %shard_map.309.a), channel_id=1, source_target_pairs={{0,128},{16,144},{32,160},{48,176},{64,192},{80,208},{96,224},{112... | collective-permute-start | bytes 442376 | tf_op jit(solution)/shard_map/ppermute | solution.py:545
  128.1 14.5 %collective-permute-start.21 = (bf16[192,384]{1,0:T(8,128)(2,1)S(1)}, bf16[192,384]{1,0:T(8,128)(2,1)S(1)}, u32[]{:S(2)}, u32[]{:S(2)}) collective-permute-start(bf16[192,384]{1,0:T(8,128)(2,1)S(1)} %shard_map.309.a), channel_id=1, source_target_pairs={{0,64},{16,80},{32,96},{48,112},{64,0},{80,16},{96,32},{112,48},{1... | collective-permute-start | bytes 442376 | tf_op jit(solution)/shard_map/ppermute | solution.py:545
  142.6 5.8 %collective-permute-start.24 = (bf16[288,384]{1,0:T(8,128)(2,1)S(1)}, bf16[288,384]{1,0:T(8,128)(2,1)S(1)}, u32[]{:S(2)}, u32[]{:S(2)}) collective-permute-start(bf16[288,384]{1,0:T(8,128)(2,1)S(1)} %shard_map.310), channel_id=1, source_target_pairs={{0,8},{4,12},{8,0},{12,4},{1,9},{5,13},{9,1},{13,5},{2,10},{6,14},... | collective-permute-start | bytes 663560 | tf_op jit(solution)/shard_map/ppermute | solution.py:545
  148.5 11.2 %collective-permute-start.26 = (bf16[2,288,384]{2,1,0:T(8,128)(2,1)S(1)}, bf16[2,288,384]{2,1,0:T(8,128)(2,1)S(1)}, u32[]{:S(2)}, u32[]{:S(2)}) collective-permute-start(bf16[2,288,384]{2,1,0:T(8,128)(2,1)S(1)} %get-tuple-element.120), channel_id=1, source_target_pairs={{0,2},{1,3},{2,0},{3,1},{4,6},{5,7},{6,4},{7,5},{8,10},{9,11},{10,... | collective-permute-start | bytes 1327112 | tf_op jit(solution)/shard_map/ppermute | solution.py:545
  148.6 18.3 %collective-permute-start.25 = (bf16[2,288,384]{2,1,0:T(8,128)(2,1)S(1)}, bf16[2,288,384]{2,1,0:T(8,128)(2,1)S(1)}, u32[]{:S(2)}, u32[]{:S(2)}) collective-permute-start(bf16[2,288,384]{2,1,0:T(8,128)(2,1)S(1)} %get-tuple-element.120), channel_id=1, source_target_pairs={{0,1},{1,0},{2,3},{3,2},{4,5},{5,4},{6,7},{7,6},{8,9},{9,8},{10,11... | collective-permute-start | bytes 1327112 | tf_op jit(solution)/shard_map/ppermute | solution.py:545
  149.3 22.4 %collective-permute-start.27 = (bf16[2,288,384]{2,1,0:T(8,128)(2,1)S(1)}, bf16[2,288,384]{2,1,0:T(8,128)(2,1)S(1)}, u32[]{:S(2)}, u32[]{:S(2)}) collective-permute-start(bf16[2,288,384]{2,1,0:T(8,128)(2,1)S(1)} %get-tuple-element.120), channel_id=1, source_target_pairs={{0,3},{1,2},{2,1},{3,0},{4,7},{5,6},{6,5},{7,4},{8,11},{9,10},{10,... | collective-permute-start | bytes 1327112 | tf_op jit(solution)/shard_map/ppermute | solution.py:545
  172.0 3.9 %collective-permute-start.28 = (bf16[4,2,288,384]{3,2,1,0:T(8,128)(2,1)S(1)}, bf16[4,2,288,384]{3,2,1,0:T(8,128)(2,1)S(1)}, u32[]{:S(2)}, u32[]{:S(2)}) collective-permute-start(bf16[4,2,288,384]{3,2,1,0:T(8,128)(2,1)S(1)} %pad_maximum_fusion.refs_2_), channel_id=1, source_target_pairs={{0,4},{4,0},{8,12},{12,8},{1,5},{5,1},{9,13},{13,9},{2,6},{6,2},{1... | collective-permute-start | bytes 5308424 | tf_op jit(solution)/shard_map/ppermute | solution.py:545
  (38 other events, 54.4 us)

commit v2 on v1

--- a/solution.py
+++ b/solution.py
@@ -21,7 +21,8 @@
 masked = -1000000000.0
 f32 = jnp.float32
 bf16 = jnp.bfloat16
-VMEM = 48 * 1024 * 1024
+VMEM = 64 * 1024 * 1024
+SMALL = 16 * 1024 * 1024
 
 
 def constants():
@@ -115,26 +116,32 @@
     return jnp.where((lane >= 32 * h) & (lane < 32 * h + 32), x.astype(f32), 0.0).astype(bf16)
 
 
-def join_rows(refs):
-    return jnp.concatenate([ref[...] for ref in refs], axis=0)
-
-
-def write_pieces(pieces, refs):
+def join_rows(refs, part):
+    return jnp.concatenate([ref[part * QUAD : (part + 1) * QUAD] for ref in refs], axis=0)
+
+
+def write_pieces(first, second, refs):
     for i, ref in enumerate(refs):
-        ref[...] = pieces[i * QUAD : (i + 1) * QUAD].astype(bf16)
-
-
-def key_mask(valid, band, shift):
+        ref[:QUAD] = first[i * QUAD : (i + 1) * QUAD].astype(bf16)
+        ref[QUAD:] = second[i * QUAD : (i + 1) * QUAD].astype(bf16)
+
+
+def kind_of(info, k, band):
+    return info[4 + 16 * k + band]
+
+
+def key_mask(info, shift):
+    band = info[0]
     lane = lax.broadcasted_iota(jnp.int32, (1, KEYS), 1)
     column = lane & 127
-    total_rows = valid.shape[0]
+    total_rows = info.shape[0] - 36
     last = jnp.where(band == total_rows // 6 - 1, 1, 0)
     allowed = jnp.zeros((1, KEYS), jnp.int32)
     for r in range(6):
         at = band * 6 + r + shift
         at = jnp.where(at >= total_rows, at - total_rows, at)
         hit = (column >= 12 * r) & (column < 12 * r + 12)
-        allowed = allowed + jnp.where(hit, valid[at], 0)
+        allowed = allowed + jnp.where(hit, info[36 + at], 0)
     if shift:
         row = lax.broadcasted_iota(jnp.int32, (TOK, KEYS), 0)
         wide = lax.broadcasted_iota(jnp.int32, (TOK, KEYS), 1)
@@ -149,9 +156,9 @@
     return jnp.where(column < 72, mask, 2 * masked)
 
 
-def make_bias(k, where, types, valid, tables, spread, place, sort, bias_ref, turn_ref, row_ref):
+def make_bias(k, info, tables, spread, place, sort, bias_ref, turn_ref, row_ref):
     row_ref[...] = jnp.zeros(row_ref.shape, f32)
-    kind = types[k, where[0]]
+    kind = kind_of(info, k, info[0])
     for h in range(HEADS):
         row_ref[h : h + 1, :REL] = tables[0, h, pl.ds(kind, 1), :]
     wide_rows = row_ref[...]
@@ -168,7 +175,7 @@
                 ].astype(bf16)
         here = dot(place, turn_ref[...])
         total = here if total is None else total + here
-    mask = key_mask(valid, where[0], 3 * k)
+    mask = key_mask(info, 3 * k)
     for h in range(HEADS):
         bias_ref[:, h * KEYS : (h + 1) * KEYS] = total[:, h * KEYS : (h + 1) * KEYS] + mask
 
@@ -298,17 +305,18 @@
     return result, dh, dense, small
 
 
-def bias_kernel(where, types, valid, tables, spread, place, sort, bias_ref, turned, rows):
-    make_bias(1, where, types, valid, tables, spread[...], low(place), low(sort), bias_ref, turned, rows)
+def bias_kernel(info, tables, spread, place, sort, bias_ref, turned, rows):
+    make_bias(1, info, tables, spread[...], low(place), low(sort), bias_ref, turned, rows)
 
 
 def first_kernel(
-    where, types, valid, fields, scales, offsets, inward, inbias, outward, outbias, expand, upbias, narrow, downbias,
+    info, fields, upstream, scales, offsets, inward, inbias, outward, outbias, expand, upbias, narrow, downbias,
     tables, turn, cut, spread, place, sort,
-    q, k, v, p, mix, h1, y1, pa, pb, pc, pd, bias, turned, rows,
+    q, k, v, p, mix, h1, pa, pb, pc, pd, bias, turned, rows,
 ):
-    make_bias(0, where, types, valid, tables, spread[...], low(place), low(sort), bias, turned, rows)
-    x = dot(low(turn), fields[...])
+    make_bias(0, info, tables, spread[...], low(place), low(sort), bias, turned, rows)
+    order, route = low(turn), low(cut)
+    x = dot(order, fields[...])
     u = norm_fwd(x, scales[0, 0:1], offsets[0, 0:1])
     branch = attend_fwd(0, u, inward, inbias, outward, outbias, bias, q, k, v, p, mix)
     carried = (x + branch.astype(f32)).astype(bf16)
@@ -317,66 +325,46 @@
         carried.astype(f32), scales[0, 1:2], offsets[0, 1:2], expand[0].astype(bf16), upbias[0:1],
         narrow[0].astype(bf16), downbias[0:1],
     )
-    y1[...] = out
-    normed = norm_fwd(out.astype(f32), scales[1, 0:1], offsets[1, 0:1])
-    write_pieces(dot(low(cut), normed), (pa, pb, pc, pd))
+    cotangent = dot(order, upstream[...]).astype(bf16)
+    write_pieces(dot(route, out), dot(route, cotangent), (pa, pb, pc, pd))
 
 
 def second_kernel(
-    qa, qb, qc, qd, inward, inbias, outward, outbias, bias, join,
-    u_ref, q, k, v, p, mix, pa, pb, pc, pd,
+    qa, qb, qc, qd, scales, offsets, inward, inbias, outward, outbias, expand, upbias, narrow, downbias,
+    bias, join, spread, place, sort,
+    pack, pa, pb, pc, pd, q, k, v, p, mix, dbias, turned,
 ):
     route = low(join)
-    u = dot(route, join_rows((qa, qb, qc, qd))).astype(bf16)
-    u_ref[...] = u
+    pieces = (qa, qb, qc, qd)
+    y1 = dot(route, join_rows(pieces, 0))
+    cotangent = dot(route, join_rows(pieces, 1)).astype(bf16)
+    u = norm_fwd(y1, scales[1, 0:1], offsets[1, 0:1])
     branch = attend_fwd(1, u, inward, inbias, outward, outbias, bias, q, k, v, p, mix)
-    write_pieces(dot_tn(route, branch), (pa, pb, pc, pd))
-
-
-def tail_kernel(
-    qa, qb, qc, qd, y1, upstream, scales, offsets, expand, upbias, narrow, downbias, turn, cut,
-    result, dh_ref, dense_ref, small_ref, pa, pb, pc, pd,
+    h2 = (y1 + branch.astype(f32)).astype(bf16).astype(f32)
+    out, dh, dense, short = mlp_both(
+        h2, scales[1, 1:2], offsets[1, 1:2], expand[0].astype(bf16), upbias[1:2],
+        narrow[0].astype(bf16), downbias[1:2], cotangent, True,
+    )
+    for i, part in enumerate(dense):
+        put(pack, i * C, part)
+    du, table, small = attend_bwd(
+        dh, u, inward, outward, spread[...], low(place), low(sort), q, k, v, p, mix, pack, dbias, turned
+    )
+    dx, dgain, dshift = norm_bwd(y1, scales[1, 0:1], du.astype(bf16).astype(f32))
+    dy1 = (dh.astype(f32) + dx.astype(bf16).astype(f32)).astype(bf16)
+    put_rest(pack, table, short + small + [jnp.concatenate([dgain, dshift], axis=1)])
+    write_pieces(dot_tn(route, dy1), dot_tn(route, out), (pa, pb, pc, pd))
+
+
+def first_back_kernel(
+    qa, qb, qc, qd, fields, h1, scales, offsets, inward, outward, expand, upbias, narrow, downbias,
+    q, k, v, p, mix, turn, cut, spread, place, sort,
+    result, adjoint, pack, dbias, turned,
 ):
-    route = low(cut)
-    order = low(turn)
-    restored = dot_tn(route, join_rows((qa, qb, qc, qd)))
-    h2 = (y1[...].astype(f32) + restored).astype(bf16).astype(f32)
-    out, dh, dense, small = mlp_both(
-        h2, scales[1, 1:2], offsets[1, 1:2], expand[0].astype(bf16), upbias[1:2],
-        narrow[0].astype(bf16), downbias[1:2], dot(order, upstream[...]).astype(bf16), True,
-    )
-    result[...] = dot_tn(order, out).astype(bf16)
-    dh_ref[...] = dh
-    for i, part in enumerate(dense):
-        dense_ref[i * C : (i + 1) * C] = part.astype(bf16)
-    for i, row in enumerate(small):
-        small_ref[i : i + 1] = row
-    write_pieces(dot(route, dh), (pa, pb, pc, pd))
-
-
-def second_back_kernel(
-    qa, qb, qc, qd, dense, short, u, inward, outward, q, k, v, p, mix, join, spread, place, sort,
-    pack, pa, pb, pc, pd, dbias, turned,
-):
-    route = low(join)
-    dout = dot(route, join_rows((qa, qb, qc, qd))).astype(bf16)
-    du, table, small = attend_bwd(
-        dout, u[...], inward, outward, spread[...], low(place), low(sort), q, k, v, p, mix, pack, dbias, turned
-    )
-    put(pack, 0, dense[...])
-    put_rest(pack, table, [short[i : i + 1] for i in range(4)] + small)
-    write_pieces(dot_tn(route, du.astype(bf16)), (pa, pb, pc, pd))
-
-
-def first_back_kernel(
-    qa, qb, qc, qd, fields, dh2, y1, h1, scales, offsets, inward, outward, expand, upbias, narrow, downbias,
-    q, k, v, p, mix, turn, cut, spread, place, sort,
-    adjoint, pack, dbias, turned,
-):
-    order = low(turn)
-    dn = dot_tn(low(cut), join_rows((qa, qb, qc, qd)))
-    dx, dgain, dshift = norm_bwd(y1[...].astype(f32), scales[1, 0:1], dn)
-    dy1 = (dh2[...].astype(f32) + dx.astype(bf16).astype(f32)).astype(bf16)
+    order, route = low(turn), low(cut)
+    pieces = (qa, qb, qc, qd)
+    result[...] = dot_tn(order, dot_tn(route, join_rows(pieces, 1)).astype(bf16)).astype(bf16)
+    dy1 = dot_tn(route, join_rows(pieces, 0)).astype(bf16)
     _, dh1, dense, short = mlp_both(
         h1[...].astype(f32), scales[0, 1:2], offsets[0, 1:2], expand[0].astype(bf16), upbias[0:1],
         narrow[0].astype(bf16), downbias[0:1], dy1, False,
@@ -390,27 +378,27 @@
     )
     dx0, dgain0, dshift0 = norm_bwd(x, scales[0, 0:1], du.astype(bf16).astype(f32))
     adjoint[...] = dot_tn(order, (dh1.astype(f32) + dx0).astype(bf16)).astype(bf16)
-    pair = lambda x, y: jnp.concatenate([x, y], axis=1)
-    put_rest(pack, table, short + small + [pair(dgain0, dshift0), pair(dgain, dshift)])
-
-
-def core_kernel(where, first, second, got_first, got_second, *outs):
-    def deal(own, got):
-        for d, out in enumerate(outs):
-            at = (where[3] ^ d) * 2
-            out[...] = (own[pl.ds(at, 2)].astype(f32) + got[pl.ds(at, 2)].astype(f32)).astype(bf16)
-
-    @pl.when(where[1] == 0)
-    def _():
-        deal(first, got_first)
-
-    @pl.when(where[1] != 0)
-    def _():
-        deal(second, got_second)
-
-
-def samples_kernel(where, a, b, c, d, keep, send):
-    for out, at in ((keep, where[2]), (send, where[2] ^ 1)):
+    put_rest(pack, table, short + small + [jnp.concatenate([dgain0, dshift0], axis=1)])
+
+
+def core_kernel(info, first, second, got_first, got_second, a, b, c, d, own, got, sems):
+    for core, sources in ((0, (first, got_first)), (1, (second, got_second))):
+
+        @pl.when(info[1] == core)
+        def _(sources=sources):
+            copies = [pltpu.make_async_copy(m, n, sems.at[i]) for i, (m, n) in enumerate(zip(sources, (own, got)))]
+            for copy in copies:
+                copy.start()
+            for copy in copies:
+                copy.wait()
+
+    for n, out in enumerate((a, b, c, d)):
+        at = (info[3] ^ n) * 2
+        out[...] = (own[pl.ds(at, 2)].astype(f32) + got[pl.ds(at, 2)].astype(f32)).astype(bf16)
+
+
+def samples_kernel(info, a, b, c, d, keep, send):
+    for out, at in ((keep, info[2]), (send, info[2] ^ 1)):
         total = a[at].astype(f32) + b[at].astype(f32) + c[at].astype(f32) + d[at].astype(f32)
         out[...] = total.astype(bf16)
 
@@ -434,14 +422,14 @@
 
 
 def final_kernel(
-    where, types, own, got,
+    info, own, got,
     scales, offsets, inward, inbias, outward, outbias, expand, upbias, narrow, downbias, tables, dense, *, factor
 ):
     def routes(k):
         lane = lax.broadcasted_iota(jnp.int32, (1, 128), 1)
         kind = jnp.zeros((1, 128), jnp.int32)
         for e in range(16):
-            kind = kind + jnp.where((lane >> 3) == e, types[k, where[0] ^ e], 0)
+            kind = kind + jnp.where((lane >> 3) == e, kind_of(info, k, info[0] ^ e), 0)
         row = lax.broadcasted_iota(jnp.int32, (96, 128), 0)
         part = lax.broadcasted_iota(jnp.int32, (96, 128), 1) & 7
         head, match = row >> 4, (row & 15) == kind
@@ -455,7 +443,7 @@
         left = None
         small = []
         for chunk in range(8):
-            at = (where[3] ^ (chunk // 2), where[2] ^ (chunk % 2))
+            at = (info[3] ^ (chunk // 2), info[2] ^ (chunk % 2))
             dense[chunk * ROWS : (chunk + 1) * ROWS] = ref[at[0], at[1], :ROWS]
             small.append(ref[at[0], at[1], ROWS:CHUNK].astype(f32)[0:1] * factor)
             here = ref[at[0], at[1], CHUNK:]
@@ -485,46 +473,81 @@
         inbias[k : k + 1, : 2 * C] = small[4]
         inbias[k : k + 1, 2 * C :] = small[5][:, :C]
         outbias[k : k + 1] = small[5][:, C:]
-        if k == 0:
-            for i in range(2):
-                scales[i, 0:1] = small[6 + i][:, :C]
-                offsets[i, 0:1] = small[6 + i][:, C:]
-
-    @pl.when(where[1] == 0)
+        scales[k, 0:1] = small[6][:, :C]
+        offsets[k, 0:1] = small[6][:, C:]
+
+    @pl.when(info[1] == 0)
     def _():
         unpack(0, own)
         unpack(1, got)
 
-    @pl.when(where[1] != 0)
+    @pl.when(info[1] != 0)
     def _():
         unpack(0, got)
         unpack(1, own)
 
 
-def call(kernel, ins, outs, scratch=(), flops=0):
-    specs = []
-    for array, block in ins:
+def call(kernel, ins, outs, scratch=(), far_outs=0, limit=VMEM):
+    specs, fetched, slots = [], [], []
+    for array, block, far in ins:
         dims = array.ndim
+        shape = array.shape if block in (None, "smem", "raw") else (1,) + array.shape[1:]
         if block == "smem":
             specs.append(pl.BlockSpec(memory_space=pltpu.SMEM))
-        elif block is None:
+        elif block == "raw":
+            specs.append(pl.BlockSpec(memory_space=pltpu.HBM))
+        elif far:
+            specs.append(pl.BlockSpec(memory_space=pltpu.HBM))
+            fetched.append((len(specs) - 1, block))
+            slots.append(pltpu.VMEM(shape, array.dtype))
+        else:
             specs.append(pl.BlockSpec(array.shape, lambda i, dims=dims: (0,) * dims))
+    out_specs = []
+    for i, o in enumerate(outs):
+        if i < far_outs:
+            out_specs.append(pl.BlockSpec(memory_space=pltpu.HBM))
+            slots.append(pltpu.VMEM(o.shape, o.dtype))
         else:
-            specs.append(
-                pl.BlockSpec((1,) + array.shape[1:], lambda i, dims=dims, block=block: (block,) + (0,) * (dims - 1))
-            )
+            out_specs.append(pl.BlockSpec(o.shape, lambda i, dims=len(o.shape): (0,) * dims))
+
+    def wrapped(*refs):
+        in_refs, refs = list(refs[: len(ins)]), refs[len(ins) :]
+        out_refs, refs = list(refs[: len(outs)]), refs[len(outs) :]
+        own, refs = refs[: len(scratch)], refs[len(scratch) :]
+        copies = []
+        for n, (at, block) in enumerate(fetched):
+            source = in_refs[at] if block is None else in_refs[at].at[block : block + 1]
+            copies.append(pltpu.make_async_copy(source, refs[n], refs[-1].at[n]))
+            in_refs[at] = refs[n]
+        for copy in copies:
+            copy.start()
+        for copy in copies:
+            copy.wait()
+        targets = out_refs[:far_outs]
+        out_refs[:far_outs] = refs[len(fetched) : len(fetched) + far_outs]
+        kernel(*in_refs, *out_refs, *own)
+        copies = [
+            pltpu.make_async_copy(out_refs[n], targets[n], refs[-1].at[len(fetched) + n]) for n in range(far_outs)
+        ]
+        for copy in copies:
+            copy.start()
+        for copy in copies:
+            copy.wait()
+
     size = lambda s: math.prod(s.shape) * jnp.dtype(s.dtype).itemsize
-    moved = sum(size(o) for o in outs) + sum(size(a) // (1 if b in (None, "smem") else a.shape[0]) for a, b in ins)
+    moved = sum(size(o) for o in outs) + sum(size(a) for a, b, _ in ins)
+    if slots:
+        slots.append(pltpu.SemaphoreType.DMA((len(slots),)))
     return pl.pallas_call(
-        kernel,
+        wrapped,
         grid=(1,),
         in_specs=specs,
-        out_specs=[pl.BlockSpec(o.shape, lambda i, dims=len(o.shape): (0,) * dims) for o in outs],
+        out_specs=out_specs,
         out_shape=outs,
-        scratch_shapes=list(scratch),
-        compiler_params=pltpu.CompilerParams(vmem_limit_bytes=VMEM),
-        cost_estimate=pl.CostEstimate(flops=flops, bytes_accessed=moved, transcendentals=0),
-    )(*[array for array, _ in ins])
+        scratch_shapes=list(scratch) + slots,
+        compiler_params=pltpu.CompilerParams(vmem_limit_bytes=limit),
+        cost_estimate=pl.CostEstimate(flops=10**9, bytes_accessed=moved, transcendentals=0),
+    )(*[array for array, _, _ in ins])
 
 
 def send_pieces(pieces, step):
@@ -550,9 +573,9 @@
     tables, window_type, row_valid,
 ):
     lon = lax.axis_index("lon")
-    where = jnp.stack([lax.axis_index("lat"), lon % 2, lon // 2, lax.axis_index("rep")]).astype(jnp.int32)
+    place = jnp.stack([lax.axis_index("lat"), lon % 2, lon // 2, lax.axis_index("rep")]).astype(jnp.int32)
+    info = jnp.concatenate([place, window_type[0, 0], window_type[1, 0], row_valid])
     const = constants()
-    types = window_type[:, 0, :]
     levels, row_count, col_count = fields.shape[1:4]
     total_rows = row_valid.shape[0]
     x = fields[0].transpose(1, 2, 0, 3).reshape(TOK, C)
@@ -560,84 +583,71 @@
     narrow = jnp.swapaxes(narrow, 1, 2)
     tables = jnp.swapaxes(tables, 1, 2)
     of = jax.ShapeDtypeStruct
-    piece = [of((QUAD, C), bf16)] * 4
+    piece = [of((2 * QUAD, C), bf16)] * 4
     token = of((TOK, C), bf16)
     state = [token, of((KEYS, C), bf16), of((KEYS, C), bf16), of((HEADS, TOK, KEYS), bf16), token]
     pack = of((8, CHUNK, 2 * C), bf16)
     turned = pltpu.VMEM((192, 1536), bf16)
     dbias = pltpu.VMEM((TOK, 1536), bf16)
     rows = pltpu.VMEM((8, 3456), f32)
-    whole = lambda *arrays: [(m, None) for m in arrays]
-    fixed = lambda *names: [(const[name], None) for name in names]
-    scalars = [(where, "smem"), (types, "smem"), (row_valid, "smem")]
-
-    *state0, h1, y1, pa, pb, pc, pd = call(
+    near = lambda *arrays: [(m, None, False) for m in arrays]
+    far = lambda *arrays: [(m, None, True) for m in arrays]
+    block = lambda k, *arrays: [(m, k, True) for m in arrays]
+    raw = lambda *arrays: [(m, "raw", True) for m in arrays]
+    fixed = lambda *names: far(*[const[name] for name in names])
+    scalars = [(info, "smem", False)]
+
+    def weights(k):
+        return (
+            far(scales, offsets) + block(k, inward) + far(inbias) + block(k, outward) + far(outbias)
+            + block(k, expand) + far(upbias) + block(k, narrow) + far(downbias)
+        )
+
+    *state0, h1, pa, pb, pc, pd = call(
         first_kernel,
-        scalars
-        + whole(x, scales, offsets)
-        + [(inward, 0)] + whole(inbias) + [(outward, 0)] + whole(outbias)
-        + [(expand, 0)] + whole(upbias) + [(narrow, 0)] + whole(downbias)
-        + [(tables, 0)]
-        + fixed("turn", "cut", "spread", "place", "sort"),
-        state + [token, token] + piece,
+        scalars + far(x, cotangent) + weights(0) + block(0, tables) + fixed("turn", "cut", "spread", "place", "sort"),
+        state + [token] + piece,
         (pltpu.VMEM((TOK, 1536), f32), turned, rows),
-        10**9,
+        6,
     )
     pieces = send_pieces((pa, pb, pc, pd), -1)
     (bias1,) = call(
         bias_kernel,
-        scalars + [(tables, 1)] + fixed("spread", "place", "sort"),
+        scalars + block(1, tables) + fixed("spread", "place", "sort"),
         [of((TOK, 1536), f32)],
         (turned, rows),
-        10**9,
-    )
-    u1, *rest = call(
+    )
+    pack1, *pieces = call(
         second_kernel,
-        whole(*pieces) + [(inward, 1)] + whole(inbias) + [(outward, 1)] + whole(outbias, bias1) + fixed("join"),
-        [token] + state + piece,
-        (),
-        10**9,
-    )
-    state1, pieces = rest[:5], send_pieces(rest[5:], 1)
-    result, dh2, dense1, small1, *pieces = call(
-        tail_kernel,
-        whole(*pieces, y1, cotangent, scales, offsets)
-        + [(expand, 1)] + whole(upbias) + [(narrow, 1)] + whole(downbias)
-        + fixed("turn", "cut"),
-        [token, token, of((4 * C, 2 * C), bf16), of((8, 2 * C), f32)] + piece,
-        (),
-        10**9,
-    )
-    pieces = send_pieces(pieces, -1)
-    pack1, *pieces = call(
-        second_back_kernel,
-        whole(*pieces, dense1, small1, u1) + [(inward, 1), (outward, 1)] + whole(*state1)
-        + fixed("join", "spread", "place", "sort"),
+        far(*pieces) + weights(1) + far(bias1) + fixed("join", "spread", "place", "sort"),
         [pack] + piece,
-        (dbias, turned),
-        10**9,
+        [pltpu.VMEM(m.shape, m.dtype) for m in state] + [dbias, turned],
     )
     pieces = send_pieces(pieces, 1)
     got1 = swap(pack1, "lon", 1, 0)
-    adjoint, pack0 = call(
+    result, adjoint, pack0 = call(
         first_back_kernel,
-        whole(*pieces, x, dh2, y1, h1, scales, offsets) + [(inward, 0), (outward, 0), (expand, 0)] + whole(upbias)
-        + [(narrow, 0)] + whole(downbias, *state0) + fixed("turn", "cut", "spread", "place", "sort"),
-        [token, pack],
+        far(*pieces, x, h1, scales, offsets) + block(0, inward, outward, expand) + far(upbias)
+        + block(0, narrow) + far(downbias, *state0) + fixed("turn", "cut", "spread", "place", "sort"),
+        [token, token, pack],
         (dbias, turned),
-        10**9,
     )
     got0 = swap(pack0, "lon", 1, 1)
 
     part = of((2, CHUNK, 2 * C), bf16)
-    a, b, c, d = call(core_kernel, scalars[:1] + whole(pack0, pack1, got0, got1), [part] * 4)
+    a, b, c, d = call(
+        core_kernel,
+        scalars + raw(pack0, pack1, got0, got1),
+        [part] * 4,
+        [pltpu.VMEM(pack.shape, bf16)] * 2 + [pltpu.SemaphoreType.DMA((2,))],
+    )
     b, c, d = (swap(m, "rep", i + 1) for i, m in enumerate((b, c, d)))
     chunk = of((CHUNK, 2 * C), bf16)
-    keep, give = call(samples_kernel, scalars[:1] + whole(a, b, c, d), [chunk, chunk])
-    (a,) = call(pair_kernel, whole(keep, swap(give, "lon", 2)), [chunk])
+    keep, give = call(samples_kernel, scalars + near(a, b, c, d), [chunk, chunk], limit=SMALL)
+    (a,) = call(pair_kernel, near(keep, swap(give, "lon", 2)), [chunk], limit=SMALL)
     for step, height in ((1, CHUNK + 32), (4, CHUNK + 128)):
         others = [swap(a, "lat", step * i) for i in (1, 2, 3)]
-        (a,) = call(band_kernel, whole(a, *others), [of((height, 2 * C), bf16)])
+        (a,) = call(band_kernel, near(a, *others), [of((height, 2 * C), bf16)], limit=SMALL)
     a = jnp.stack([a, swap(a, "lon", 2)])
     a = jnp.stack([a] + [swap(a, "rep", i) for i in (1, 2, 3)])
     got = swap(a, "lon", 1)
@@ -654,9 +664,10 @@
     joined = list(
         call(
             finish,
-            scalars[:2] + whole(a, got),
+            scalars + near(a, got),
             [of(s, f32) for s in outs],
             (pltpu.VMEM((8 * ROWS, 2 * C), bf16),),
+            limit=2 * SMALL,
         )
     )
     joined[8] = jnp.swapaxes(joined[8], 1, 2)

time: 181 us -> 148 us (0.82)
  local copies, waits for them, and re-layouts: 32.4 us -> 9.9 us
  waiting for transfers between devices: 73.5 us -> 55.6 us
  Pallas kernels: 27.7 us -> 38.4 us
  starting transfers between devices: 44.8 us -> 42.7 us
    unnamed x146 -> x6, local copies, waits for them, and re-layouts: 26.7 us -> 1.63 us
    ppermute x17, waiting for transfers between devices: 60.6 us -> 49.4 us  [swap(): lax.ppermute(array, axis, [(i, i ^ distance) for i in devices if only is...]
    pallas_call x12 -> x10, Pallas kernels: 27.7 us -> 38.4 us  [call(): pl.pallas_call(wrapped, grid=(1,), in_specs=specs, out_specs=out_specs, o...]
    ppermute x17, starting transfers between devices: 22.6 us -> 28.9 us  [swap(): lax.ppermute(array, axis, [(i, i ^ distance) for i in devices if only is...]
    ppermute x4 -> x2, waiting for transfers between devices: 6.96 us -> 2.48 us  [send_pieces(): lax.ppermute(pieces[3], ('lat', 'lon'), both)]
    ppermute x4 -> x2, starting transfers between devices: 4.83 us -> 1.37 us  [send_pieces(): lax.ppermute(pieces[3], ('lat', 'lon'), both)]
    ppermute x4 -> x2, starting transfers between devices: 13.1 us -> 10.5 us  [send_pieces(): lax.ppermute(pieces[1], 'lat', rows)]
    ppermute x4 -> x2, starting transfers between devices: 4.29 us -> 1.93 us  [send_pieces(): lax.ppermute(pieces[2], 'lon', cols)]
  transfers between devices with their start and end apart: 29 -> 23, of which waited for: 21 -> 17; matrix products, arithmetic and copies ran while one was open for 3% -> 2% of each run, Pallas kernels for 4% -> 8%
where the time goes in v2:
time: 148 us
  waiting for transfers between devices  55.6 us (38%)
  starting transfers between devices  42.7 us (29%)
  Pallas kernels  38.4 us (26%)
  local copies, waits for them, and re-layouts  9.9 us (7%)
    ppermute x17, waiting for transfers between devices, swap(): lax.ppermute(array, axis, [(i, i ^ distance) for i in devices if only is...  49.4 us
    pallas_call x10, Pallas kernels, call(): pl.pallas_call(wrapped, grid=(1,), in_specs=specs, out_specs=out_specs, o...  38.4 us
    ppermute x17, starting transfers between devices, swap(): lax.ppermute(array, axis, [(i, i ^ distance) for i in devices if only is...  28.9 us
    ppermute x2, starting transfers between devices, send_pieces(): lax.ppermute(pieces[1], 'lat', rows)  10.5 us
    ppermute x2, waiting for transfers between devices, send_pieces(): lax.ppermute(pieces[1], 'lat', rows)  3.67 us
    reshape x2, local copies, waits for them, and re-layouts, body(): m.reshape(row_count, col_count, levels, C).transpose(2, 0, 1, 3)[None]  3.12 us
  transfers between devices with their start and end apart: 23, of which 17 were waited for; matrix products, arithmetic and copies ran while one was open for 2% of the time, Pallas kernels for 8%

profile of v2, /device:TPU:1, one launch (start us, length us, event | category | flops | bytes accessed | tf_op | source)
XLA Modules:
  0.0 147.7 jit_solution(9106496288464039690)
XLA Ops:
  0.7 0.7 slice_bitcast_fusion
  1.3 1.6 %reshape.38.refs_1_.refs_4_ = bf16[144,192]{1,0:T(8,128)(2,1)} reshape(bf16[6,12,2,192]{3,2,1,0:T(2,128)(2,1)} %bitcast.41) | data formatting | bytes 110592 | tf_op jit(solution)/shard_map/reshape | solution.py:581
  2.9 1.6 %reshape.39.refs_2_ = bf16[144,192]{1,0:T(8,128)(2,1)} reshape(bf16[6,12,2,192]{3,2,1,0:T(2,128)(2,1)} %bitcast.42) | data formatting | bytes 110592 | tf_op jit(solution)/shard_map/reshape | solution.py:582
  4.5 1.3 concatenate.3.refs_0_
  5.8 8.8 %shard_map.300 = (bf16[144,192]{1,0:T(8,128)(2,1)}, bf16[256,192]{1,0:T(8,128)(2,1)}, bf16[256,192]{1,0:T(8,128)(2,1)}, bf16[6,144,256]{2,1,0:T(8,128)(2,1)}, bf...) custom-call(s32[132]{0:T(256)} %concatenate.3.refs_0_, ...), custom_call_target="tpu_custom_call" | custom-call | flops 1000000000 | bytes 8403984 | tf_op jit(solution)/shard_map/pallas_call | solution.py:541
  14.6 8.9 %collective-permute-start = (bf16[96,192]{1,0:T(8,128)(2,1)}, bf16[96,192]{1,0:T(8,128)(2,1)}, u32[]{:S(2)}, u32[]{:S(2)}) collective-permute-start(bf16[96,192]{1,0:T(8,128)(2,1)} %get-tuple-element.49), channel_id=1, source_target_pairs={{0,240},{16,0},{32,16},{48,32},{64,48},{80,64},{96,80},{112,96},{1... | collective-permute-start | bytes 110600 | tf_op jit(solution)/shard_map/ppermute | solution.py:560
  23.5 1.0 collective-permute-start.1
  24.5 1.4 collective-permute-start.2
  25.9 5.0 %shard_map.301.refs_14_ = f32[144,1536]{1,0:T(8,128)} custom-call(s32[132]{0:T(256)} %concatenate.3.refs_0_, f32[2,6,16,3312]{3,2,1,0:T(8,128)} %bitcast.36, bf16[256,1536]{1,0:T(8,128)(2,1)} %constant.53.clone.refs_16_.refs_2_.refs_21_, f32[144,192]{1,0:T(8,128)} %constant.51.clone.refs_17_.refs_3_.refs_22_, f32[192,192]{1,0:T(8,128)} %constant.52.clone.refs_18_.refs_4_.refs_23_), custom_call_target="tpu_custom_call" | custom-call | flops 1000000000 | bytes 4473360 | tf_op jit(solution)/shard_map/pallas_call | solution.py:541
  30.9 0.0 collective-permute-done.refs_1_
  30.9 0.0 collective-permute-done.1.refs_2_
  30.9 0.0 collective-permute-done.2.refs_3_
  30.9 9.2 %shard_map.302 = (bf16[8,160,384]{2,1,0:T(8,128)(2,1)}, bf16[96,192]{1,0:T(8,128)(2,1)}, bf16[96,192]{1,0:T(8,128)(2,1)}, bf16[96,192]{1,0:T(8,128)(2,1)}, bf16[96,192]{1,0:T(8,128)(2,1)}) custom-call(bf16[96,192]{1,0:T(8,128)(2,1)} %get-tuple-element.48.refs_0_, bf16[96,192]{1,0:T(8,128)(2,1)} %collective-permute-done.refs_1_, ...), custom_call_target="tpu_custom_call" | custom-call | flops 1000000000 | bytes 6876672 | tf_op jit(solution)/shard_map/pallas_call | solution.py:541
  40.1 1.6 %collective-permute-start.3 = (bf16[96,192]{1,0:T(8,128)(2,1)}, bf16[96,192]{1,0:T(8,128)(2,1)}, u32[]{:S(2)}, u32[]{:S(2)}) collective-permute-start(bf16[96,192]{1,0:T(8,128)(2,1)} %get-tuple-element.53), channel_id=1, source_target_pairs={{0,16},{16,32},{32,48},{48,64},{64,80},{80,96},{96,112},{112,128},... | collective-permute-start | bytes 110600 | tf_op jit(solution)/shard_map/ppermute | solution.py:560
  41.7 1.0 collective-permute-start.4
  42.7 0.0 collective-permute-start.5
  42.7 1.3 collective-permute-start.7
  44.0 3.7 %collective-permute-done.3.refs_1_ = bf16[96,192]{1,0:T(8,128)(2,1)} collective-permute-done((bf16[96,192]{1,0:T(8,128)(2,1)}, bf16[96,192]{1,0:T(8,128)(2,1)}, u32[]{:S(2)}, u32[]{:S(2)}) %collective-permute-start.3) | collective-permute-done | bytes 36896 | tf_op jit(solution)/shard_map/ppermute | solution.py:560
  47.6 0.0 collective-permute-done.4.refs_2_
  47.7 2.5 %collective-permute-done.5.refs_3_ = bf16[96,192]{1,0:T(8,128)(2,1)} collective-permute-done((bf16[96,192]{1,0:T(8,128)(2,1)}, bf16[96,192]{1,0:T(8,128)(2,1)}, u32[]{:S(2)}, u32[]{:S(2)}) %collective-permute-start.5) | collective-permute-done | bytes 36896 | tf_op jit(solution)/shard_map/ppermute | solution.py:562
  50.1 7.1 %shard_map.303 = (bf16[144,192]{1,0:T(8,128)(2,1)}, bf16[144,192]{1,0:T(8,128)(2,1)}, bf16[8,160,384]{2,1,0:T(8,128)(2,1)}) custom-call(bf16[96,192]{1,0:T(8,128)(2,1)} %get-tuple-element.52.refs_0_, bf16[96,192]{1,0:T(8,128)(2,1)} %collective-permute-done.3.refs_1_, bf16[96,192]{1,0:T(8,128)(2,1)} %collective-permute-done.4.refs_2_, ...), custom_call_target="tpu_custom_call" | custom-call | flops 1000000000 | bytes 6892032 | tf_op jit(solution)/shard_map/pallas_call | solution.py:541
  57.2 2.2 %collective-permute-start.6 = (bf16[8,160,384]{2,1,0:T(8,128)(2,1)}, bf16[8,160,384]{2,1,0:T(8,128)(2,1)}, u32[]{:S(2)}, u32[]{:S(2)}) collective-permute-start(bf16[8,160,384]{2,1,0:T(8,128)(2,1)} %get-tuple-element.64.refs_1_), channel_id=1, source_target_pairs={{4,0},{12,8},{5,1},{13,9},{6,2},{14,10},{7,3},{15,11},{20,16},{28,... | collective-permute-start | bytes 2949128 | tf_op jit(solution)/shard_map/ppermute | solution.py:568
  59.5 1.6 %collective-permute-done.6.refs_3_ = bf16[8,160,384]{2,1,0:T(8,128)(2,1)} collective-permute-done((bf16[8,160,384]{2,1,0:T(8,128)(2,1)}, bf16[8,160,384]{2,1,0:T(8,128)(2,1)}, u32[]{:S(2)}, u32[]{:S(2)}) %collective-permute-start.6) | collective-permute-done | bytes 983072 | tf_op jit(solution)/shard_map/ppermute | solution.py:568
  61.1 3.2 %shard_map.304 = (bf16[2,160,384]{2,1,0:T(8,128)(2,1)}, bf16[2,160,384]{2,1,0:T(8,128)(2,1)}, bf16[2,160,384]{2,1,0:T(8,128)(2,1)}, bf16[2,160,384]{2,1,0:T(8,128)(2,1)}) custom-call(s32[132]{0:T(256)} %concatenate.3.refs_0_, bf16[8,160,384]{2,1,0:T(8,128)(2,1)} %get-tuple-element.64.refs_1_, bf16[8,160,384]{2,1,0:T(8,128)(2,1)} %get-tuple-element.65.refs_2_, ...), custom_call_target="tpu_custom_call" | custom-call | flops 1000000000 | bytes 4915728 | tf_op jit(solution)/shard_map/pallas_call | solution.py:541
  64.3 1.4 collective-permute-start.8
  65.7 2.6 %collective-permute-start.9 = (bf16[2,160,384]{2,1,0:T(8,128)(2,1)}, bf16[2,160,384]{2,1,0:T(8,128)(2,1)S(1)}, u32[]{:S(2)}, u32[]{:S(2)}) collective-permute-start(bf16[2,160,384]{2,1,0:T(8,128)(2,1)} %get-tuple-element.68), channel_id=1, source_target_pairs={{0,2},{1,3},{2,0},{3,1},{4,6},{5,7},{6,4},{7,5},{8,10},{9,11},{10,... | collective-permute-start | bytes 737288 | tf_op jit(solution)/shard_map/ppermute | solution.py:568
  68.3 0.0 collective-permute-start.10
  68.3 3.5 %collective-permute-done.8.refs_2_ = bf16[2,160,384]{2,1,0:T(8,128)(2,1)S(1)} collective-permute-done((bf16[2,160,384]{2,1,0:T(8,128)(2,1)}, bf16[2,160,384]{2,1,0:T(8,128)(2,1)S(1)}, u32[]{:S(2)}, u32[]{:S(2)}) %collective-permute-start.8) | collective-permute-done | bytes 245792 | tf_op jit(solution)/shard_map/ppermute | solution.py:568
  71.8 7.7 %collective-permute-done.9.refs_3_ = bf16[2,160,384]{2,1,0:T(8,128)(2,1)S(1)} collective-permute-done((bf16[2,160,384]{2,1,0:T(8,128)(2,1)}, bf16[2,160,384]{2,1,0:T(8,128)(2,1)S(1)}, u32[]{:S(2)}, u32[]{:S(2)}) %collective-permute-start.9) | collective-permute-done | bytes 245792 | tf_op jit(solution)/shard_map/ppermute | solution.py:568
  79.5 2.0 %collective-permute-done.10.refs_4_ = bf16[2,160,384]{2,1,0:T(8,128)(2,1)S(1)} collective-permute-done((bf16[2,160,384]{2,1,0:T(8,128)(2,1)}, bf16[2,160,384]{2,1,0:T(8,128)(2,1)S(1)}, u32[]{:S(2)}, u32[]{:S(2)}) %collective-permute-start.10) | collective-permute-done | bytes 245792 | tf_op jit(solution)/shard_map/ppermute | solution.py:568
  81.5 0.7 copy-done
  82.2 0.9 copy-done.2
  83.1 0.7 shard_map.305
  83.8 0.4 collective-permute-start.11
  84.2 3.4 %collective-permute-done.11.refs_1_ = bf16[160,384]{1,0:T(8,128)(2,1)S(1)} collective-permute-done((bf16[160,384]{1,0:T(8,128)(2,1)S(1)}, bf16[160,384]{1,0:T(8,128)(2,1)S(1)}, u32[]{:S(2)}, u32[]{:S(2)}) %collective-permute-start.11) | collective-permute-done | bytes 122912 | tf_op jit(solution)/shard_map/ppermute | solution.py:568
  87.7 0.1 collective-permute-start.14
  87.8 0.2 collective-permute-start.13
  87.9 4.0 %collective-permute-start.12 = (bf16[160,384]{1,0:T(8,128)(2,1)S(1)}, bf16[160,384]{1,0:T(8,128)(2,1)S(1)}, u32[]{:S(2)}, u32[]{:S(2)}) collective-permute-start(bf16[160,384]{1,0:T(8,128)(2,1)S(1)} %shard_map.306.refs_0_), channel_id=1, source_target_pairs={{0,16},{16,0},{32,48},{48,32},{64,80},{80,64},{96,112},{112,96},{1... | collective-permute-start | bytes 368648 | tf_op jit(solution)/shard_map/ppermute | solution.py:568
  91.9 2.1 %collective-permute-done.14.refs_3_ = bf16[160,384]{1,0:T(8,128)(2,1)S(1)} collective-permute-done((bf16[160,384]{1,0:T(8,128)(2,1)S(1)}, bf16[160,384]{1,0:T(8,128)(2,1)S(1)}, u32[]{:S(2)}, u32[]{:S(2)}) %collective-permute-start.14) | collective-permute-done | bytes 122912 | tf_op jit(solution)/shard_map/ppermute | solution.py:568
  94.0 0.0 collective-permute-done.13.refs_2_
  94.0 1.2 collective-permute-done.12.refs_1_
  95.2 0.1 shard_map.307.refs_0_
  95.3 0.3 collective-permute-start.17
  95.6 2.6 %collective-permute-start.16 = (bf16[192,384]{1,0:T(8,128)(2,1)S(1)}, bf16[192,384]{1,0:T(8,128)(2,1)S(1)}, u32[]{:S(2)}, u32[]{:S(2)}) collective-permute-start(bf16[192,384]{1,0:T(8,128)(2,1)S(1)} %shard_map.307.refs_0_), channel_id=1, source_target_pairs={{0,128},{16,144},{32,160},{48,176},{64,192},{80,208},{96,224},{112... | collective-permute-start | bytes 442376 | tf_op jit(solution)/shard_map/ppermute | solution.py:568
  98.2 2.8 %collective-permute-start.15 = (bf16[192,384]{1,0:T(8,128)(2,1)S(1)}, bf16[192,384]{1,0:T(8,128)(2,1)S(1)}, u32[]{:S(2)}, u32[]{:S(2)}) collective-permute-start(bf16[192,384]{1,0:T(8,128)(2,1)S(1)} %shard_map.307.refs_0_), channel_id=1, source_target_pairs={{0,64},{16,80},{32,96},{48,112},{64,0},{80,16},{96,32},{112,48},{1... | collective-permute-start | bytes 442376 | tf_op jit(solution)/shard_map/ppermute | solution.py:568
  101.0 0.5 collective-permute-done.17.refs_3_
  101.6 2.4 %collective-permute-done.16.refs_2_ = bf16[192,384]{1,0:T(8,128)(2,1)S(1)} collective-permute-done((bf16[192,384]{1,0:T(8,128)(2,1)S(1)}, bf16[192,384]{1,0:T(8,128)(2,1)S(1)}, u32[]{:S(2)}, u32[]{:S(2)}) %collective-permute-start.16) | collective-permute-done | bytes 147488 | tf_op jit(solution)/shard_map/ppermute | solution.py:568
  103.9 3.7 %collective-permute-done.15.refs_1_ = bf16[192,384]{1,0:T(8,128)(2,1)S(1)} collective-permute-done((bf16[192,384]{1,0:T(8,128)(2,1)S(1)}, bf16[192,384]{1,0:T(8,128)(2,1)S(1)}, u32[]{:S(2)}, u32[]{:S(2)}) %collective-permute-start.15) | collective-permute-done | bytes 147488 | tf_op jit(solution)/shard_map/ppermute | solution.py:568
  107.6 0.1 shard_map.308
  107.7 5.1 %collective-permute-start.18 = (bf16[288,384]{1,0:T(8,128)(2,1)S(1)}, bf16[288,384]{1,0:T(8,128)(2,1)S(1)}, u32[]{:S(2)}, u32[]{:S(2)}) collective-permute-start(bf16[288,384]{1,0:T(8,128)(2,1)S(1)} %shard_map.308), channel_id=1, source_target_pairs={{0,8},{4,12},{8,0},{12,4},{1,9},{5,13},{9,1},{13,5},{2,10},{6,14},... | collective-permute-start | bytes 663560 | tf_op jit(solution)/shard_map/ppermute | solution.py:568
  112.7 3.3 %collective-permute-done.18 = bf16[288,384]{1,0:T(8,128)(2,1)S(1)} collective-permute-done((bf16[288,384]{1,0:T(8,128)(2,1)S(1)}, bf16[288,384]{1,0:T(8,128)(2,1)S(1)}, u32[]{:S(2)}, u32[]{:S(2)}) %collective-permute-start.18) | collective-permute-done | bytes 221216 | tf_op jit(solution)/shard_map/ppermute | solution.py:568
  116.1 0.1 fusion
  116.2 0.1 collective-permute-start.20
  116.3 0.9 collective-permute-start.19
  117.1 2.4 %collective-permute-start.21 = (bf16[2,288,384]{2,1,0:T(8,128)(2,1)S(1)}, bf16[2,288,384]{2,1,0:T(8,128)(2,1)S(1)}, u32[]{:S(2)}, u32[]{:S(2)}) collective-permute-start(bf16[2,288,384]{2,1,0:T(8,128)(2,1)S(1)} %get-tuple-element.84), channel_id=1, source_target_pairs={{0,3},{1,2},{2,1},{3,0},{4,7},{5,6},{6,5},{7,4},{8,11},{9,10},{10,... | collective-permute-start | bytes 1327112 | tf_op jit(solution)/shard_map/ppermute | solution.py:568
  119.5 5.5 %collective-permute-done.20 = bf16[2,288,384]{2,1,0:T(8,128)(2,1)S(1)} collective-permute-done((bf16[2,288,384]{2,1,0:T(8,128)(2,1)S(1)}, bf16[2,288,384]{2,1,0:T(8,128)(2,1)S(1)}, u32[]{:S(2)}, u32[]{:S(2)}) %collective-permute-start.20) | collective-permute-done | bytes 442400 | tf_op jit(solution)/shard_map/ppermute | solution.py:568
  125.0 6.3 %collective-permute-done.19 = bf16[2,288,384]{2,1,0:T(8,128)(2,1)S(1)} collective-permute-done((bf16[2,288,384]{2,1,0:T(8,128)(2,1)S(1)}, bf16[2,288,384]{2,1,0:T(8,128)(2,1)S(1)}, u32[]{:S(2)}, u32[]{:S(2)}) %collective-permute-start.19) | collective-permute-done | bytes 442400 | tf_op jit(solution)/shard_map/ppermute | solution.py:568
  131.3 6.0 %collective-permute-done.21 = bf16[2,288,384]{2,1,0:T(8,128)(2,1)S(1)} collective-permute-done((bf16[2,288,384]{2,1,0:T(8,128)(2,1)S(1)}, bf16[2,288,384]{2,1,0:T(8,128)(2,1)S(1)}, u32[]{:S(2)}, u32[]{:S(2)}) %collective-permute-start.21) | collective-permute-done | bytes 442400 | tf_op jit(solution)/shard_map/ppermute | solution.py:568
  137.3 0.3 pad_maximum_fusion.refs_1_
  137.6 2.6 %collective-permute-start.22 = (bf16[4,2,288,384]{3,2,1,0:T(8,128)(2,1)S(1)}, bf16[4,2,288,384]{3,2,1,0:T(8,128)(2,1)S(1)}, u32[]{:S(2)}, u32[]{:S(2)}) collective-permute-start(bf16[4,2,288,384]{3,2,1,0:T(8,128)(2,1)S(1)} %pad_maximum_fusion.refs_1_), channel_id=1, source_target_pairs={{0,4},{4,0},{8,12},{12,8},{1,5},{5,1},{9,13},{13,9},{2,6},{6,2},{1... | collective-permute-start | bytes 5308424 | tf_op jit(solution)/shard_map/ppermute | solution.py:568
  140.2 1.6 %reshape.40 = bf16[6,12,2,192]{3,2,1,0:T(2,128)(2,1)} reshape(bf16[144,192]{1,0:T(8,128)(2,1)} %get-tuple-element.62) | data formatting | bytes 110592 | tf_op jit(solution)/shard_map/reshape | solution.py:675
  141.7 1.6 %reshape.41 = bf16[6,12,2,192]{3,2,1,0:T(2,128)(2,1)} reshape(bf16[144,192]{1,0:T(8,128)(2,1)} %get-tuple-element.63) | data formatting | bytes 110592 | tf_op jit(solution)/shard_map/reshape | solution.py:675
  143.3 0.2 collective-permute-done.22.refs_2_
  143.5 4.2 %shard_map.309 = (f32[2,2,192]{2,1,0:T(2,128)}, f32[2,2,192]{2,1,0:T(2,128)}, f32[2,192,576]{2,1,0:T(8,128)}, f32[2,576]{1,0:T(2,128)}, f32[2,192,192]{2,1,0:T(8...) custom-call(s32[132]{0:T(256)S(1)} %copy-done.1, ...), custom_call_target="tpu_custom_call" | custom-call | flops 1000000000 | bytes 9642000 | tf_op jit(solution)/shard_map/pallas_call | solution.py:541
  (6 shorter events, 0.0 us)
Async XLA Ops:
  14.6 16.3 %collective-permute-start = (bf16[96,192]{1,0:T(8,128)(2,1)}, bf16[96,192]{1,0:T(8,128)(2,1)}, u32[]{:S(2)}, u32[]{:S(2)}) collective-permute-start(bf16[96,192]{1,0:T(8,128)(2,1)} %get-tuple-element.49), channel_id=1, source_target_pairs={{0,240},{16,0},{32,16},{48,32},{64,48},{80,64},{96,80},{112,96},{1... | collective-permute-start | bytes 110600 | tf_op jit(solution)/shard_map/ppermute | solution.py:560
  23.5 7.4 %collective-permute-start.1 = (bf16[96,192]{1,0:T(8,128)(2,1)}, bf16[96,192]{1,0:T(8,128)(2,1)}, u32[]{:S(2)}, u32[]{:S(2)}) collective-permute-start(bf16[96,192]{1,0:T(8,128)(2,1)} %get-tuple-element.50), channel_id=1, source_target_pairs={{0,12},{4,0},{8,4},{12,8},{1,13},{5,1},{9,5},{13,9},{2,14},{6,2},{... | collective-permute-start | bytes 110600 | tf_op jit(solution)/shard_map/ppermute | solution.py:561
  24.5 6.4 %collective-permute-start.2 = (bf16[96,192]{1,0:T(8,128)(2,1)}, bf16[96,192]{1,0:T(8,128)(2,1)}, u32[]{:S(2)}, u32[]{:S(2)}) collective-permute-start(bf16[96,192]{1,0:T(8,128)(2,1)} %get-tuple-element.51), channel_id=1, source_target_pairs={{0,252},{4,240},{8,244},{12,248},{16,12},{20,0},{24,4},{28,8},{32,... | collective-permute-start | bytes 110600 | tf_op jit(solution)/shard_map/ppermute | solution.py:562
  40.1 7.5 %collective-permute-start.3 = (bf16[96,192]{1,0:T(8,128)(2,1)}, bf16[96,192]{1,0:T(8,128)(2,1)}, u32[]{:S(2)}, u32[]{:S(2)}) collective-permute-start(bf16[96,192]{1,0:T(8,128)(2,1)} %get-tuple-element.53), channel_id=1, source_target_pairs={{0,16},{16,32},{32,48},{48,64},{64,80},{80,96},{96,112},{112,128},... | collective-permute-start | bytes 110600 | tf_op jit(solution)/shard_map/ppermute | solution.py:560
  41.7 5.9 %collective-permute-start.4 = (bf16[96,192]{1,0:T(8,128)(2,1)}, bf16[96,192]{1,0:T(8,128)(2,1)}, u32[]{:S(2)}, u32[]{:S(2)}) collective-permute-start(bf16[96,192]{1,0:T(8,128)(2,1)} %get-tuple-element.54), channel_id=1, source_target_pairs={{0,4},{4,8},{8,12},{12,0},{1,5},{5,9},{9,13},{13,1},{2,6},{6,10},{... | collective-permute-start | bytes 110600 | tf_op jit(solution)/shard_map/ppermute | solution.py:561
  42.7 7.4 %collective-permute-start.5 = (bf16[96,192]{1,0:T(8,128)(2,1)}, bf16[96,192]{1,0:T(8,128)(2,1)}, u32[]{:S(2)}, u32[]{:S(2)}) collective-permute-start(bf16[96,192]{1,0:T(8,128)(2,1)} %get-tuple-element.55), channel_id=1, source_target_pairs={{0,20},{4,24},{8,28},{12,16},{16,36},{20,40},{24,44},{28,32},{32,5... | collective-permute-start | bytes 110600 | tf_op jit(solution)/shard_map/ppermute | solution.py:562
  42.7 16.8 %collective-permute-start.7 = (bf16[8,160,384]{2,1,0:T(8,128)(2,1)}, bf16[8,160,384]{2,1,0:T(8,128)(2,1)}, u32[]{:S(2)}, u32[]{:S(2)}) collective-permute-start(bf16[8,160,384]{2,1,0:T(8,128)(2,1)} %get-tuple-element.65.refs_2_), channel_id=1, source_target_pairs={{0,4},{8,12},{1,5},{9,13},{2,6},{10,14},{3,7},{11,15},{16,20},{24,... | collective-permute-start | bytes 2949128 | tf_op jit(solution)/shard_map/ppermute | solution.py:568
  57.2 3.8 %collective-permute-start.6 = (bf16[8,160,384]{2,1,0:T(8,128)(2,1)}, bf16[8,160,384]{2,1,0:T(8,128)(2,1)}, u32[]{:S(2)}, u32[]{:S(2)}) collective-permute-start(bf16[8,160,384]{2,1,0:T(8,128)(2,1)} %get-tuple-element.64.refs_1_), channel_id=1, source_target_pairs={{4,0},{12,8},{5,1},{13,9},{6,2},{14,10},{7,3},{15,11},{20,16},{28,... | collective-permute-start | bytes 2949128 | tf_op jit(solution)/shard_map/ppermute | solution.py:568
  64.3 7.5 %collective-permute-start.8 = (bf16[2,160,384]{2,1,0:T(8,128)(2,1)}, bf16[2,160,384]{2,1,0:T(8,128)(2,1)S(1)}, u32[]{:S(2)}, u32[]{:S(2)}) collective-permute-start(bf16[2,160,384]{2,1,0:T(8,128)(2,1)} %get-tuple-element.67), channel_id=1, source_target_pairs={{0,1},{1,0},{2,3},{3,2},{4,5},{5,4},{6,7},{7,6},{8,9},{9,8},{10,11... | collective-permute-start | bytes 737288 | tf_op jit(solution)/shard_map/ppermute | solution.py:568
  65.7 13.8 %collective-permute-start.9 = (bf16[2,160,384]{2,1,0:T(8,128)(2,1)}, bf16[2,160,384]{2,1,0:T(8,128)(2,1)S(1)}, u32[]{:S(2)}, u32[]{:S(2)}) collective-permute-start(bf16[2,160,384]{2,1,0:T(8,128)(2,1)} %get-tuple-element.68), channel_id=1, source_target_pairs={{0,2},{1,3},{2,0},{3,1},{4,6},{5,7},{6,4},{7,5},{8,10},{9,11},{10,... | collective-permute-start | bytes 737288 | tf_op jit(solution)/shard_map/ppermute | solution.py:568
  68.3 13.2 %collective-permute-start.10 = (bf16[2,160,384]{2,1,0:T(8,128)(2,1)}, bf16[2,160,384]{2,1,0:T(8,128)(2,1)S(1)}, u32[]{:S(2)}, u32[]{:S(2)}) collective-permute-start(bf16[2,160,384]{2,1,0:T(8,128)(2,1)} %get-tuple-element.69), channel_id=1, source_target_pairs={{0,3},{1,2},{2,1},{3,0},{4,7},{5,6},{6,5},{7,4},{8,11},{9,10},{10,... | collective-permute-start | bytes 737288 | tf_op jit(solution)/shard_map/ppermute | solution.py:568
  81.5 0.7 copy-start
  82.2 0.9 copy-start.2
  83.8 3.8 %collective-permute-start.11 = (bf16[160,384]{1,0:T(8,128)(2,1)S(1)}, bf16[160,384]{1,0:T(8,128)(2,1)S(1)}, u32[]{:S(2)}, u32[]{:S(2)}) collective-permute-start(bf16[160,384]{1,0:T(8,128)(2,1)S(1)} %get-tuple-element.71), channel_id=1, source_target_pairs={{0,8},{4,12},{8,0},{12,4},{1,9},{5,13},{9,1},{13,5},{2,10},{6,14},... | collective-permute-start | bytes 368648 | tf_op jit(solution)/shard_map/ppermute | solution.py:568
  87.7 6.3 %collective-permute-start.14 = (bf16[160,384]{1,0:T(8,128)(2,1)S(1)}, bf16[160,384]{1,0:T(8,128)(2,1)S(1)}, u32[]{:S(2)}, u32[]{:S(2)}) collective-permute-start(bf16[160,384]{1,0:T(8,128)(2,1)S(1)} %shard_map.306.refs_0_), channel_id=1, source_target_pairs={{0,48},{16,32},{32,16},{48,0},{64,112},{80,96},{96,80},{112,64},{1... | collective-permute-start | bytes 368648 | tf_op jit(solution)/shard_map/ppermute | solution.py:568
  87.8 6.2 %collective-permute-start.13 = (bf16[160,384]{1,0:T(8,128)(2,1)S(1)}, bf16[160,384]{1,0:T(8,128)(2,1)S(1)}, u32[]{:S(2)}, u32[]{:S(2)}) collective-permute-start(bf16[160,384]{1,0:T(8,128)(2,1)S(1)} %shard_map.306.refs_0_), channel_id=1, source_target_pairs={{0,32},{16,48},{32,0},{48,16},{64,96},{80,112},{96,64},{112,80},{1... | collective-permute-start | bytes 368648 | tf_op jit(solution)/shard_map/ppermute | solution.py:568
  87.9 7.3 %collective-permute-start.12 = (bf16[160,384]{1,0:T(8,128)(2,1)S(1)}, bf16[160,384]{1,0:T(8,128)(2,1)S(1)}, u32[]{:S(2)}, u32[]{:S(2)}) collective-permute-start(bf16[160,384]{1,0:T(8,128)(2,1)S(1)} %shard_map.306.refs_0_), channel_id=1, source_target_pairs={{0,16},{16,0},{32,48},{48,32},{64,80},{80,64},{96,112},{112,96},{1... | collective-permute-start | bytes 368648 | tf_op jit(solution)/shard_map/ppermute | solution.py:568
  95.3 6.3 %collective-permute-start.17 = (bf16[192,384]{1,0:T(8,128)(2,1)S(1)}, bf16[192,384]{1,0:T(8,128)(2,1)S(1)}, u32[]{:S(2)}, u32[]{:S(2)}) collective-permute-start(bf16[192,384]{1,0:T(8,128)(2,1)S(1)} %shard_map.307.refs_0_), channel_id=1, source_target_pairs={{0,192},{16,208},{32,224},{48,240},{64,128},{80,144},{96,160},{112... | collective-permute-start | bytes 442376 | tf_op jit(solution)/shard_map/ppermute | solution.py:568
  95.6 8.4 %collective-permute-start.16 = (bf16[192,384]{1,0:T(8,128)(2,1)S(1)}, bf16[192,384]{1,0:T(8,128)(2,1)S(1)}, u32[]{:S(2)}, u32[]{:S(2)}) collective-permute-start(bf16[192,384]{1,0:T(8,128)(2,1)S(1)} %shard_map.307.refs_0_), channel_id=1, source_target_pairs={{0,128},{16,144},{32,160},{48,176},{64,192},{80,208},{96,224},{112... | collective-permute-start | bytes 442376 | tf_op jit(solution)/shard_map/ppermute | solution.py:568
  98.2 9.4 %collective-permute-start.15 = (bf16[192,384]{1,0:T(8,128)(2,1)S(1)}, bf16[192,384]{1,0:T(8,128)(2,1)S(1)}, u32[]{:S(2)}, u32[]{:S(2)}) collective-permute-start(bf16[192,384]{1,0:T(8,128)(2,1)S(1)} %shard_map.307.refs_0_), channel_id=1, source_target_pairs={{0,64},{16,80},{32,96},{48,112},{64,0},{80,16},{96,32},{112,48},{1... | collective-permute-start | bytes 442376 | tf_op jit(solution)/shard_map/ppermute | solution.py:568
  107.7 8.4 %collective-permute-start.18 = (bf16[288,384]{1,0:T(8,128)(2,1)S(1)}, bf16[288,384]{1,0:T(8,128)(2,1)S(1)}, u32[]{:S(2)}, u32[]{:S(2)}) collective-permute-start(bf16[288,384]{1,0:T(8,128)(2,1)S(1)} %shard_map.308), channel_id=1, source_target_pairs={{0,8},{4,12},{8,0},{12,4},{1,9},{5,13},{9,1},{13,5},{2,10},{6,14},... | collective-permute-start | bytes 663560 | tf_op jit(solution)/shard_map/ppermute | solution.py:568
  116.2 8.8 %collective-permute-start.20 = (bf16[2,288,384]{2,1,0:T(8,128)(2,1)S(1)}, bf16[2,288,384]{2,1,0:T(8,128)(2,1)S(1)}, u32[]{:S(2)}, u32[]{:S(2)}) collective-permute-start(bf16[2,288,384]{2,1,0:T(8,128)(2,1)S(1)} %get-tuple-element.84), channel_id=1, source_target_pairs={{0,2},{1,3},{2,0},{3,1},{4,6},{5,7},{6,4},{7,5},{8,10},{9,11},{10,... | collective-permute-start | bytes 1327112 | tf_op jit(solution)/shard_map/ppermute | solution.py:568
  116.3 15.0 %collective-permute-start.19 = (bf16[2,288,384]{2,1,0:T(8,128)(2,1)S(1)}, bf16[2,288,384]{2,1,0:T(8,128)(2,1)S(1)}, u32[]{:S(2)}, u32[]{:S(2)}) collective-permute-start(bf16[2,288,384]{2,1,0:T(8,128)(2,1)S(1)} %get-tuple-element.84), channel_id=1, source_target_pairs={{0,1},{1,0},{2,3},{3,2},{4,5},{5,4},{6,7},{7,6},{8,9},{9,8},{10,11... | collective-permute-start | bytes 1327112 | tf_op jit(solution)/shard_map/ppermute | solution.py:568
  117.1 20.2 %collective-permute-start.21 = (bf16[2,288,384]{2,1,0:T(8,128)(2,1)S(1)}, bf16[2,288,384]{2,1,0:T(8,128)(2,1)S(1)}, u32[]{:S(2)}, u32[]{:S(2)}) collective-permute-start(bf16[2,288,384]{2,1,0:T(8,128)(2,1)S(1)} %get-tuple-element.84), channel_id=1, source_target_pairs={{0,3},{1,2},{2,1},{3,0},{4,7},{5,6},{6,5},{7,4},{8,11},{9,10},{10,... | collective-permute-start | bytes 1327112 | tf_op jit(solution)/shard_map/ppermute | solution.py:568
  137.3 6.2 %copy-start.1 = (s32[132]{0:T(256)S(1)}, s32[132]{0:T(256)}, u32[]{:S(2)}) copy-start(s32[132]{0:T(256)} %concatenate.3.refs_0_) | copy-start | bytes 1588
  137.6 5.9 %collective-permute-start.22 = (bf16[4,2,288,384]{3,2,1,0:T(8,128)(2,1)S(1)}, bf16[4,2,288,384]{3,2,1,0:T(8,128)(2,1)S(1)}, u32[]{:S(2)}, u32[]{:S(2)}) collective-permute-start(bf16[4,2,288,384]{3,2,1,0:T(8,128)(2,1)S(1)} %pad_maximum_fusion.refs_1_), channel_id=1, source_target_pairs={{0,4},{4,0},{8,12},{12,8},{1,5},{5,1},{9,13},{13,9},{2,6},{6,2},{1... | collective-permute-start | bytes 5308424 | tf_op jit(solution)/shard_map/ppermute | solution.py:568

commit v3 on v2

--- a/solution.py
+++ b/solution.py
@@ -1,3 +1,4 @@
+import functools
 import math
 
 import jax
@@ -126,22 +127,22 @@
         ref[QUAD:] = second[i * QUAD : (i + 1) * QUAD].astype(bf16)
 
 
-def kind_of(info, k, band):
-    return info[4 + 16 * k + band]
-
-
-def key_mask(info, shift):
-    band = info[0]
+def place_of():
+    lon = lax.axis_index("lon")
+    return lax.axis_index("lat"), lon & 1, lon >> 1, lax.axis_index("rep")
+
+
+def key_mask(valid, band, shift):
     lane = lax.broadcasted_iota(jnp.int32, (1, KEYS), 1)
     column = lane & 127
-    total_rows = info.shape[0] - 36
+    total_rows = valid.shape[0]
     last = jnp.where(band == total_rows // 6 - 1, 1, 0)
     allowed = jnp.zeros((1, KEYS), jnp.int32)
     for r in range(6):
         at = band * 6 + r + shift
         at = jnp.where(at >= total_rows, at - total_rows, at)
         hit = (column >= 12 * r) & (column < 12 * r + 12)
-        allowed = allowed + jnp.where(hit, info[36 + at], 0)
+        allowed = allowed + jnp.where(hit, valid[at], 0)
     if shift:
         row = lax.broadcasted_iota(jnp.int32, (TOK, KEYS), 0)
         wide = lax.broadcasted_iota(jnp.int32, (TOK, KEYS), 1)
@@ -156,9 +157,10 @@
     return jnp.where(column < 72, mask, 2 * masked)
 
 
-def make_bias(k, info, tables, spread, place, sort, bias_ref, turn_ref, row_ref):
+def make_bias(k, types, valid, tables, spread, place, sort, bias_ref, turn_ref, row_ref):
     row_ref[...] = jnp.zeros(row_ref.shape, f32)
-    kind = kind_of(info, k, info[0])
+    band = place_of()[0]
+    kind = types[k, 0, band]
     for h in range(HEADS):
         row_ref[h : h + 1, :REL] = tables[0, h, pl.ds(kind, 1), :]
     wide_rows = row_ref[...]
@@ -175,7 +177,7 @@
                 ].astype(bf16)
         here = dot(place, turn_ref[...])
         total = here if total is None else total + here
-    mask = key_mask(info, 3 * k)
+    mask = key_mask(valid, band, 3 * k)
     for h in range(HEADS):
         bias_ref[:, h * KEYS : (h + 1) * KEYS] = total[:, h * KEYS : (h + 1) * KEYS] + mask
 
@@ -305,16 +307,16 @@
     return result, dh, dense, small
 
 
-def bias_kernel(info, tables, spread, place, sort, bias_ref, turned, rows):
-    make_bias(1, info, tables, spread[...], low(place), low(sort), bias_ref, turned, rows)
+def bias_kernel(types, valid, tables, spread, place, sort, bias_ref, turned, rows):
+    make_bias(1, types, valid, tables, spread[...], low(place), low(sort), bias_ref, turned, rows)
 
 
 def first_kernel(
-    info, fields, upstream, scales, offsets, inward, inbias, outward, outbias, expand, upbias, narrow, downbias,
+    types, valid, fields, upstream, scales, offsets, inward, inbias, outward, outbias, expand, upbias, narrow, downbias,
     tables, turn, cut, spread, place, sort,
     q, k, v, p, mix, h1, pa, pb, pc, pd, bias, turned, rows,
 ):
-    make_bias(0, info, tables, spread[...], low(place), low(sort), bias, turned, rows)
+    make_bias(0, types, valid, tables, spread[...], low(place), low(sort), bias, turned, rows)
     order, route = low(turn), low(cut)
     x = dot(order, fields[...])
     u = norm_fwd(x, scales[0, 0:1], offsets[0, 0:1])
@@ -381,30 +383,35 @@
     put_rest(pack, table, short + small + [jnp.concatenate([dgain0, dshift0], axis=1)])
 
 
-def core_kernel(info, first, second, got_first, got_second, a, b, c, d, own, got, sems):
-    for core, sources in ((0, (first, got_first)), (1, (second, got_second))):
-
-        @pl.when(info[1] == core)
-        def _(sources=sources):
-            copies = [pltpu.make_async_copy(m, n, sems.at[i]) for i, (m, n) in enumerate(zip(sources, (own, got)))]
-            for copy in copies:
-                copy.start()
-            for copy in copies:
-                copy.wait()
-
-    for n, out in enumerate((a, b, c, d)):
-        at = (info[3] ^ n) * 2
-        out[...] = (own[pl.ds(at, 2)].astype(f32) + got[pl.ds(at, 2)].astype(f32)).astype(bf16)
-
-
-def samples_kernel(info, a, b, c, d, keep, send):
-    for out, at in ((keep, info[2]), (send, info[2] ^ 1)):
-        total = a[at].astype(f32) + b[at].astype(f32) + c[at].astype(f32) + d[at].astype(f32)
-        out[...] = total.astype(bf16)
-
-
-def pair_kernel(a, b, out):
-    out[...] = (a[...].astype(f32) + b[...].astype(f32)).astype(bf16)
+def core_kernel(first, second, got_first, got_second, *refs):
+    outs, (own, got, made, sems) = refs[:8], refs[8:]
+    _, core, side, rep = place_of()
+    part = lambda n: pl.ds((rep ^ (n // 2)) * 2 + (side ^ (n % 2)), 1)
+    order = (4, 5, 2, 3, 6, 7, 1, 0)
+    for k, (mine, theirs) in enumerate(((first, got_first), (second, got_second))):
+
+        @pl.when(core == k)
+        def _(mine=mine, theirs=theirs):
+            for n in order:
+                pltpu.make_async_copy(mine.at[part(n)], own.at[n], sems.at[n]).start()
+                pltpu.make_async_copy(theirs.at[part(n)], got.at[n], sems.at[8 + n]).start()
+
+    sent = []
+    for n in order:
+        pltpu.make_async_copy(first.at[part(n)], own.at[n], sems.at[n]).wait()
+        pltpu.make_async_copy(got_first.at[part(n)], got.at[n], sems.at[8 + n]).wait()
+        made[n] = (own[n].astype(f32) + got[n].astype(f32)).astype(bf16)
+        sent.append(pltpu.make_async_copy(made.at[n], outs[n], sems.at[16 + n]))
+        sent[-1].start()
+    for copy in sent:
+        copy.wait()
+
+
+def add_kernel(*refs):
+    total = refs[0][0].astype(f32)
+    for ref in refs[1:-1]:
+        total = total + ref[0].astype(f32)
+    refs[-1][...] = total.astype(bf16)
 
 
 def band_kernel(a, b, c, d, out):
@@ -421,32 +428,31 @@
             out[CHUNK + 32 * i : CHUNK + 32 * i + 32] = ref[CHUNK:]
 
 
-def final_kernel(
-    info, own, got,
-    scales, offsets, inward, inbias, outward, outbias, expand, upbias, narrow, downbias, tables, dense, *, factor
-):
-    def routes(k):
-        lane = lax.broadcasted_iota(jnp.int32, (1, 128), 1)
+def final_kernel(factor, types, own, got, *refs):
+    big, short = refs[:5], refs[5:11]
+    inward, outward, expand, narrow, tables, dense, sems = refs[11:]
+    scales, offsets, inbias, outbias, upbias, downbias = short
+    band, core, side, rep = place_of()
+    lane = lax.broadcasted_iota(jnp.int32, (1, 128), 1)
+    row = lax.broadcasted_iota(jnp.int32, (96, 128), 0)
+    part = lax.broadcasted_iota(jnp.int32, (96, 128), 1) & 7
+    head = row >> 4
+
+    def unpack(k, ref):
         kind = jnp.zeros((1, 128), jnp.int32)
         for e in range(16):
-            kind = kind + jnp.where((lane >> 3) == e, kind_of(info, k, info[0] ^ e), 0)
-        row = lax.broadcasted_iota(jnp.int32, (96, 128), 0)
-        part = lax.broadcasted_iota(jnp.int32, (96, 128), 1) & 7
-        head, match = row >> 4, (row & 15) == kind
+            kind = kind + jnp.where((lane >> 3) == e, types[k, 0, band ^ e], 0)
+        match = (row & 15) == kind
         made = [match & (part == head)]
         for i in range(3):
             made.append(match & ((head >> 1) == i) & (part == 6 + (head & 1)))
-        return [jnp.where(m, 1.0, 0.0).astype(bf16) for m in made]
-
-    def unpack(k, ref):
-        route = routes(k)
-        left = None
+        route = [jnp.where(m, 1.0, 0.0).astype(bf16) for m in made]
         small = []
         for chunk in range(8):
-            at = (info[3] ^ (chunk // 2), info[2] ^ (chunk % 2))
-            dense[chunk * ROWS : (chunk + 1) * ROWS] = ref[at[0], at[1], :ROWS]
-            small.append(ref[at[0], at[1], ROWS:CHUNK].astype(f32)[0:1] * factor)
-            here = ref[at[0], at[1], CHUNK:]
+            y, x = rep ^ (chunk // 2), side ^ (chunk % 2)
+            dense[chunk * ROWS : (chunk + 1) * ROWS] = ref[y, x, :ROWS]
+            small.append(ref[y, x, ROWS:CHUNK].astype(f32)[0:1] * factor)
+            here = ref[y, x, CHUNK:]
             rows = dot(route[0], here) * factor
             for h in range(HEADS):
                 tables[k, h, :, 384 * chunk : 384 * chunk + 384] = rows[16 * h : 16 * h + 16]
@@ -476,18 +482,22 @@
         scales[k, 0:1] = small[6][:, :C]
         offsets[k, 0:1] = small[6][:, C:]
 
-    @pl.when(info[1] == 0)
-    def _():
-        unpack(0, own)
-        unpack(1, got)
-
-    @pl.when(info[1] != 0)
-    def _():
-        unpack(0, got)
-        unpack(1, own)
-
-
-def call(kernel, ins, outs, scratch=(), far_outs=0, limit=VMEM):
+    sent = []
+    for k in range(2):
+        for source, wanted in ((own, core == k), (got, core != k)):
+
+            @pl.when(wanted)
+            def _(k=k, source=source):
+                unpack(k, source)
+
+        for n, array in enumerate((inward, outward, expand, narrow, tables)):
+            sent.append(pltpu.make_async_copy(array.at[k], big[n].at[k], sems.at[5 * k + n]))
+            sent[-1].start()
+    for copy in sent:
+        copy.wait()
+
+
+def call(kernel, ins, outs, scratch=(), far_outs=0, raw_outs=0, aliases={}, limit=VMEM):
     specs, fetched, slots = [], [], []
     for array, block, far in ins:
         dims = array.ndim
@@ -504,7 +514,9 @@
             specs.append(pl.BlockSpec(array.shape, lambda i, dims=dims: (0,) * dims))
     out_specs = []
     for i, o in enumerate(outs):
-        if i < far_outs:
+        if i < raw_outs:
+            out_specs.append(pl.BlockSpec(memory_space=pltpu.HBM))
+        elif i < far_outs:
             out_specs.append(pl.BlockSpec(memory_space=pltpu.HBM))
             slots.append(pltpu.VMEM(o.shape, o.dtype))
         else:
@@ -545,6 +557,7 @@
         out_specs=out_specs,
         out_shape=outs,
         scratch_shapes=list(scratch) + slots,
+        input_output_aliases=aliases,
         compiler_params=pltpu.CompilerParams(vmem_limit_bytes=limit),
         cost_estimate=pl.CostEstimate(flops=10**9, bytes_accessed=moved, transcendentals=0),
     )(*[array for array, _, _ in ins])
@@ -563,18 +576,24 @@
     )
 
 
-def swap(array, axis, distance, only=None):
-    devices = range(lax.axis_size(axis))
-    return lax.ppermute(array, axis, [(i, i ^ distance) for i in devices if only is None or i % 2 == only])
+def swap(array, axis, distance):
+    return lax.ppermute(array, axis, [(i, i ^ distance) for i in range(lax.axis_size(axis))])
+
+
+def trade(array, over_rep, over_side):
+    if not over_rep and not over_side:
+        return array
+    lon, rep = lax.axis_size("lon"), lax.axis_size("rep")
+    pairs = [
+        (i * rep + j, (i ^ (2 * over_side)) * rep + (j ^ over_rep)) for i in range(lon) for j in range(rep)
+    ]
+    return lax.ppermute(array, ("lon", "rep"), pairs)
 
 
 def body(
     fields, upstream, scales, offsets, inward, inbias, outward, outbias, expand, upbias, narrow, downbias,
     tables, window_type, row_valid,
 ):
-    lon = lax.axis_index("lon")
-    place = jnp.stack([lax.axis_index("lat"), lon % 2, lon // 2, lax.axis_index("rep")]).astype(jnp.int32)
-    info = jnp.concatenate([place, window_type[0, 0], window_type[1, 0], row_valid])
     const = constants()
     levels, row_count, col_count = fields.shape[1:4]
     total_rows = row_valid.shape[0]
@@ -595,7 +614,7 @@
     block = lambda k, *arrays: [(m, k, True) for m in arrays]
     raw = lambda *arrays: [(m, "raw", True) for m in arrays]
     fixed = lambda *names: far(*[const[name] for name in names])
-    scalars = [(info, "smem", False)]
+    scalars = [(window_type, "smem", False), (row_valid, "smem", False)]
 
     def weights(k):
         return (
@@ -624,7 +643,7 @@
         [pltpu.VMEM(m.shape, m.dtype) for m in state] + [dbias, turned],
     )
     pieces = send_pieces(pieces, 1)
-    got1 = swap(pack1, "lon", 1, 0)
+    got1 = swap(pack1, "lon", 1)
     result, adjoint, pack0 = call(
         first_back_kernel,
         far(*pieces, x, h1, scales, offsets) + block(0, inward, outward, expand) + far(upbias)
@@ -632,48 +651,44 @@
         [token, token, pack],
         (dbias, turned),
     )
-    got0 = swap(pack0, "lon", 1, 1)
-
-    part = of((2, CHUNK, 2 * C), bf16)
-    a, b, c, d = call(
+    got0 = swap(pack0, "lon", 1)
+
+    part = of((1, CHUNK, 2 * C), bf16)
+    dealt = call(
         core_kernel,
-        scalars + raw(pack0, pack1, got0, got1),
-        [part] * 4,
-        [pltpu.VMEM(pack.shape, bf16)] * 2 + [pltpu.SemaphoreType.DMA((2,))],
-    )
-    b, c, d = (swap(m, "rep", i + 1) for i, m in enumerate((b, c, d)))
-    chunk = of((CHUNK, 2 * C), bf16)
-    keep, give = call(samples_kernel, scalars + near(a, b, c, d), [chunk, chunk], limit=SMALL)
-    (a,) = call(pair_kernel, near(keep, swap(give, "lon", 2)), [chunk], limit=SMALL)
+        raw(pack0, pack1, got0, got1),
+        [part] * 8,
+        [pltpu.VMEM((8,) + part.shape, bf16)] * 3 + [pltpu.SemaphoreType.DMA((24,))],
+        raw_outs=8,
+    )
+    dealt = [trade(m, n // 2, n % 2) for n, m in enumerate(dealt)]
+    (a,) = call(add_kernel, near(*dealt), [of((CHUNK, 2 * C), bf16)], limit=SMALL)
     for step, height in ((1, CHUNK + 32), (4, CHUNK + 128)):
         others = [swap(a, "lat", step * i) for i in (1, 2, 3)]
         (a,) = call(band_kernel, near(a, *others), [of((height, 2 * C), bf16)], limit=SMALL)
-    a = jnp.stack([a, swap(a, "lon", 2)])
-    a = jnp.stack([a] + [swap(a, "rep", i) for i in (1, 2, 3)])
+    a = jnp.stack([trade(a, n // 2, n % 2) for n in range(8)]).reshape((4, 2) + a.shape)
     got = swap(a, "lon", 1)
 
     factor = 1.0 / math.sqrt(lax.axis_size("rep") * levels * total_rows * col_count * lax.axis_size("lon"))
 
-    def finish(*refs):
-        final_kernel(*refs, factor=factor)
-
-    outs = [
-        (2, 2, C), (2, 2, C), (2, C, 3 * C), (2, 3 * C), (2, C, C), (2, C), (2, C, FFN), (2, FFN), (2, C, FFN),
-        (2, C), tables.shape,
-    ]
-    joined = list(
-        call(
-            finish,
-            scalars + near(a, got),
-            [of(s, f32) for s in outs],
-            (pltpu.VMEM((8 * ROWS, 2 * C), bf16),),
-            limit=2 * SMALL,
-        )
-    )
-    joined[8] = jnp.swapaxes(joined[8], 1, 2)
-    joined[10] = jnp.swapaxes(joined[10], 1, 2)
+    wide = [(2, C, 3 * C), (2, C, C), (2, C, FFN), (2, C, FFN), tables.shape]
+    short = [(2, 2, C), (2, 2, C), (2, 3 * C), (2, C), (2, FFN), (2, C)]
+    joined = call(
+        functools.partial(final_kernel, factor),
+        scalars[:1] + near(a, got),
+        [of(m, f32) for m in wide + short],
+        [pltpu.VMEM(m, f32) for m in wide]
+        + [pltpu.VMEM((8 * ROWS, 2 * C), bf16), pltpu.SemaphoreType.DMA((10,))],
+        raw_outs=5,
+        limit=2 * SMALL,
+    )
+    inward_out, outward_out, expand_out, narrow_out, tables_out = joined[:5]
+    scales_out, offsets_out, inbias_out, outbias_out, upbias_out, downbias_out = joined[5:]
     back = lambda m: m.reshape(row_count, col_count, levels, C).transpose(2, 0, 1, 3)[None]
-    return (back(result), back(adjoint), *joined)
+    return (
+        back(result), back(adjoint), scales_out, offsets_out, inward_out, inbias_out, outward_out, outbias_out,
+        expand_out, upbias_out, jnp.swapaxes(narrow_out, 1, 2), downbias_out, jnp.swapaxes(tables_out, 1, 2),
+    )
 
 
 def solution(mesh):

time: 148 us -> 150 us (1.014)
  starting transfers between devices: 42.7 us -> 47.8 us
  local copies, waits for them, and re-layouts: 9.9 us -> 7.48 us
    ppermute x17 -> x23, starting transfers between devices: 28.9 us -> 34 us  [the longest x14 19.1 us: trade(): return lax.ppermute(array, ('lon', 'rep'), pairs)]
    pallas_call x10 -> x9, Pallas kernels: 38.4 us -> 37.3 us  [call(): pl.pallas_call(wrapped, grid=(1,), in_specs=specs, out_specs=out_specs, o...]
    ppermute x17 -> x23, waiting for transfers between devices: 49.4 us -> 49.2 us  [the longest x14 27.4 us: trade(): return lax.ppermute(array, ('lon', 'rep'), pairs)]
  transfers between devices with their start and end apart: 23 -> 29, of which waited for: 17 -> 14; matrix products, arithmetic and copies ran while one was open for 2% -> 2% of each run, Pallas kernels for 8% -> 8%
where the time goes in v3:
time: 150 us; the launch traced here: 149 us
  waiting for transfers between devices  55.7 us (37%)
  starting transfers between devices  47.8 us (32%)
  Pallas kernels  37.3 us (25%)
  local copies, waits for them, and re-layouts  7.48 us (5%)
    pallas_call x9, Pallas kernels, call(): pl.pallas_call(wrapped, grid=(1,), in_specs=specs, out_specs=out_specs, o...  37.3 us
    ppermute x14, waiting for transfers between devices, trade(): return lax.ppermute(array, ('lon', 'rep'), pairs)  27.4 us
    ppermute x9, waiting for transfers between devices, swap(): lax.ppermute(array, axis, [(i, i ^ distance) for i in range(lax.axis_size...  21.8 us
    ppermute x14, starting transfers between devices, trade(): return lax.ppermute(array, ('lon', 'rep'), pairs)  19.1 us
    ppermute x9, starting transfers between devices, swap(): lax.ppermute(array, axis, [(i, i ^ distance) for i in range(lax.axis_size...  14.9 us
    ppermute x2, starting transfers between devices, send_pieces(): lax.ppermute(pieces[1], 'lat', rows)  10.5 us
    ppermute x2, waiting for transfers between devices, send_pieces(): lax.ppermute(pieces[1], 'lat', rows)  3.99 us
    reshape x2, local copies, waits for them, and re-layouts, body(): m.reshape(row_count, col_count, levels, C).transpose(2, 0, 1, 3)[None]  3.12 us
  transfers between devices with their start and end apart: 29, of which 14 were waited for; matrix products, arithmetic and copies ran while one was open for 2% of the time, Pallas kernels for 8%

profile of v3, /device:TPU:1, one launch (start us, length us, event | category | flops | bytes accessed | tf_op | source)
XLA Modules:
  0.0 149.3 jit_solution(13879299885303055540)
XLA Ops:
  0.6 1.6 %reshape.41.refs_2_.refs_4_ = bf16[144,192]{1,0:T(8,128)(2,1)} reshape(bf16[6,12,2,192]{3,2,1,0:T(2,128)(2,1)} %bitcast.40) | data formatting | bytes 110592 | tf_op jit(solution)/shard_map/reshape | solution.py:600
  2.2 1.6 %reshape.42.refs_3_ = bf16[144,192]{1,0:T(8,128)(2,1)} reshape(bf16[6,12,2,192]{3,2,1,0:T(2,128)(2,1)} %bitcast.41) | data formatting | bytes 110592 | tf_op jit(solution)/shard_map/reshape | solution.py:601
  3.8 8.8 %shard_map.300 = (bf16[144,192]{1,0:T(8,128)(2,1)}, bf16[256,192]{1,0:T(8,128)(2,1)}, bf16[256,192]{1,0:T(8,128)(2,1)}, bf16[6,144,256]{2,1,0:T(8,128)(2,1)}, bf...) custom-call(s32[2,1,16]{2,1,0:T(1,128)} %refs_0_.5, ...), custom_call_target="tpu_custom_call" | custom-call | flops 1000000000 | bytes 8403968 | tf_op jit(solution)/shard_map/pallas_call | solution.py:553
  12.6 8.9 %collective-permute-start = (bf16[96,192]{1,0:T(8,128)(2,1)}, bf16[96,192]{1,0:T(8,128)(2,1)}, u32[]{:S(2)}, u32[]{:S(2)}) collective-permute-start(bf16[96,192]{1,0:T(8,128)(2,1)} %get-tuple-element.51), channel_id=1, source_target_pairs={{0,240},{16,0},{32,16},{48,32},{64,48},{80,64},{96,80},{112,96},{1... | collective-permute-start | bytes 110600 | tf_op jit(solution)/shard_map/ppermute | solution.py:573
  21.5 1.0 collective-permute-start.1
  22.5 1.4 collective-permute-start.2
  23.9 5.0 %shard_map.301.refs_14_ = f32[144,1536]{1,0:T(8,128)} custom-call(s32[2,1,16]{2,1,0:T(1,128)} %refs_0_.5, s32[96]{0:T(128)} %refs_1_.3, f32[2,6,16,3312]{3,2,1,0:T(8,128)} %bitcast.39, bf16[256,1536]{1,0:T(8,128)(2,1)} %constant.17.clone.refs_17_.refs_3_.refs_16_.refs_21_, f32[144,192]{1,0:T(8,128)} %constant.15.clone.refs_18_.refs_4_.refs_17_.refs_22_, ...), custom_call_target="tpu_custom_call" | custom-call | flops 1000000000 | bytes 4473344 | tf_op jit(solution)/shard_map/pallas_call | solution.py:553
  28.9 0.0 collective-permute-done.refs_1_
  28.9 0.0 collective-permute-done.2.refs_3_
  28.9 9.2 %shard_map.302 = (bf16[8,160,384]{2,1,0:T(8,128)(2,1)}, bf16[96,192]{1,0:T(8,128)(2,1)}, bf16[96,192]{1,0:T(8,128)(2,1)}, bf16[96,192]{1,0:T(8,128)(2,1)}, bf16[96,192]{1,0:T(8,128)(2,1)}) custom-call(bf16[96,192]{1,0:T(8,128)(2,1)} %get-tuple-element.50.refs_0_, bf16[96,192]{1,0:T(8,128)(2,1)} %collective-permute-done.refs_1_, ...), custom_call_target="tpu_custom_call" | custom-call | flops 1000000000 | bytes 6876672 | tf_op jit(solution)/shard_map/pallas_call | solution.py:553
  38.1 1.6 %collective-permute-start.3 = (bf16[96,192]{1,0:T(8,128)(2,1)}, bf16[96,192]{1,0:T(8,128)(2,1)}, u32[]{:S(2)}, u32[]{:S(2)}) collective-permute-start(bf16[96,192]{1,0:T(8,128)(2,1)} %get-tuple-element.55), channel_id=1, source_target_pairs={{0,16},{16,32},{32,48},{48,64},{64,80},{80,96},{96,112},{112,128},... | collective-permute-start | bytes 110600 | tf_op jit(solution)/shard_map/ppermute | solution.py:573
  39.7 1.0 collective-permute-start.4
  40.7 0.0 collective-permute-start.5
  40.7 1.0 collective-permute-start.7
  41.7 4.0 %collective-permute-done.3.refs_1_ = bf16[96,192]{1,0:T(8,128)(2,1)} collective-permute-done((bf16[96,192]{1,0:T(8,128)(2,1)}, bf16[96,192]{1,0:T(8,128)(2,1)}, u32[]{:S(2)}, u32[]{:S(2)}) %collective-permute-start.3) | collective-permute-done | bytes 36896 | tf_op jit(solution)/shard_map/ppermute | solution.py:573
  45.6 0.0 collective-permute-done.4.refs_2_
  45.6 2.5 %collective-permute-done.5.refs_3_ = bf16[96,192]{1,0:T(8,128)(2,1)} collective-permute-done((bf16[96,192]{1,0:T(8,128)(2,1)}, bf16[96,192]{1,0:T(8,128)(2,1)}, u32[]{:S(2)}, u32[]{:S(2)}) %collective-permute-start.5) | collective-permute-done | bytes 36896 | tf_op jit(solution)/shard_map/ppermute | solution.py:575
  48.1 7.1 %shard_map.303 = (bf16[144,192]{1,0:T(8,128)(2,1)}, bf16[144,192]{1,0:T(8,128)(2,1)}, bf16[8,160,384]{2,1,0:T(8,128)(2,1)}) custom-call(bf16[96,192]{1,0:T(8,128)(2,1)} %get-tuple-element.54.refs_0_, bf16[96,192]{1,0:T(8,128)(2,1)} %collective-permute-done.3.refs_1_, bf16[96,192]{1,0:T(8,128)(2,1)} %collective-permute-done.4.refs_2_, ...), custom_call_target="tpu_custom_call" | custom-call | flops 1000000000 | bytes 6892032 | tf_op jit(solution)/shard_map/pallas_call | solution.py:553
  55.2 0.1 collective-permute-start.6
  55.3 2.9 %collective-permute-done.6.refs_2_ = bf16[8,160,384]{2,1,0:T(8,128)(2,1)} collective-permute-done((bf16[8,160,384]{2,1,0:T(8,128)(2,1)}, bf16[8,160,384]{2,1,0:T(8,128)(2,1)}, u32[]{:S(2)}, u32[]{:S(2)}) %collective-permute-start.6) | collective-permute-done | bytes 983072 | tf_op jit(solution)/shard_map/ppermute | solution.py:580
  58.2 2.5 %shard_map.304 = (bf16[1,160,384]{2,1,0:T(8,128)(2,1)}, bf16[1,160,384]{2,1,0:T(8,128)(2,1)}, bf16[1,160,384]{2,1,0:T(8,128)(2,1)}, bf16[1,160,384]{2,1,0:T(8,12...) custom-call(bf16[8,160,384]{2,1,0:T(8,128)(2,1)} %get-tuple-element., ...), custom_call_target="tpu_custom_call" | custom-call | flops 1000000000 | bytes 4915200 | tf_op jit(solution)/shard_map/pallas_call | solution.py:553
  60.7 0.4 collective-permute-start.8
  61.1 1.3 collective-permute-start.9
  62.4 1.0 collective-permute-start.10
  63.4 2.9 %collective-permute-start.11 = (bf16[1,160,384]{2,1,0:T(8,128)(2,1)}, bf16[1,160,384]{2,1,0:T(8,128)(2,1)S(1)}, u32[]{:S(2)}, u32[]{:S(2)}) collective-permute-start(bf16[1,160,384]{2,1,0:T(8,128)(2,1)} %get-tuple-element.72), channel_id=1, source_target_pairs={{0,2},{1,3},{2,0},{3,1},{4,6},{5,7},{6,4},{7,5},{8,10},{9,11},{10,... | collective-permute-start | bytes 368648 | tf_op jit(solution)/shard_map/ppermute | solution.py:590
  66.3 0.1 collective-permute-start.12
  66.4 0.0 collective-permute-done.8.refs_1_
  66.4 2.8 %collective-permute-start.13 = (bf16[1,160,384]{2,1,0:T(8,128)(2,1)}, bf16[1,160,384]{2,1,0:T(8,128)(2,1)S(1)}, u32[]{:S(2)}, u32[]{:S(2)}) collective-permute-start(bf16[1,160,384]{2,1,0:T(8,128)(2,1)} %get-tuple-element.74), channel_id=1, source_target_pairs={{0,3},{1,2},{2,1},{3,0},{4,7},{5,6},{6,5},{7,4},{8,11},{9,10},{10,... | collective-permute-start | bytes 368648 | tf_op jit(solution)/shard_map/ppermute | solution.py:590
  69.2 0.9 collective-permute-start.14
  70.1 7.0 %collective-permute-done.11.refs_4_ = bf16[1,160,384]{2,1,0:T(8,128)(2,1)S(1)} collective-permute-done((bf16[1,160,384]{2,1,0:T(8,128)(2,1)}, bf16[1,160,384]{2,1,0:T(8,128)(2,1)S(1)}, u32[]{:S(2)}, u32[]{:S(2)}) %collective-permute-start.11) | collective-permute-done | bytes 122912 | tf_op jit(solution)/shard_map/ppermute | solution.py:590
  77.1 0.0 collective-permute-done.12.refs_5_
  77.1 2.2 %collective-permute-done.13.refs_6_ = bf16[1,160,384]{2,1,0:T(8,128)(2,1)S(1)} collective-permute-done((bf16[1,160,384]{2,1,0:T(8,128)(2,1)}, bf16[1,160,384]{2,1,0:T(8,128)(2,1)S(1)}, u32[]{:S(2)}, u32[]{:S(2)}) %collective-permute-start.13) | collective-permute-done | bytes 122912 | tf_op jit(solution)/shard_map/ppermute | solution.py:590
  79.4 0.0 collective-permute-done.14.refs_7_
  79.4 0.9 copy-done.1
  80.3 0.1 shard_map.305.refs_0_
  80.4 0.1 collective-permute-start.17
  80.5 1.3 collective-permute-start.16
  81.8 2.8 %collective-permute-start.15 = (bf16[160,384]{1,0:T(8,128)(2,1)S(1)}, bf16[160,384]{1,0:T(8,128)(2,1)S(1)}, u32[]{:S(2)}, u32[]{:S(2)}) collective-permute-start(bf16[160,384]{1,0:T(8,128)(2,1)S(1)} %shard_map.305.refs_0_), channel_id=1, source_target_pairs={{0,16},{16,0},{32,48},{48,32},{64,80},{80,64},{96,112},{112,96},{1... | collective-permute-start | bytes 368648 | tf_op jit(solution)/shard_map/ppermute | solution.py:580
  84.6 2.1 %collective-permute-done.17.refs_3_ = bf16[160,384]{1,0:T(8,128)(2,1)S(1)} collective-permute-done((bf16[160,384]{1,0:T(8,128)(2,1)S(1)}, bf16[160,384]{1,0:T(8,128)(2,1)S(1)}, u32[]{:S(2)}, u32[]{:S(2)}) %collective-permute-start.17) | collective-permute-done | bytes 122912 | tf_op jit(solution)/shard_map/ppermute | solution.py:580
  86.7 1.8 %collective-permute-done.15.refs_1_ = bf16[160,384]{1,0:T(8,128)(2,1)S(1)} collective-permute-done((bf16[160,384]{1,0:T(8,128)(2,1)S(1)}, bf16[160,384]{1,0:T(8,128)(2,1)S(1)}, u32[]{:S(2)}, u32[]{:S(2)}) %collective-permute-start.15) | collective-permute-done | bytes 122912 | tf_op jit(solution)/shard_map/ppermute | solution.py:580
  88.5 0.1 shard_map.306.refs_0_
  88.6 2.3 %collective-permute-start.20 = (bf16[192,384]{1,0:T(8,128)(2,1)S(1)}, bf16[192,384]{1,0:T(8,128)(2,1)S(1)}, u32[]{:S(2)}, u32[]{:S(2)}) collective-permute-start(bf16[192,384]{1,0:T(8,128)(2,1)S(1)} %shard_map.306.refs_0_), channel_id=1, source_target_pairs={{0,192},{16,208},{32,224},{48,240},{64,128},{80,144},{96,160},{112... | collective-permute-start | bytes 442376 | tf_op jit(solution)/shard_map/ppermute | solution.py:580
  90.9 3.6 %collective-permute-start.19 = (bf16[192,384]{1,0:T(8,128)(2,1)S(1)}, bf16[192,384]{1,0:T(8,128)(2,1)S(1)}, u32[]{:S(2)}, u32[]{:S(2)}) collective-permute-start(bf16[192,384]{1,0:T(8,128)(2,1)S(1)} %shard_map.306.refs_0_), channel_id=1, source_target_pairs={{0,128},{16,144},{32,160},{48,176},{64,192},{80,208},{96,224},{112... | collective-permute-start | bytes 442376 | tf_op jit(solution)/shard_map/ppermute | solution.py:580
  94.6 0.2 collective-permute-start.18
  94.8 0.1 collective-permute-done.20.refs_3_
  94.9 6.1 %collective-permute-done.19.refs_2_ = bf16[192,384]{1,0:T(8,128)(2,1)S(1)} collective-permute-done((bf16[192,384]{1,0:T(8,128)(2,1)S(1)}, bf16[192,384]{1,0:T(8,128)(2,1)S(1)}, u32[]{:S(2)}, u32[]{:S(2)}) %collective-permute-start.19) | collective-permute-done | bytes 147488 | tf_op jit(solution)/shard_map/ppermute | solution.py:580
  101.0 8.5 %collective-permute-done.18.refs_1_ = bf16[192,384]{1,0:T(8,128)(2,1)S(1)} collective-permute-done((bf16[192,384]{1,0:T(8,128)(2,1)S(1)}, bf16[192,384]{1,0:T(8,128)(2,1)S(1)}, u32[]{:S(2)}, u32[]{:S(2)}) %collective-permute-start.18) | collective-permute-done | bytes 147488 | tf_op jit(solution)/shard_map/ppermute | solution.py:580
  109.5 0.1 shard_map.307
  109.6 2.5 %collective-permute-start.27 = (bf16[288,384]{1,0:T(8,128)(2,1)S(1)}, bf16[288,384]{1,0:T(8,128)(2,1)S(1)}, u32[]{:S(2)}, u32[]{:S(2)}) collective-permute-start(bf16[288,384]{1,0:T(8,128)(2,1)S(1)} %shard_map.307), channel_id=1, source_target_pairs={{0,11},{1,10},{2,9},{3,8},{4,15},{5,14},{6,13},{7,12},{8,3},{9,2},... | collective-permute-start | bytes 663560 | tf_op jit(solution)/shard_map/ppermute | solution.py:590
  112.1 4.1 %collective-permute-start.24 = (bf16[288,384]{1,0:T(8,128)(2,1)S(1)}, bf16[288,384]{1,0:T(8,128)(2,1)S(1)}, u32[]{:S(2)}, u32[]{:S(2)}) collective-permute-start(bf16[288,384]{1,0:T(8,128)(2,1)S(1)} %shard_map.307), channel_id=1, source_target_pairs={{0,2},{1,3},{2,0},{3,1},{4,6},{5,7},{6,4},{7,5},{8,10},{9,11},{10,... | collective-permute-start | bytes 663560 | tf_op jit(solution)/shard_map/ppermute | solution.py:590
  116.2 0.0 collective-permute-start.21
  116.3 0.0 copy-start
  116.3 10.0 %collective-permute-done.21 = bf16[288,384]{1,0:T(8,128)(2,1)S(1)} collective-permute-done((bf16[288,384]{1,0:T(8,128)(2,1)S(1)}, bf16[288,384]{1,0:T(8,128)(2,1)S(1)}, u32[]{:S(2)}, u32[]{:S(2)}) %collective-permute-start.21) | collective-permute-done | bytes 221216 | tf_op jit(solution)/shard_map/ppermute | solution.py:590
  126.3 0.9 collective-permute-start.22
  127.2 4.6 %collective-permute-done.22 = bf16[288,384]{1,0:T(8,128)(2,1)S(1)} collective-permute-done((bf16[288,384]{1,0:T(8,128)(2,1)S(1)}, bf16[288,384]{1,0:T(8,128)(2,1)S(1)}, u32[]{:S(2)}, u32[]{:S(2)}) %collective-permute-start.22) | collective-permute-done | bytes 221216 | tf_op jit(solution)/shard_map/ppermute | solution.py:590
  131.9 2.0 %collective-permute-start.23 = (bf16[288,384]{1,0:T(8,128)(2,1)S(1)}, bf16[288,384]{1,0:T(8,128)(2,1)S(1)}, u32[]{:S(2)}, u32[]{:S(2)}) collective-permute-start(bf16[288,384]{1,0:T(8,128)(2,1)S(1)} %shard_map.307), channel_id=1, source_target_pairs={{0,9},{1,8},{2,11},{3,10},{4,13},{5,12},{6,15},{7,14},{8,1},{9,0},... | collective-permute-start | bytes 663560 | tf_op jit(solution)/shard_map/ppermute | solution.py:590
  133.9 3.6 %collective-permute-done.23 = bf16[288,384]{1,0:T(8,128)(2,1)S(1)} collective-permute-done((bf16[288,384]{1,0:T(8,128)(2,1)S(1)}, bf16[288,384]{1,0:T(8,128)(2,1)S(1)}, u32[]{:S(2)}, u32[]{:S(2)}) %collective-permute-start.23) | collective-permute-done | bytes 221216 | tf_op jit(solution)/shard_map/ppermute | solution.py:590
  137.6 0.0 collective-permute-done.24
  137.7 0.0 collective-permute-done.26
  137.8 3.5 %collective-permute-start.28 = (bf16[4,2,288,384]{3,2,1,0:T(8,128)(2,1)S(1)}, bf16[4,2,288,384]{3,2,1,0:T(8,128)(2,1)S(1)}, u32[]{:S(2)}, u32[]{:S(2)}) collective-permute-start(bf16[4,2,288,384]{3,2,1,0:T(8,128)(2,1)S(1)} %bitcast.33), channel_id=1, source_target_pairs={{0,4},{4,0},{8,12},{12,8},{1,5},{5,1},{9,13},{13,9},{2,6},{6,2},{1... | collective-permute-start | bytes 5308424 | tf_op jit(solution)/shard_map/ppermute | solution.py:580
  141.3 1.6 %reshape.43 = bf16[6,12,2,192]{3,2,1,0:T(2,128)(2,1)} reshape(bf16[144,192]{1,0:T(8,128)(2,1)} %get-tuple-element.64) | data formatting | bytes 110592 | tf_op jit(solution)/shard_map/reshape | solution.py:687
  142.9 1.6 %reshape.44 = bf16[6,12,2,192]{3,2,1,0:T(2,128)(2,1)} reshape(bf16[144,192]{1,0:T(8,128)(2,1)} %get-tuple-element.65) | data formatting | bytes 110592 | tf_op jit(solution)/shard_map/reshape | solution.py:687
  144.4 0.2 collective-permute-done.28.refs_2_
  144.6 4.4 %shard_map.308 = (f32[2,192,576]{2,1,0:T(8,128)}, f32[2,192,192]{2,1,0:T(8,128)}, f32[2,192,768]{2,1,0:T(8,128)}, f32[2,192,768]{2,1,0:T(8,128)}, f32[2,6,16,331...) custom-call(s32[2,1,16]{2,1,0:T(1,128)S(1)} %copy-done, ...), custom_call_target="tpu_custom_call" | custom-call | flops 1000000000 | bytes 9641600 | tf_op jit(solution)/shard_map/pallas_call | solution.py:553
  (19 shorter events, 0.3 us)
Async XLA Ops:
  12.6 16.3 %collective-permute-start = (bf16[96,192]{1,0:T(8,128)(2,1)}, bf16[96,192]{1,0:T(8,128)(2,1)}, u32[]{:S(2)}, u32[]{:S(2)}) collective-permute-start(bf16[96,192]{1,0:T(8,128)(2,1)} %get-tuple-element.51), channel_id=1, source_target_pairs={{0,240},{16,0},{32,16},{48,32},{64,48},{80,64},{96,80},{112,96},{1... | collective-permute-start | bytes 110600 | tf_op jit(solution)/shard_map/ppermute | solution.py:573
  21.5 7.4 %collective-permute-start.1 = (bf16[96,192]{1,0:T(8,128)(2,1)}, bf16[96,192]{1,0:T(8,128)(2,1)}, u32[]{:S(2)}, u32[]{:S(2)}) collective-permute-start(bf16[96,192]{1,0:T(8,128)(2,1)} %get-tuple-element.52), channel_id=1, source_target_pairs={{0,12},{4,0},{8,4},{12,8},{1,13},{5,1},{9,5},{13,9},{2,14},{6,2},{... | collective-permute-start | bytes 110600 | tf_op jit(solution)/shard_map/ppermute | solution.py:574
  22.5 6.4 %collective-permute-start.2 = (bf16[96,192]{1,0:T(8,128)(2,1)}, bf16[96,192]{1,0:T(8,128)(2,1)}, u32[]{:S(2)}, u32[]{:S(2)}) collective-permute-start(bf16[96,192]{1,0:T(8,128)(2,1)} %get-tuple-element.53), channel_id=1, source_target_pairs={{0,252},{4,240},{8,244},{12,248},{16,12},{20,0},{24,4},{28,8},{32,... | collective-permute-start | bytes 110600 | tf_op jit(solution)/shard_map/ppermute | solution.py:575
  38.1 7.5 %collective-permute-start.3 = (bf16[96,192]{1,0:T(8,128)(2,1)}, bf16[96,192]{1,0:T(8,128)(2,1)}, u32[]{:S(2)}, u32[]{:S(2)}) collective-permute-start(bf16[96,192]{1,0:T(8,128)(2,1)} %get-tuple-element.55), channel_id=1, source_target_pairs={{0,16},{16,32},{32,48},{48,64},{64,80},{80,96},{96,112},{112,128},... | collective-permute-start | bytes 110600 | tf_op jit(solution)/shard_map/ppermute | solution.py:573
  39.7 5.9 %collective-permute-start.4 = (bf16[96,192]{1,0:T(8,128)(2,1)}, bf16[96,192]{1,0:T(8,128)(2,1)}, u32[]{:S(2)}, u32[]{:S(2)}) collective-permute-start(bf16[96,192]{1,0:T(8,128)(2,1)} %get-tuple-element.56), channel_id=1, source_target_pairs={{0,4},{4,8},{8,12},{12,0},{1,5},{5,9},{9,13},{13,1},{2,6},{6,10},{... | collective-permute-start | bytes 110600 | tf_op jit(solution)/shard_map/ppermute | solution.py:574
  40.7 7.4 %collective-permute-start.5 = (bf16[96,192]{1,0:T(8,128)(2,1)}, bf16[96,192]{1,0:T(8,128)(2,1)}, u32[]{:S(2)}, u32[]{:S(2)}) collective-permute-start(bf16[96,192]{1,0:T(8,128)(2,1)} %get-tuple-element.57), channel_id=1, source_target_pairs={{0,20},{4,24},{8,28},{12,16},{16,36},{20,40},{24,44},{28,32},{32,5... | collective-permute-start | bytes 110600 | tf_op jit(solution)/shard_map/ppermute | solution.py:575
  40.7 14.6 %collective-permute-start.7 = (bf16[8,160,384]{2,1,0:T(8,128)(2,1)}, bf16[8,160,384]{2,1,0:T(8,128)(2,1)}, u32[]{:S(2)}, u32[]{:S(2)}) collective-permute-start(bf16[8,160,384]{2,1,0:T(8,128)(2,1)} %get-tuple-element.67.refs_1_), channel_id=1, source_target_pairs={{0,4},{4,0},{8,12},{12,8},{1,5},{5,1},{9,13},{13,9},{2,6},{6,2},{1... | collective-permute-start | bytes 2949128 | tf_op jit(solution)/shard_map/ppermute | solution.py:580
  55.2 3.0 %collective-permute-start.6 = (bf16[8,160,384]{2,1,0:T(8,128)(2,1)}, bf16[8,160,384]{2,1,0:T(8,128)(2,1)}, u32[]{:S(2)}, u32[]{:S(2)}) collective-permute-start(bf16[8,160,384]{2,1,0:T(8,128)(2,1)} %get-tuple-element.66.refs_0_), channel_id=1, source_target_pairs={{0,4},{4,0},{8,12},{12,8},{1,5},{5,1},{9,13},{13,9},{2,6},{6,2},{1... | collective-permute-start | bytes 2949128 | tf_op jit(solution)/shard_map/ppermute | solution.py:580
  60.7 5.7 %collective-permute-start.8 = (bf16[1,160,384]{2,1,0:T(8,128)(2,1)}, bf16[1,160,384]{2,1,0:T(8,128)(2,1)S(1)}, u32[]{:S(2)}, u32[]{:S(2)}) collective-permute-start(bf16[1,160,384]{2,1,0:T(8,128)(2,1)} %get-tuple-element.69), channel_id=1, source_target_pairs={{0,8},{1,9},{2,10},{3,11},{4,12},{5,13},{6,14},{7,15},{8,0},{9,1},... | collective-permute-start | bytes 368648 | tf_op jit(solution)/shard_map/ppermute | solution.py:590
  61.1 8.1 %collective-permute-start.9 = (bf16[1,160,384]{2,1,0:T(8,128)(2,1)}, bf16[1,160,384]{2,1,0:T(8,128)(2,1)S(1)}, u32[]{:S(2)}, u32[]{:S(2)}) collective-permute-start(bf16[1,160,384]{2,1,0:T(8,128)(2,1)} %get-tuple-element.70), channel_id=1, source_target_pairs={{0,1},{1,0},{2,3},{3,2},{4,5},{5,4},{6,7},{7,6},{8,9},{9,8},{10,11... | collective-permute-start | bytes 368648 | tf_op jit(solution)/shard_map/ppermute | solution.py:590
  62.4 7.7 %collective-permute-start.10 = (bf16[1,160,384]{2,1,0:T(8,128)(2,1)}, bf16[1,160,384]{2,1,0:T(8,128)(2,1)S(1)}, u32[]{:S(2)}, u32[]{:S(2)}) collective-permute-start(bf16[1,160,384]{2,1,0:T(8,128)(2,1)} %get-tuple-element.71), channel_id=1, source_target_pairs={{0,9},{1,8},{2,11},{3,10},{4,13},{5,12},{6,15},{7,14},{8,1},{9,0},... | collective-permute-start | bytes 368648 | tf_op jit(solution)/shard_map/ppermute | solution.py:590
  63.4 13.7 %collective-permute-start.11 = (bf16[1,160,384]{2,1,0:T(8,128)(2,1)}, bf16[1,160,384]{2,1,0:T(8,128)(2,1)S(1)}, u32[]{:S(2)}, u32[]{:S(2)}) collective-permute-start(bf16[1,160,384]{2,1,0:T(8,128)(2,1)} %get-tuple-element.72), channel_id=1, source_target_pairs={{0,2},{1,3},{2,0},{3,1},{4,6},{5,7},{6,4},{7,5},{8,10},{9,11},{10,... | collective-permute-start | bytes 368648 | tf_op jit(solution)/shard_map/ppermute | solution.py:590
  66.3 10.8 %collective-permute-start.12 = (bf16[1,160,384]{2,1,0:T(8,128)(2,1)}, bf16[1,160,384]{2,1,0:T(8,128)(2,1)S(1)}, u32[]{:S(2)}, u32[]{:S(2)}) collective-permute-start(bf16[1,160,384]{2,1,0:T(8,128)(2,1)} %get-tuple-element.73), channel_id=1, source_target_pairs={{0,10},{1,11},{2,8},{3,9},{4,14},{5,15},{6,12},{7,13},{8,2},{9,3},... | collective-permute-start | bytes 368648 | tf_op jit(solution)/shard_map/ppermute | solution.py:590
  66.4 12.9 %collective-permute-start.13 = (bf16[1,160,384]{2,1,0:T(8,128)(2,1)}, bf16[1,160,384]{2,1,0:T(8,128)(2,1)S(1)}, u32[]{:S(2)}, u32[]{:S(2)}) collective-permute-start(bf16[1,160,384]{2,1,0:T(8,128)(2,1)} %get-tuple-element.74), channel_id=1, source_target_pairs={{0,3},{1,2},{2,1},{3,0},{4,7},{5,6},{6,5},{7,4},{8,11},{9,10},{10,... | collective-permute-start | bytes 368648 | tf_op jit(solution)/shard_map/ppermute | solution.py:590
  69.2 10.2 %collective-permute-start.14 = (bf16[1,160,384]{2,1,0:T(8,128)(2,1)}, bf16[1,160,384]{2,1,0:T(8,128)(2,1)S(1)}, u32[]{:S(2)}, u32[]{:S(2)}) collective-permute-start(bf16[1,160,384]{2,1,0:T(8,128)(2,1)} %get-tuple-element.75), channel_id=1, source_target_pairs={{0,11},{1,10},{2,9},{3,8},{4,15},{5,14},{6,13},{7,12},{8,3},{9,2},... | collective-permute-start | bytes 368648 | tf_op jit(solution)/shard_map/ppermute | solution.py:590
  79.4 0.9 copy-start.1
  80.4 6.3 %collective-permute-start.17 = (bf16[160,384]{1,0:T(8,128)(2,1)S(1)}, bf16[160,384]{1,0:T(8,128)(2,1)S(1)}, u32[]{:S(2)}, u32[]{:S(2)}) collective-permute-start(bf16[160,384]{1,0:T(8,128)(2,1)S(1)} %shard_map.305.refs_0_), channel_id=1, source_target_pairs={{0,48},{16,32},{32,16},{48,0},{64,112},{80,96},{96,80},{112,64},{1... | collective-permute-start | bytes 368648 | tf_op jit(solution)/shard_map/ppermute | solution.py:580
  80.5 6.2 %collective-permute-start.16 = (bf16[160,384]{1,0:T(8,128)(2,1)S(1)}, bf16[160,384]{1,0:T(8,128)(2,1)S(1)}, u32[]{:S(2)}, u32[]{:S(2)}) collective-permute-start(bf16[160,384]{1,0:T(8,128)(2,1)S(1)} %shard_map.305.refs_0_), channel_id=1, source_target_pairs={{0,32},{16,48},{32,0},{48,16},{64,96},{80,112},{96,64},{112,80},{1... | collective-permute-start | bytes 368648 | tf_op jit(solution)/shard_map/ppermute | solution.py:580
  81.8 6.7 %collective-permute-start.15 = (bf16[160,384]{1,0:T(8,128)(2,1)S(1)}, bf16[160,384]{1,0:T(8,128)(2,1)S(1)}, u32[]{:S(2)}, u32[]{:S(2)}) collective-permute-start(bf16[160,384]{1,0:T(8,128)(2,1)S(1)} %shard_map.305.refs_0_), channel_id=1, source_target_pairs={{0,16},{16,0},{32,48},{48,32},{64,80},{80,64},{96,112},{112,96},{1... | collective-permute-start | bytes 368648 | tf_op jit(solution)/shard_map/ppermute | solution.py:580
  88.6 6.3 %collective-permute-start.20 = (bf16[192,384]{1,0:T(8,128)(2,1)S(1)}, bf16[192,384]{1,0:T(8,128)(2,1)S(1)}, u32[]{:S(2)}, u32[]{:S(2)}) collective-permute-start(bf16[192,384]{1,0:T(8,128)(2,1)S(1)} %shard_map.306.refs_0_), channel_id=1, source_target_pairs={{0,192},{16,208},{32,224},{48,240},{64,128},{80,144},{96,160},{112... | collective-permute-start | bytes 442376 | tf_op jit(solution)/shard_map/ppermute | solution.py:580
  90.9 10.1 %collective-permute-start.19 = (bf16[192,384]{1,0:T(8,128)(2,1)S(1)}, bf16[192,384]{1,0:T(8,128)(2,1)S(1)}, u32[]{:S(2)}, u32[]{:S(2)}) collective-permute-start(bf16[192,384]{1,0:T(8,128)(2,1)S(1)} %shard_map.306.refs_0_), channel_id=1, source_target_pairs={{0,128},{16,144},{32,160},{48,176},{64,192},{80,208},{96,224},{112... | collective-permute-start | bytes 442376 | tf_op jit(solution)/shard_map/ppermute | solution.py:580
  94.6 15.0 %collective-permute-start.18 = (bf16[192,384]{1,0:T(8,128)(2,1)S(1)}, bf16[192,384]{1,0:T(8,128)(2,1)S(1)}, u32[]{:S(2)}, u32[]{:S(2)}) collective-permute-start(bf16[192,384]{1,0:T(8,128)(2,1)S(1)} %shard_map.306.refs_0_), channel_id=1, source_target_pairs={{0,64},{16,80},{32,96},{48,112},{64,0},{80,16},{96,32},{112,48},{1... | collective-permute-start | bytes 442376 | tf_op jit(solution)/shard_map/ppermute | solution.py:580
  109.6 28.2 %collective-permute-start.27 = (bf16[288,384]{1,0:T(8,128)(2,1)S(1)}, bf16[288,384]{1,0:T(8,128)(2,1)S(1)}, u32[]{:S(2)}, u32[]{:S(2)}) collective-permute-start(bf16[288,384]{1,0:T(8,128)(2,1)S(1)} %shard_map.307), channel_id=1, source_target_pairs={{0,11},{1,10},{2,9},{3,8},{4,15},{5,14},{6,13},{7,12},{8,3},{9,2},... | collective-permute-start | bytes 663560 | tf_op jit(solution)/shard_map/ppermute | solution.py:590
  112.1 25.6 %collective-permute-start.26 = (bf16[288,384]{1,0:T(8,128)(2,1)S(1)}, bf16[288,384]{1,0:T(8,128)(2,1)S(1)}, u32[]{:S(2)}, u32[]{:S(2)}) collective-permute-start(bf16[288,384]{1,0:T(8,128)(2,1)S(1)} %shard_map.307), channel_id=1, source_target_pairs={{0,3},{1,2},{2,1},{3,0},{4,7},{5,6},{6,5},{7,4},{8,11},{9,10},{10,... | collective-permute-start | bytes 663560 | tf_op jit(solution)/shard_map/ppermute | solution.py:590
  112.1 25.5 %collective-permute-start.25 = (bf16[288,384]{1,0:T(8,128)(2,1)S(1)}, bf16[288,384]{1,0:T(8,128)(2,1)S(1)}, u32[]{:S(2)}, u32[]{:S(2)}) collective-permute-start(bf16[288,384]{1,0:T(8,128)(2,1)S(1)} %shard_map.307), channel_id=1, source_target_pairs={{0,10},{1,11},{2,8},{3,9},{4,14},{5,15},{6,12},{7,13},{8,2},{9,3},... | collective-permute-start | bytes 663560 | tf_op jit(solution)/shard_map/ppermute | solution.py:590
  112.1 25.5 %collective-permute-start.24 = (bf16[288,384]{1,0:T(8,128)(2,1)S(1)}, bf16[288,384]{1,0:T(8,128)(2,1)S(1)}, u32[]{:S(2)}, u32[]{:S(2)}) collective-permute-start(bf16[288,384]{1,0:T(8,128)(2,1)S(1)} %shard_map.307), channel_id=1, source_target_pairs={{0,2},{1,3},{2,0},{3,1},{4,6},{5,7},{6,4},{7,5},{8,10},{9,11},{10,... | collective-permute-start | bytes 663560 | tf_op jit(solution)/shard_map/ppermute | solution.py:590
  116.2 10.0 %collective-permute-start.21 = (bf16[288,384]{1,0:T(8,128)(2,1)S(1)}, bf16[288,384]{1,0:T(8,128)(2,1)S(1)}, u32[]{:S(2)}, u32[]{:S(2)}) collective-permute-start(bf16[288,384]{1,0:T(8,128)(2,1)S(1)} %shard_map.307), channel_id=1, source_target_pairs={{0,8},{1,9},{2,10},{3,11},{4,12},{5,13},{6,14},{7,15},{8,0},{9,1},... | collective-permute-start | bytes 663560 | tf_op jit(solution)/shard_map/ppermute | solution.py:590
  116.3 28.3 %copy-start = (s32[2,1,16]{2,1,0:T(1,128)S(1)}, s32[2,1,16]{2,1,0:T(1,128)}, u32[]{:S(2)}) copy-start(s32[2,1,16]{2,1,0:T(1,128)} %refs_0_.5) | copy-start | bytes 388
  126.3 5.6 %collective-permute-start.22 = (bf16[288,384]{1,0:T(8,128)(2,1)S(1)}, bf16[288,384]{1,0:T(8,128)(2,1)S(1)}, u32[]{:S(2)}, u32[]{:S(2)}) collective-permute-start(bf16[288,384]{1,0:T(8,128)(2,1)S(1)} %shard_map.307), channel_id=1, source_target_pairs={{0,1},{1,0},{2,3},{3,2},{4,5},{5,4},{6,7},{7,6},{8,9},{9,8},{10,11... | collective-permute-start | bytes 663560 | tf_op jit(solution)/shard_map/ppermute | solution.py:590
  131.9 5.7 %collective-permute-start.23 = (bf16[288,384]{1,0:T(8,128)(2,1)S(1)}, bf16[288,384]{1,0:T(8,128)(2,1)S(1)}, u32[]{:S(2)}, u32[]{:S(2)}) collective-permute-start(bf16[288,384]{1,0:T(8,128)(2,1)S(1)} %shard_map.307), channel_id=1, source_target_pairs={{0,9},{1,8},{2,11},{3,10},{4,13},{5,12},{6,15},{7,14},{8,1},{9,0},... | collective-permute-start | bytes 663560 | tf_op jit(solution)/shard_map/ppermute | solution.py:590
  137.8 6.8 %collective-permute-start.28 = (bf16[4,2,288,384]{3,2,1,0:T(8,128)(2,1)S(1)}, bf16[4,2,288,384]{3,2,1,0:T(8,128)(2,1)S(1)}, u32[]{:S(2)}, u32[]{:S(2)}) collective-permute-start(bf16[4,2,288,384]{3,2,1,0:T(8,128)(2,1)S(1)} %bitcast.33), channel_id=1, source_target_pairs={{0,4},{4,0},{8,12},{12,8},{1,5},{5,1},{9,13},{13,9},{2,6},{6,2},{1... | collective-permute-start | bytes 5308424 | tf_op jit(solution)/shard_map/ppermute | solution.py:580

commit v4 on v3

--- a/solution.py
+++ b/solution.py
@@ -387,7 +387,7 @@
     outs, (own, got, made, sems) = refs[:8], refs[8:]
     _, core, side, rep = place_of()
     part = lambda n: pl.ds((rep ^ (n // 2)) * 2 + (side ^ (n % 2)), 1)
-    order = (4, 5, 2, 3, 6, 7, 1, 0)
+    order = (5, 3, 7, 1, 4, 2, 6, 0)
     for k, (mine, theirs) in enumerate(((first, got_first), (second, got_second))):
 
         @pl.when(core == k)
@@ -408,9 +408,9 @@
 
 
 def add_kernel(*refs):
-    total = refs[0][0].astype(f32)
+    total = refs[0][...].astype(f32)
     for ref in refs[1:-1]:
-        total = total + ref[0].astype(f32)
+        total = total + ref[...].astype(f32)
     refs[-1][...] = total.astype(bf16)
 
 
@@ -580,16 +580,6 @@
     return lax.ppermute(array, axis, [(i, i ^ distance) for i in range(lax.axis_size(axis))])
 
 
-def trade(array, over_rep, over_side):
-    if not over_rep and not over_side:
-        return array
-    lon, rep = lax.axis_size("lon"), lax.axis_size("rep")
-    pairs = [
-        (i * rep + j, (i ^ (2 * over_side)) * rep + (j ^ over_rep)) for i in range(lon) for j in range(rep)
-    ]
-    return lax.ppermute(array, ("lon", "rep"), pairs)
-
-
 def body(
     fields, upstream, scales, offsets, inward, inbias, outward, outbias, expand, upbias, narrow, downbias,
     tables, window_type, row_valid,
@@ -661,12 +651,14 @@
         [pltpu.VMEM((8,) + part.shape, bf16)] * 3 + [pltpu.SemaphoreType.DMA((24,))],
         raw_outs=8,
     )
-    dealt = [trade(m, n // 2, n % 2) for n, m in enumerate(dealt)]
-    (a,) = call(add_kernel, near(*dealt), [of((CHUNK, 2 * C), bf16)], limit=SMALL)
+    over = lambda parts: [parts[0]] + [swap(parts[d], "rep", d) for d in (1, 2, 3)]
+    give = call(add_kernel, near(*over(dealt[1::2])), [part], limit=SMALL)[0]
+    a = call(add_kernel, near(*over(dealt[0::2]), swap(give, "lon", 2)), [part], limit=SMALL)[0][0]
     for step, height in ((1, CHUNK + 32), (4, CHUNK + 128)):
         others = [swap(a, "lat", step * i) for i in (1, 2, 3)]
         (a,) = call(band_kernel, near(a, *others), [of((height, 2 * C), bf16)], limit=SMALL)
-    a = jnp.stack([trade(a, n // 2, n % 2) for n in range(8)]).reshape((4, 2) + a.shape)
+    beside = swap(a, "lon", 2)
+    a = jnp.stack([m for pair in zip(over([a] * 4), over([beside] * 4)) for m in pair]).reshape((4, 2) + a.shape)
     got = swap(a, "lon", 1)
 
     factor = 1.0 / math.sqrt(lax.axis_size("rep") * levels * total_rows * col_count * lax.axis_size("lon"))

time: 150 us -> 138 us (0.920); the launches traced: 149 us -> 135 us
  waiting for transfers between devices: 55.7 us -> 43.7 us
  starting transfers between devices: 47.8 us -> 45.6 us
    ppermute x14 -> x0, waiting for transfers between devices: 27.4 us -> none  [trade(): return lax.ppermute(array, ('lon', 'rep'), pairs)]
    ppermute x14 -> x0, starting transfers between devices: 19.1 us -> none  [trade(): return lax.ppermute(array, ('lon', 'rep'), pairs)]
    ppermute x9 -> x23, starting transfers between devices: 14.9 us -> 31.8 us  [swap(): lax.ppermute(array, axis, [(i, i ^ distance) for i in range(lax.axis_size...]
    ppermute x9 -> x23, waiting for transfers between devices: 21.8 us -> 37.2 us  [swap(): lax.ppermute(array, axis, [(i, i ^ distance) for i in range(lax.axis_size...]
    pallas_call x9 -> x10, Pallas kernels: 37.3 us -> 37.3 us  [call(): pl.pallas_call(wrapped, grid=(1,), in_specs=specs, out_specs=out_specs, o...]
  transfers between devices with their start and end apart: 29 -> 29, of which waited for: 14 -> 16; matrix products, arithmetic and copies ran while one was open for 2% -> 2% of each run, Pallas kernels for 8% -> 9%
where the time goes in v4:
time: 138 us; the launch traced here: 135 us
  starting transfers between devices  45.6 us (33%)
  waiting for transfers between devices  43.7 us (32%)
  Pallas kernels  37.3 us (27%)
  local copies, waits for them, and re-layouts  7.48 us (5%)
    pallas_call x10, Pallas kernels, call(): pl.pallas_call(wrapped, grid=(1,), in_specs=specs, out_specs=out_specs, o...  37.3 us
    ppermute x23, waiting for transfers between devices, swap(): lax.ppermute(array, axis, [(i, i ^ distance) for i in range(lax.axis_size...  37.2 us
    ppermute x23, starting transfers between devices, swap(): lax.ppermute(array, axis, [(i, i ^ distance) for i in range(lax.axis_size...  31.8 us
    ppermute x2, starting transfers between devices, send_pieces(): lax.ppermute(pieces[1], 'lat', rows)  10.5 us
    ppermute x2, waiting for transfers between devices, send_pieces(): lax.ppermute(pieces[1], 'lat', rows)  4 us
    reshape x2, local copies, waits for them, and re-layouts, body(): m.reshape(row_count, col_count, levels, C).transpose(2, 0, 1, 3)[None]  3.12 us
  transfers between devices with their start and end apart: 29, of which 16 were waited for; matrix products, arithmetic and copies ran while one was open for 2% of the time, Pallas kernels for 9%

profile of v4, /device:TPU:1, one launch (start us, length us, event | category | flops | bytes accessed | tf_op | source)
XLA Modules:
  0.0 135.1 jit_solution(7528192948641417464)
XLA Ops:
  0.6 1.6 %reshape.41.refs_2_.refs_4_ = bf16[144,192]{1,0:T(8,128)(2,1)} reshape(bf16[6,12,2,192]{3,2,1,0:T(2,128)(2,1)} %bitcast.45) | data formatting | bytes 110592 | tf_op jit(solution)/shard_map/reshape | solution.py:590
  2.2 1.6 %reshape.42.refs_3_ = bf16[144,192]{1,0:T(8,128)(2,1)} reshape(bf16[6,12,2,192]{3,2,1,0:T(2,128)(2,1)} %bitcast.46) | data formatting | bytes 110592 | tf_op jit(solution)/shard_map/reshape | solution.py:591
  3.8 8.8 %shard_map.300 = (bf16[144,192]{1,0:T(8,128)(2,1)}, bf16[256,192]{1,0:T(8,128)(2,1)}, bf16[256,192]{1,0:T(8,128)(2,1)}, bf16[6,144,256]{2,1,0:T(8,128)(2,1)}, bf...) custom-call(s32[2,1,16]{2,1,0:T(1,128)} %refs_0_.5, ...), custom_call_target="tpu_custom_call" | custom-call | flops 1000000000 | bytes 8403968 | tf_op jit(solution)/shard_map/pallas_call | solution.py:553
  12.6 8.9 %collective-permute-start = (bf16[96,192]{1,0:T(8,128)(2,1)}, bf16[96,192]{1,0:T(8,128)(2,1)}, u32[]{:S(2)}, u32[]{:S(2)}) collective-permute-start(bf16[96,192]{1,0:T(8,128)(2,1)} %get-tuple-element.51), channel_id=1, source_target_pairs={{0,240},{16,0},{32,16},{48,32},{64,48},{80,64},{96,80},{112,96},{1... | collective-permute-start | bytes 110600 | tf_op jit(solution)/shard_map/ppermute | solution.py:573
  21.6 1.0 collective-permute-start.1
  22.5 1.4 %collective-permute-start.2 = (bf16[96,192]{1,0:T(8,128)(2,1)}, bf16[96,192]{1,0:T(8,128)(2,1)}, u32[]{:S(2)}, u32[]{:S(2)}) collective-permute-start(bf16[96,192]{1,0:T(8,128)(2,1)} %get-tuple-element.53), channel_id=1, source_target_pairs={{0,252},{4,240},{8,244},{12,248},{16,12},{20,0},{24,4},{28,8},{32,... | collective-permute-start | bytes 110600 | tf_op jit(solution)/shard_map/ppermute | solution.py:575
  23.9 5.0 %shard_map.301.refs_14_ = f32[144,1536]{1,0:T(8,128)} custom-call(s32[2,1,16]{2,1,0:T(1,128)} %refs_0_.5, s32[96]{0:T(128)} %refs_1_.3, f32[2,6,16,3312]{3,2,1,0:T(8,128)} %bitcast.44, bf16[256,1536]{1,0:T(8,128)(2,1)} %constant.17.clone.refs_17_.refs_3_.refs_16_.refs_21_, f32[144,192]{1,0:T(8,128)} %constant.15.clone.refs_18_.refs_4_.refs_17_.refs_22_, ...), custom_call_target="tpu_custom_call" | custom-call | flops 1000000000 | bytes 4473344 | tf_op jit(solution)/shard_map/pallas_call | solution.py:553
  28.9 0.0 collective-permute-done.refs_1_
  28.9 0.0 collective-permute-done.1.refs_2_
  28.9 9.2 %shard_map.302 = (bf16[8,160,384]{2,1,0:T(8,128)(2,1)}, bf16[96,192]{1,0:T(8,128)(2,1)}, bf16[96,192]{1,0:T(8,128)(2,1)}, bf16[96,192]{1,0:T(8,128)(2,1)}, bf16[96,192]{1,0:T(8,128)(2,1)}) custom-call(bf16[96,192]{1,0:T(8,128)(2,1)} %get-tuple-element.50.refs_0_, bf16[96,192]{1,0:T(8,128)(2,1)} %collective-permute-done.refs_1_, ...), custom_call_target="tpu_custom_call" | custom-call | flops 1000000000 | bytes 6876672 | tf_op jit(solution)/shard_map/pallas_call | solution.py:553
  38.2 1.6 %collective-permute-start.3 = (bf16[96,192]{1,0:T(8,128)(2,1)}, bf16[96,192]{1,0:T(8,128)(2,1)}, u32[]{:S(2)}, u32[]{:S(2)}) collective-permute-start(bf16[96,192]{1,0:T(8,128)(2,1)} %get-tuple-element.55), channel_id=1, source_target_pairs={{0,16},{16,32},{32,48},{48,64},{64,80},{80,96},{96,112},{112,128},... | collective-permute-start | bytes 110600 | tf_op jit(solution)/shard_map/ppermute | solution.py:573
  39.7 1.0 collective-permute-start.4
  40.7 0.0 collective-permute-start.5
  40.7 1.0 collective-permute-start.7
  41.7 4.0 %collective-permute-done.3.refs_1_ = bf16[96,192]{1,0:T(8,128)(2,1)} collective-permute-done((bf16[96,192]{1,0:T(8,128)(2,1)}, bf16[96,192]{1,0:T(8,128)(2,1)}, u32[]{:S(2)}, u32[]{:S(2)}) %collective-permute-start.3) | collective-permute-done | bytes 36896 | tf_op jit(solution)/shard_map/ppermute | solution.py:573
  45.7 0.0 collective-permute-done.4.refs_2_
  45.7 2.5 %collective-permute-done.5.refs_3_ = bf16[96,192]{1,0:T(8,128)(2,1)} collective-permute-done((bf16[96,192]{1,0:T(8,128)(2,1)}, bf16[96,192]{1,0:T(8,128)(2,1)}, u32[]{:S(2)}, u32[]{:S(2)}) %collective-permute-start.5) | collective-permute-done | bytes 36896 | tf_op jit(solution)/shard_map/ppermute | solution.py:575
  48.1 7.1 %shard_map.303 = (bf16[144,192]{1,0:T(8,128)(2,1)}, bf16[144,192]{1,0:T(8,128)(2,1)}, bf16[8,160,384]{2,1,0:T(8,128)(2,1)}) custom-call(bf16[96,192]{1,0:T(8,128)(2,1)} %get-tuple-element.54.refs_0_, bf16[96,192]{1,0:T(8,128)(2,1)} %collective-permute-done.3.refs_1_, bf16[96,192]{1,0:T(8,128)(2,1)} %collective-permute-done.4.refs_2_, ...), custom_call_target="tpu_custom_call" | custom-call | flops 1000000000 | bytes 6892032 | tf_op jit(solution)/shard_map/pallas_call | solution.py:553
  55.2 0.1 collective-permute-start.6
  55.4 2.9 %collective-permute-done.6.refs_2_ = bf16[8,160,384]{2,1,0:T(8,128)(2,1)} collective-permute-done((bf16[8,160,384]{2,1,0:T(8,128)(2,1)}, bf16[8,160,384]{2,1,0:T(8,128)(2,1)}, u32[]{:S(2)}, u32[]{:S(2)}) %collective-permute-start.6) | collective-permute-done | bytes 983072 | tf_op jit(solution)/shard_map/ppermute | solution.py:580
  58.2 2.5 %shard_map.304 = (bf16[1,160,384]{2,1,0:T(8,128)(2,1)}, bf16[1,160,384]{2,1,0:T(8,128)(2,1)}, bf16[1,160,384]{2,1,0:T(8,128)(2,1)}, bf16[1,160,384]{2,1,0:T(8,12...) custom-call(bf16[8,160,384]{2,1,0:T(8,128)(2,1)} %get-tuple-element., ...), custom_call_target="tpu_custom_call" | custom-call | flops 1000000000 | bytes 4915200 | tf_op jit(solution)/shard_map/pallas_call | solution.py:553
  60.7 1.4 %collective-permute-start.11 = (bf16[1,160,384]{2,1,0:T(8,128)(2,1)}, bf16[1,160,384]{2,1,0:T(8,128)(2,1)S(1)}, u32[]{:S(2)}, u32[]{:S(2)}) collective-permute-start(bf16[1,160,384]{2,1,0:T(8,128)(2,1)} %get-tuple-element.73), channel_id=1, source_target_pairs={{0,1},{1,0},{2,3},{3,2},{4,5},{5,4},{6,7},{7,6},{8,9},{9,8},{10,11... | collective-permute-start | bytes 368648 | tf_op jit(solution)/shard_map/ppermute | solution.py:580
  62.1 2.6 %collective-permute-start.12 = (bf16[1,160,384]{2,1,0:T(8,128)(2,1)}, bf16[1,160,384]{2,1,0:T(8,128)(2,1)S(1)}, u32[]{:S(2)}, u32[]{:S(2)}) collective-permute-start(bf16[1,160,384]{2,1,0:T(8,128)(2,1)} %get-tuple-element.74), channel_id=1, source_target_pairs={{0,2},{1,3},{2,0},{3,1},{4,6},{5,7},{6,4},{7,5},{8,10},{9,11},{10,... | collective-permute-start | bytes 368648 | tf_op jit(solution)/shard_map/ppermute | solution.py:580
  64.7 0.0 collective-permute-start.8
  64.7 3.8 %collective-permute-start.9 = (bf16[1,160,384]{2,1,0:T(8,128)(2,1)}, bf16[1,160,384]{2,1,0:T(8,128)(2,1)S(1)}, u32[]{:S(2)}, u32[]{:S(2)}) collective-permute-start(bf16[1,160,384]{2,1,0:T(8,128)(2,1)} %get-tuple-element.70), channel_id=1, source_target_pairs={{0,2},{1,3},{2,0},{3,1},{4,6},{5,7},{6,4},{7,5},{8,10},{9,11},{10,... | collective-permute-start | bytes 368648 | tf_op jit(solution)/shard_map/ppermute | solution.py:580
  68.6 2.3 %collective-permute-done.12.refs_2_ = bf16[1,160,384]{2,1,0:T(8,128)(2,1)S(1)} collective-permute-done((bf16[1,160,384]{2,1,0:T(8,128)(2,1)}, bf16[1,160,384]{2,1,0:T(8,128)(2,1)S(1)}, u32[]{:S(2)}, u32[]{:S(2)}) %collective-permute-start.12) | collective-permute-done | bytes 122912 | tf_op jit(solution)/shard_map/ppermute | solution.py:580
  70.9 2.5 %collective-permute-done.13.refs_3_ = bf16[1,160,384]{2,1,0:T(8,128)(2,1)S(1)} collective-permute-done((bf16[1,160,384]{2,1,0:T(8,128)(2,1)}, bf16[1,160,384]{2,1,0:T(8,128)(2,1)S(1)}, u32[]{:S(2)}, u32[]{:S(2)}) %collective-permute-start.13) | collective-permute-done | bytes 122912 | tf_op jit(solution)/shard_map/ppermute | solution.py:580
  73.4 0.9 copy-done.2
  74.3 0.1 shard_map.305
  74.4 0.4 collective-permute-start.14
  74.8 1.4 %collective-permute-done.9.refs_2_ = bf16[1,160,384]{2,1,0:T(8,128)(2,1)S(1)} collective-permute-done((bf16[1,160,384]{2,1,0:T(8,128)(2,1)}, bf16[1,160,384]{2,1,0:T(8,128)(2,1)S(1)}, u32[]{:S(2)}, u32[]{:S(2)}) %collective-permute-start.9) | collective-permute-done | bytes 122912 | tf_op jit(solution)/shard_map/ppermute | solution.py:580
  76.2 2.5 %collective-permute-done.10.refs_3_ = bf16[1,160,384]{2,1,0:T(8,128)(2,1)S(1)} collective-permute-done((bf16[1,160,384]{2,1,0:T(8,128)(2,1)}, bf16[1,160,384]{2,1,0:T(8,128)(2,1)S(1)}, u32[]{:S(2)}, u32[]{:S(2)}) %collective-permute-start.10) | collective-permute-done | bytes 122912 | tf_op jit(solution)/shard_map/ppermute | solution.py:580
  78.7 0.0 collective-permute-done.14.refs_4_
  78.7 0.1 shard_map.306
  78.8 0.1 collective-permute-start.17
  78.9 0.1 collective-permute-start.16
  79.0 4.0 %collective-permute-start.15 = (bf16[160,384]{1,0:T(8,128)(2,1)S(1)}, bf16[160,384]{1,0:T(8,128)(2,1)S(1)}, u32[]{:S(2)}, u32[]{:S(2)}) collective-permute-start(bf16[160,384]{1,0:T(8,128)(2,1)S(1)} %bitcast.38), channel_id=1, source_target_pairs={{0,16},{16,0},{32,48},{48,32},{64,80},{80,64},{96,112},{112,96},{1... | collective-permute-start | bytes 368648 | tf_op jit(solution)/shard_map/ppermute | solution.py:580
  83.0 2.1 %collective-permute-done.17.refs_3_ = bf16[160,384]{1,0:T(8,128)(2,1)S(1)} collective-permute-done((bf16[160,384]{1,0:T(8,128)(2,1)S(1)}, bf16[160,384]{1,0:T(8,128)(2,1)S(1)}, u32[]{:S(2)}, u32[]{:S(2)}) %collective-permute-start.17) | collective-permute-done | bytes 122912 | tf_op jit(solution)/shard_map/ppermute | solution.py:580
  85.1 1.2 collective-permute-done.15.refs_1_
  86.3 0.1 shard_map.307.refs_0_
  86.4 0.1 collective-permute-start.20
  86.5 2.3 %collective-permute-start.19 = (bf16[192,384]{1,0:T(8,128)(2,1)S(1)}, bf16[192,384]{1,0:T(8,128)(2,1)S(1)}, u32[]{:S(2)}, u32[]{:S(2)}) collective-permute-start(bf16[192,384]{1,0:T(8,128)(2,1)S(1)} %shard_map.307.refs_0_), channel_id=1, source_target_pairs={{0,128},{16,144},{32,160},{48,176},{64,192},{80,208},{96,224},{112... | collective-permute-start | bytes 442376 | tf_op jit(solution)/shard_map/ppermute | solution.py:580
  88.8 3.3 %collective-permute-start.18 = (bf16[192,384]{1,0:T(8,128)(2,1)S(1)}, bf16[192,384]{1,0:T(8,128)(2,1)S(1)}, u32[]{:S(2)}, u32[]{:S(2)}) collective-permute-start(bf16[192,384]{1,0:T(8,128)(2,1)S(1)} %shard_map.307.refs_0_), channel_id=1, source_target_pairs={{0,64},{16,80},{32,96},{48,112},{64,0},{80,16},{96,32},{112,48},{1... | collective-permute-start | bytes 442376 | tf_op jit(solution)/shard_map/ppermute | solution.py:580
  92.1 0.5 collective-permute-done.20.refs_3_
  92.7 2.7 %collective-permute-done.19.refs_2_ = bf16[192,384]{1,0:T(8,128)(2,1)S(1)} collective-permute-done((bf16[192,384]{1,0:T(8,128)(2,1)S(1)}, bf16[192,384]{1,0:T(8,128)(2,1)S(1)}, u32[]{:S(2)}, u32[]{:S(2)}) %collective-permute-start.19) | collective-permute-done | bytes 147488 | tf_op jit(solution)/shard_map/ppermute | solution.py:580
  95.4 6.0 %collective-permute-done.18.refs_1_ = bf16[192,384]{1,0:T(8,128)(2,1)S(1)} collective-permute-done((bf16[192,384]{1,0:T(8,128)(2,1)S(1)}, bf16[192,384]{1,0:T(8,128)(2,1)S(1)}, u32[]{:S(2)}, u32[]{:S(2)}) %collective-permute-start.18) | collective-permute-done | bytes 147488 | tf_op jit(solution)/shard_map/ppermute | solution.py:580
  101.4 0.1 shard_map.308
  101.5 3.9 %collective-permute-start.26 = (bf16[288,384]{1,0:T(8,128)(2,1)S(1)}, bf16[288,384]{1,0:T(8,128)(2,1)S(1)}, u32[]{:S(2)}, u32[]{:S(2)}) collective-permute-start(bf16[288,384]{1,0:T(8,128)(2,1)S(1)} %shard_map.308), channel_id=1, source_target_pairs={{0,3},{1,2},{2,1},{3,0},{4,7},{5,6},{6,5},{7,4},{8,11},{9,10},{10,... | collective-permute-start | bytes 663560 | tf_op jit(solution)/shard_map/ppermute | solution.py:580
  105.4 0.0 collective-permute-start.24
  105.4 0.7 collective-permute-start.22
  106.0 0.7 collective-permute-start.21
  106.8 0.0 copy-start
  106.8 4.3 %collective-permute-done.21 = bf16[288,384]{1,0:T(8,128)(2,1)S(1)} collective-permute-done((bf16[288,384]{1,0:T(8,128)(2,1)S(1)}, bf16[288,384]{1,0:T(8,128)(2,1)S(1)}, u32[]{:S(2)}, u32[]{:S(2)}) %collective-permute-start.21) | collective-permute-done | bytes 221216 | tf_op jit(solution)/shard_map/ppermute | solution.py:580
  111.1 2.6 %collective-permute-start.27 = (bf16[288,384]{1,0:T(8,128)(2,1)S(1)}, bf16[288,384]{1,0:T(8,128)(2,1)S(1)}, u32[]{:S(2)}, u32[]{:S(2)}) collective-permute-start(bf16[288,384]{1,0:T(8,128)(2,1)S(1)} %collective-permute-done.21), channel_id=1, source_target_pairs={{0,3},{1,2},{2,1},{3,0},{4,7},{5,6},{6,5},{7,4},{8,11},{9,10},{10,... | collective-permute-start | bytes 663560 | tf_op jit(solution)/shard_map/ppermute | solution.py:580
  113.7 0.0 collective-permute-start.25
  113.7 1.6 %collective-permute-start.23 = (bf16[288,384]{1,0:T(8,128)(2,1)S(1)}, bf16[288,384]{1,0:T(8,128)(2,1)S(1)}, u32[]{:S(2)}, u32[]{:S(2)}) collective-permute-start(bf16[288,384]{1,0:T(8,128)(2,1)S(1)} %collective-permute-done.21), channel_id=1, source_target_pairs={{0,1},{1,0},{2,3},{3,2},{4,5},{5,4},{6,7},{7,6},{8,9},{9,8},{10,11... | collective-permute-start | bytes 663560 | tf_op jit(solution)/shard_map/ppermute | solution.py:580
  115.4 6.3 %collective-permute-done.23 = bf16[288,384]{1,0:T(8,128)(2,1)S(1)} collective-permute-done((bf16[288,384]{1,0:T(8,128)(2,1)S(1)}, bf16[288,384]{1,0:T(8,128)(2,1)S(1)}, u32[]{:S(2)}, u32[]{:S(2)}) %collective-permute-start.23) | collective-permute-done | bytes 221216 | tf_op jit(solution)/shard_map/ppermute | solution.py:580
  121.7 0.0 collective-permute-done.24
  121.8 2.2 %collective-permute-done.27 = bf16[288,384]{1,0:T(8,128)(2,1)S(1)} collective-permute-done((bf16[288,384]{1,0:T(8,128)(2,1)S(1)}, bf16[288,384]{1,0:T(8,128)(2,1)S(1)}, u32[]{:S(2)}, u32[]{:S(2)}) %collective-permute-start.27) | collective-permute-done | bytes 221216 | tf_op jit(solution)/shard_map/ppermute | solution.py:580
  124.1 3.1 %collective-permute-start.28 = (bf16[4,2,288,384]{3,2,1,0:T(8,128)(2,1)S(1)}, bf16[4,2,288,384]{3,2,1,0:T(8,128)(2,1)S(1)}, u32[]{:S(2)}, u32[]{:S(2)}) collective-permute-start(bf16[4,2,288,384]{3,2,1,0:T(8,128)(2,1)S(1)} %bitcast.34), channel_id=1, source_target_pairs={{0,4},{4,0},{8,12},{12,8},{1,5},{5,1},{9,13},{13,9},{2,6},{6,2},{1... | collective-permute-start | bytes 5308424 | tf_op jit(solution)/shard_map/ppermute | solution.py:580
  127.2 1.6 %reshape.43 = bf16[6,12,2,192]{3,2,1,0:T(2,128)(2,1)} reshape(bf16[144,192]{1,0:T(8,128)(2,1)} %get-tuple-element.64) | data formatting | bytes 110592 | tf_op jit(solution)/shard_map/reshape | solution.py:679
  128.7 1.6 %reshape.44 = bf16[6,12,2,192]{3,2,1,0:T(2,128)(2,1)} reshape(bf16[144,192]{1,0:T(8,128)(2,1)} %get-tuple-element.65) | data formatting | bytes 110592 | tf_op jit(solution)/shard_map/reshape | solution.py:679
  130.3 0.2 collective-permute-done.28.refs_2_
  130.5 4.4 %shard_map.309 = (f32[2,192,576]{2,1,0:T(8,128)}, f32[2,192,192]{2,1,0:T(8,128)}, f32[2,192,768]{2,1,0:T(8,128)}, f32[2,192,768]{2,1,0:T(8,128)}, f32[2,6,16,331...) custom-call(s32[2,1,16]{2,1,0:T(1,128)S(1)} %copy-done, ...), custom_call_target="tpu_custom_call" | custom-call | flops 1000000000 | bytes 9641600 | tf_op jit(solution)/shard_map/pallas_call | solution.py:553
  (22 shorter events, 0.3 us)
Async XLA Ops:
  12.6 16.3 %collective-permute-start = (bf16[96,192]{1,0:T(8,128)(2,1)}, bf16[96,192]{1,0:T(8,128)(2,1)}, u32[]{:S(2)}, u32[]{:S(2)}) collective-permute-start(bf16[96,192]{1,0:T(8,128)(2,1)} %get-tuple-element.51), channel_id=1, source_target_pairs={{0,240},{16,0},{32,16},{48,32},{64,48},{80,64},{96,80},{112,96},{1... | collective-permute-start | bytes 110600 | tf_op jit(solution)/shard_map/ppermute | solution.py:573
  21.6 7.4 %collective-permute-start.1 = (bf16[96,192]{1,0:T(8,128)(2,1)}, bf16[96,192]{1,0:T(8,128)(2,1)}, u32[]{:S(2)}, u32[]{:S(2)}) collective-permute-start(bf16[96,192]{1,0:T(8,128)(2,1)} %get-tuple-element.52), channel_id=1, source_target_pairs={{0,12},{4,0},{8,4},{12,8},{1,13},{5,1},{9,5},{13,9},{2,14},{6,2},{... | collective-permute-start | bytes 110600 | tf_op jit(solution)/shard_map/ppermute | solution.py:574
  22.5 6.4 %collective-permute-start.2 = (bf16[96,192]{1,0:T(8,128)(2,1)}, bf16[96,192]{1,0:T(8,128)(2,1)}, u32[]{:S(2)}, u32[]{:S(2)}) collective-permute-start(bf16[96,192]{1,0:T(8,128)(2,1)} %get-tuple-element.53), channel_id=1, source_target_pairs={{0,252},{4,240},{8,244},{12,248},{16,12},{20,0},{24,4},{28,8},{32,... | collective-permute-start | bytes 110600 | tf_op jit(solution)/shard_map/ppermute | solution.py:575
  38.2 7.5 %collective-permute-start.3 = (bf16[96,192]{1,0:T(8,128)(2,1)}, bf16[96,192]{1,0:T(8,128)(2,1)}, u32[]{:S(2)}, u32[]{:S(2)}) collective-permute-start(bf16[96,192]{1,0:T(8,128)(2,1)} %get-tuple-element.55), channel_id=1, source_target_pairs={{0,16},{16,32},{32,48},{48,64},{64,80},{80,96},{96,112},{112,128},... | collective-permute-start | bytes 110600 | tf_op jit(solution)/shard_map/ppermute | solution.py:573
  39.7 5.9 %collective-permute-start.4 = (bf16[96,192]{1,0:T(8,128)(2,1)}, bf16[96,192]{1,0:T(8,128)(2,1)}, u32[]{:S(2)}, u32[]{:S(2)}) collective-permute-start(bf16[96,192]{1,0:T(8,128)(2,1)} %get-tuple-element.56), channel_id=1, source_target_pairs={{0,4},{4,8},{8,12},{12,0},{1,5},{5,9},{9,13},{13,1},{2,6},{6,10},{... | collective-permute-start | bytes 110600 | tf_op jit(solution)/shard_map/ppermute | solution.py:574
  40.7 7.4 %collective-permute-start.5 = (bf16[96,192]{1,0:T(8,128)(2,1)}, bf16[96,192]{1,0:T(8,128)(2,1)}, u32[]{:S(2)}, u32[]{:S(2)}) collective-permute-start(bf16[96,192]{1,0:T(8,128)(2,1)} %get-tuple-element.57), channel_id=1, source_target_pairs={{0,20},{4,24},{8,28},{12,16},{16,36},{20,40},{24,44},{28,32},{32,5... | collective-permute-start | bytes 110600 | tf_op jit(solution)/shard_map/ppermute | solution.py:575
  40.7 14.6 %collective-permute-start.7 = (bf16[8,160,384]{2,1,0:T(8,128)(2,1)}, bf16[8,160,384]{2,1,0:T(8,128)(2,1)}, u32[]{:S(2)}, u32[]{:S(2)}) collective-permute-start(bf16[8,160,384]{2,1,0:T(8,128)(2,1)} %get-tuple-element.67.refs_1_), channel_id=1, source_target_pairs={{0,4},{4,0},{8,12},{12,8},{1,5},{5,1},{9,13},{13,9},{2,6},{6,2},{1... | collective-permute-start | bytes 2949128 | tf_op jit(solution)/shard_map/ppermute | solution.py:580
  55.2 3.0 %collective-permute-start.6 = (bf16[8,160,384]{2,1,0:T(8,128)(2,1)}, bf16[8,160,384]{2,1,0:T(8,128)(2,1)}, u32[]{:S(2)}, u32[]{:S(2)}) collective-permute-start(bf16[8,160,384]{2,1,0:T(8,128)(2,1)} %get-tuple-element.66.refs_0_), channel_id=1, source_target_pairs={{0,4},{4,0},{8,12},{12,8},{1,5},{5,1},{9,13},{13,9},{2,6},{6,2},{1... | collective-permute-start | bytes 2949128 | tf_op jit(solution)/shard_map/ppermute | solution.py:580
  60.7 7.9 %collective-permute-start.11 = (bf16[1,160,384]{2,1,0:T(8,128)(2,1)}, bf16[1,160,384]{2,1,0:T(8,128)(2,1)S(1)}, u32[]{:S(2)}, u32[]{:S(2)}) collective-permute-start(bf16[1,160,384]{2,1,0:T(8,128)(2,1)} %get-tuple-element.73), channel_id=1, source_target_pairs={{0,1},{1,0},{2,3},{3,2},{4,5},{5,4},{6,7},{7,6},{8,9},{9,8},{10,11... | collective-permute-start | bytes 368648 | tf_op jit(solution)/shard_map/ppermute | solution.py:580
  62.1 8.8 %collective-permute-start.12 = (bf16[1,160,384]{2,1,0:T(8,128)(2,1)}, bf16[1,160,384]{2,1,0:T(8,128)(2,1)S(1)}, u32[]{:S(2)}, u32[]{:S(2)}) collective-permute-start(bf16[1,160,384]{2,1,0:T(8,128)(2,1)} %get-tuple-element.74), channel_id=1, source_target_pairs={{0,2},{1,3},{2,0},{3,1},{4,6},{5,7},{6,4},{7,5},{8,10},{9,11},{10,... | collective-permute-start | bytes 368648 | tf_op jit(solution)/shard_map/ppermute | solution.py:580
  64.7 8.7 %collective-permute-start.13 = (bf16[1,160,384]{2,1,0:T(8,128)(2,1)}, bf16[1,160,384]{2,1,0:T(8,128)(2,1)S(1)}, u32[]{:S(2)}, u32[]{:S(2)}) collective-permute-start(bf16[1,160,384]{2,1,0:T(8,128)(2,1)} %get-tuple-element.75), channel_id=1, source_target_pairs={{0,3},{1,2},{2,1},{3,0},{4,7},{5,6},{6,5},{7,4},{8,11},{9,10},{10,... | collective-permute-start | bytes 368648 | tf_op jit(solution)/shard_map/ppermute | solution.py:580
  64.7 10.1 %collective-permute-start.8 = (bf16[1,160,384]{2,1,0:T(8,128)(2,1)}, bf16[1,160,384]{2,1,0:T(8,128)(2,1)S(1)}, u32[]{:S(2)}, u32[]{:S(2)}) collective-permute-start(bf16[1,160,384]{2,1,0:T(8,128)(2,1)} %get-tuple-element.69), channel_id=1, source_target_pairs={{0,1},{1,0},{2,3},{3,2},{4,5},{5,4},{6,7},{7,6},{8,9},{9,8},{10,11... | collective-permute-start | bytes 368648 | tf_op jit(solution)/shard_map/ppermute | solution.py:580
  64.7 11.5 %collective-permute-start.9 = (bf16[1,160,384]{2,1,0:T(8,128)(2,1)}, bf16[1,160,384]{2,1,0:T(8,128)(2,1)S(1)}, u32[]{:S(2)}, u32[]{:S(2)}) collective-permute-start(bf16[1,160,384]{2,1,0:T(8,128)(2,1)} %get-tuple-element.70), channel_id=1, source_target_pairs={{0,2},{1,3},{2,0},{3,1},{4,6},{5,7},{6,4},{7,5},{8,10},{9,11},{10,... | collective-permute-start | bytes 368648 | tf_op jit(solution)/shard_map/ppermute | solution.py:580
  68.6 10.1 %collective-permute-start.10 = (bf16[1,160,384]{2,1,0:T(8,128)(2,1)}, bf16[1,160,384]{2,1,0:T(8,128)(2,1)S(1)}, u32[]{:S(2)}, u32[]{:S(2)}) collective-permute-start(bf16[1,160,384]{2,1,0:T(8,128)(2,1)} %get-tuple-element.71), channel_id=1, source_target_pairs={{0,3},{1,2},{2,1},{3,0},{4,7},{5,6},{6,5},{7,4},{8,11},{9,10},{10,... | collective-permute-start | bytes 368648 | tf_op jit(solution)/shard_map/ppermute | solution.py:580
  73.4 0.9 copy-start.2
  74.3 4.4 %copy-start.1 = (bf16[1,160,384]{2,1,0:T(8,128)(2,1)S(1)}, bf16[1,160,384]{2,1,0:T(8,128)(2,1)}, u32[]{:S(2)}) copy-start(bf16[1,160,384]{2,1,0:T(8,128)(2,1)} %get-tuple-element.68.refs_0_) | copy-start | bytes 368644
  74.4 4.3 %collective-permute-start.14 = (bf16[1,160,384]{2,1,0:T(8,128)(2,1)S(1)}, bf16[1,160,384]{2,1,0:T(8,128)(2,1)S(1)}, u32[]{:S(2)}, u32[]{:S(2)}) collective-permute-start(bf16[1,160,384]{2,1,0:T(8,128)(2,1)S(1)} %shard_map.305), channel_id=1, source_target_pairs={{0,8},{4,12},{8,0},{12,4},{1,9},{5,13},{9,1},{13,5},{2,10},{6,14},... | collective-permute-start | bytes 368648 | tf_op jit(solution)/shard_map/ppermute | solution.py:580
  78.8 6.3 %collective-permute-start.17 = (bf16[160,384]{1,0:T(8,128)(2,1)S(1)}, bf16[160,384]{1,0:T(8,128)(2,1)S(1)}, u32[]{:S(2)}, u32[]{:S(2)}) collective-permute-start(bf16[160,384]{1,0:T(8,128)(2,1)S(1)} %bitcast.36), channel_id=1, source_target_pairs={{0,48},{16,32},{32,16},{48,0},{64,112},{80,96},{96,80},{112,64},{1... | collective-permute-start | bytes 368648 | tf_op jit(solution)/shard_map/ppermute | solution.py:580
  78.9 6.2 %collective-permute-start.16 = (bf16[160,384]{1,0:T(8,128)(2,1)S(1)}, bf16[160,384]{1,0:T(8,128)(2,1)S(1)}, u32[]{:S(2)}, u32[]{:S(2)}) collective-permute-start(bf16[160,384]{1,0:T(8,128)(2,1)S(1)} %bitcast.37), channel_id=1, source_target_pairs={{0,32},{16,48},{32,0},{48,16},{64,96},{80,112},{96,64},{112,80},{1... | collective-permute-start | bytes 368648 | tf_op jit(solution)/shard_map/ppermute | solution.py:580
  79.0 7.3 %collective-permute-start.15 = (bf16[160,384]{1,0:T(8,128)(2,1)S(1)}, bf16[160,384]{1,0:T(8,128)(2,1)S(1)}, u32[]{:S(2)}, u32[]{:S(2)}) collective-permute-start(bf16[160,384]{1,0:T(8,128)(2,1)S(1)} %bitcast.38), channel_id=1, source_target_pairs={{0,16},{16,0},{32,48},{48,32},{64,80},{80,64},{96,112},{112,96},{1... | collective-permute-start | bytes 368648 | tf_op jit(solution)/shard_map/ppermute | solution.py:580
  86.4 6.3 %collective-permute-start.20 = (bf16[192,384]{1,0:T(8,128)(2,1)S(1)}, bf16[192,384]{1,0:T(8,128)(2,1)S(1)}, u32[]{:S(2)}, u32[]{:S(2)}) collective-permute-start(bf16[192,384]{1,0:T(8,128)(2,1)S(1)} %shard_map.307.refs_0_), channel_id=1, source_target_pairs={{0,192},{16,208},{32,224},{48,240},{64,128},{80,144},{96,160},{112... | collective-permute-start | bytes 442376 | tf_op jit(solution)/shard_map/ppermute | solution.py:580
  86.5 8.9 %collective-permute-start.19 = (bf16[192,384]{1,0:T(8,128)(2,1)S(1)}, bf16[192,384]{1,0:T(8,128)(2,1)S(1)}, u32[]{:S(2)}, u32[]{:S(2)}) collective-permute-start(bf16[192,384]{1,0:T(8,128)(2,1)S(1)} %shard_map.307.refs_0_), channel_id=1, source_target_pairs={{0,128},{16,144},{32,160},{48,176},{64,192},{80,208},{96,224},{112... | collective-permute-start | bytes 442376 | tf_op jit(solution)/shard_map/ppermute | solution.py:580
  88.8 12.6 %collective-permute-start.18 = (bf16[192,384]{1,0:T(8,128)(2,1)S(1)}, bf16[192,384]{1,0:T(8,128)(2,1)S(1)}, u32[]{:S(2)}, u32[]{:S(2)}) collective-permute-start(bf16[192,384]{1,0:T(8,128)(2,1)S(1)} %shard_map.307.refs_0_), channel_id=1, source_target_pairs={{0,64},{16,80},{32,96},{48,112},{64,0},{80,16},{96,32},{112,48},{1... | collective-permute-start | bytes 442376 | tf_op jit(solution)/shard_map/ppermute | solution.py:580
  101.5 20.3 %collective-permute-start.26 = (bf16[288,384]{1,0:T(8,128)(2,1)S(1)}, bf16[288,384]{1,0:T(8,128)(2,1)S(1)}, u32[]{:S(2)}, u32[]{:S(2)}) collective-permute-start(bf16[288,384]{1,0:T(8,128)(2,1)S(1)} %shard_map.308), channel_id=1, source_target_pairs={{0,3},{1,2},{2,1},{3,0},{4,7},{5,6},{6,5},{7,4},{8,11},{9,10},{10,... | collective-permute-start | bytes 663560 | tf_op jit(solution)/shard_map/ppermute | solution.py:580
  105.4 16.3 %collective-permute-start.24 = (bf16[288,384]{1,0:T(8,128)(2,1)S(1)}, bf16[288,384]{1,0:T(8,128)(2,1)S(1)}, u32[]{:S(2)}, u32[]{:S(2)}) collective-permute-start(bf16[288,384]{1,0:T(8,128)(2,1)S(1)} %shard_map.308), channel_id=1, source_target_pairs={{0,2},{1,3},{2,0},{3,1},{4,6},{5,7},{6,4},{7,5},{8,10},{9,11},{10,... | collective-permute-start | bytes 663560 | tf_op jit(solution)/shard_map/ppermute | solution.py:580
  105.4 8.4 %collective-permute-start.22 = (bf16[288,384]{1,0:T(8,128)(2,1)S(1)}, bf16[288,384]{1,0:T(8,128)(2,1)S(1)}, u32[]{:S(2)}, u32[]{:S(2)}) collective-permute-start(bf16[288,384]{1,0:T(8,128)(2,1)S(1)} %shard_map.308), channel_id=1, source_target_pairs={{0,1},{1,0},{2,3},{3,2},{4,5},{5,4},{6,7},{7,6},{8,9},{9,8},{10,11... | collective-permute-start | bytes 663560 | tf_op jit(solution)/shard_map/ppermute | solution.py:580
  106.0 5.1 %collective-permute-start.21 = (bf16[288,384]{1,0:T(8,128)(2,1)S(1)}, bf16[288,384]{1,0:T(8,128)(2,1)S(1)}, u32[]{:S(2)}, u32[]{:S(2)}) collective-permute-start(bf16[288,384]{1,0:T(8,128)(2,1)S(1)} %shard_map.308), channel_id=1, source_target_pairs={{0,8},{4,12},{8,0},{12,4},{1,9},{5,13},{9,1},{13,5},{2,10},{6,14},... | collective-permute-start | bytes 663560 | tf_op jit(solution)/shard_map/ppermute | solution.py:580
  106.8 23.7 %copy-start = (s32[2,1,16]{2,1,0:T(1,128)S(1)}, s32[2,1,16]{2,1,0:T(1,128)}, u32[]{:S(2)}) copy-start(s32[2,1,16]{2,1,0:T(1,128)} %refs_0_.5) | copy-start | bytes 388
  111.1 12.9 %collective-permute-start.27 = (bf16[288,384]{1,0:T(8,128)(2,1)S(1)}, bf16[288,384]{1,0:T(8,128)(2,1)S(1)}, u32[]{:S(2)}, u32[]{:S(2)}) collective-permute-start(bf16[288,384]{1,0:T(8,128)(2,1)S(1)} %collective-permute-done.21), channel_id=1, source_target_pairs={{0,3},{1,2},{2,1},{3,0},{4,7},{5,6},{6,5},{7,4},{8,11},{9,10},{10,... | collective-permute-start | bytes 663560 | tf_op jit(solution)/shard_map/ppermute | solution.py:580
  113.7 8.0 %collective-permute-start.25 = (bf16[288,384]{1,0:T(8,128)(2,1)S(1)}, bf16[288,384]{1,0:T(8,128)(2,1)S(1)}, u32[]{:S(2)}, u32[]{:S(2)}) collective-permute-start(bf16[288,384]{1,0:T(8,128)(2,1)S(1)} %collective-permute-done.21), channel_id=1, source_target_pairs={{0,2},{1,3},{2,0},{3,1},{4,6},{5,7},{6,4},{7,5},{8,10},{9,11},{10,... | collective-permute-start | bytes 663560 | tf_op jit(solution)/shard_map/ppermute | solution.py:580
  113.7 7.9 %collective-permute-start.23 = (bf16[288,384]{1,0:T(8,128)(2,1)S(1)}, bf16[288,384]{1,0:T(8,128)(2,1)S(1)}, u32[]{:S(2)}, u32[]{:S(2)}) collective-permute-start(bf16[288,384]{1,0:T(8,128)(2,1)S(1)} %collective-permute-done.21), channel_id=1, source_target_pairs={{0,1},{1,0},{2,3},{3,2},{4,5},{5,4},{6,7},{7,6},{8,9},{9,8},{10,11... | collective-permute-start | bytes 663560 | tf_op jit(solution)/shard_map/ppermute | solution.py:580
  124.1 6.4 %collective-permute-start.28 = (bf16[4,2,288,384]{3,2,1,0:T(8,128)(2,1)S(1)}, bf16[4,2,288,384]{3,2,1,0:T(8,128)(2,1)S(1)}, u32[]{:S(2)}, u32[]{:S(2)}) collective-permute-start(bf16[4,2,288,384]{3,2,1,0:T(8,128)(2,1)S(1)} %bitcast.34), channel_id=1, source_target_pairs={{0,4},{4,0},{8,12},{12,8},{1,5},{5,1},{9,13},{13,9},{2,6},{6,2},{1... | collective-permute-start | bytes 5308424 | tf_op jit(solution)/shard_map/ppermute | solution.py:580

commit v5 on v4

--- a/solution.py
+++ b/solution.py
@@ -428,7 +428,8 @@
             out[CHUNK + 32 * i : CHUNK + 32 * i + 32] = ref[CHUNK:]
 
 
-def final_kernel(factor, types, own, got, *refs):
+def final_kernel(factor, types, own_near, own_far, got_near, got_far, *refs):
+    own, got = (own_near, own_far), (got_near, got_far)
     big, short = refs[:5], refs[5:11]
     inward, outward, expand, narrow, tables, dense, sems = refs[11:]
     scales, offsets, inbias, outbias, upbias, downbias = short
@@ -438,7 +439,7 @@
     part = lax.broadcasted_iota(jnp.int32, (96, 128), 1) & 7
     head = row >> 4
 
-    def unpack(k, ref):
+    def unpack(k, sides, s):
         kind = jnp.zeros((1, 128), jnp.int32)
         for e in range(16):
             kind = kind + jnp.where((lane >> 3) == e, types[k, 0, band ^ e], 0)
@@ -449,10 +450,10 @@
         route = [jnp.where(m, 1.0, 0.0).astype(bf16) for m in made]
         small = []
         for chunk in range(8):
-            y, x = rep ^ (chunk // 2), side ^ (chunk % 2)
-            dense[chunk * ROWS : (chunk + 1) * ROWS] = ref[y, x, :ROWS]
-            small.append(ref[y, x, ROWS:CHUNK].astype(f32)[0:1] * factor)
-            here = ref[y, x, CHUNK:]
+            y, ref = rep ^ (chunk // 2), sides[s ^ (chunk % 2)]
+            dense[chunk * ROWS : (chunk + 1) * ROWS] = ref[y, :ROWS]
+            small.append(ref[y, ROWS:CHUNK].astype(f32)[0:1] * factor)
+            here = ref[y, CHUNK:]
             rows = dot(route[0], here) * factor
             for h in range(HEADS):
                 tables[k, h, :, 384 * chunk : 384 * chunk + 384] = rows[16 * h : 16 * h + 16]
@@ -486,9 +487,11 @@
     for k in range(2):
         for source, wanted in ((own, core == k), (got, core != k)):
 
-            @pl.when(wanted)
-            def _(k=k, source=source):
-                unpack(k, source)
+            for s in range(2):
+
+                @pl.when(wanted & (side == s))
+                def _(k=k, source=source, s=s):
+                    unpack(k, source, s)
 
         for n, array in enumerate((inward, outward, expand, narrow, tables)):
             sent.append(pltpu.make_async_copy(array.at[k], big[n].at[k], sems.at[5 * k + n]))
@@ -658,8 +661,8 @@
         others = [swap(a, "lat", step * i) for i in (1, 2, 3)]
         (a,) = call(band_kernel, near(a, *others), [of((height, 2 * C), bf16)], limit=SMALL)
     beside = swap(a, "lon", 2)
-    a = jnp.stack([m for pair in zip(over([a] * 4), over([beside] * 4)) for m in pair]).reshape((4, 2) + a.shape)
-    got = swap(a, "lon", 1)
+    own = [jnp.stack(over([m] * 4)) for m in (a, beside)]
+    got = [swap(m, "lon", 1) for m in own]
 
     factor = 1.0 / math.sqrt(lax.axis_size("rep") * levels * total_rows * col_count * lax.axis_size("lon"))
 
@@ -667,7 +670,7 @@
     short = [(2, 2, C), (2, 2, C), (2, 3 * C), (2, C), (2, FFN), (2, C)]
     joined = call(
         functools.partial(final_kernel, factor),
-        scalars[:1] + near(a, got),
+        scalars[:1] + near(*own, *got),
         [of(m, f32) for m in wide + short],
         [pltpu.VMEM(m, f32) for m in wide]
         + [pltpu.VMEM((8 * ROWS, 2 * C), bf16), pltpu.SemaphoreType.DMA((10,))],

time: 138 us -> 136 us (0.986); the launches traced: 135 us -> 135 us
  starting transfers between devices: 45.6 us -> 49 us
  waiting for transfers between devices: 43.7 us -> 40.5 us
    ppermute x23 -> x24, starting transfers between devices: 31.8 us -> 35.1 us  [swap(): lax.ppermute(array, axis, [(i, i ^ distance) for i in range(lax.axis_size...]
    ppermute x23 -> x24, waiting for transfers between devices: 37.2 us -> 34 us  [swap(): lax.ppermute(array, axis, [(i, i ^ distance) for i in range(lax.axis_size...]
  transfers between devices with their start and end apart: 29 -> 30, of which waited for: 16 -> 15; matrix products, arithmetic and copies ran while one was open for 2% -> 3% of each run, Pallas kernels for 9% -> 9%
where the time goes in v5:
time: 136 us; the launch traced here: 135 us
  starting transfers between devices  49 us (36%)
  waiting for transfers between devices  40.5 us (30%)
  Pallas kernels  37.3 us (27%)
  local copies, waits for them, and re-layouts  7.21 us (5%)
    pallas_call x10, Pallas kernels, call(): pl.pallas_call(wrapped, grid=(1,), in_specs=specs, out_specs=out_specs, o...  37.3 us
    ppermute x24, starting transfers between devices, swap(): lax.ppermute(array, axis, [(i, i ^ distance) for i in range(lax.axis_size...  35.1 us
    ppermute x24, waiting for transfers between devices, swap(): lax.ppermute(array, axis, [(i, i ^ distance) for i in range(lax.axis_size...  34 us
    ppermute x2, starting transfers between devices, send_pieces(): lax.ppermute(pieces[1], 'lat', rows)  10.5 us
    ppermute x2, waiting for transfers between devices, send_pieces(): lax.ppermute(pieces[1], 'lat', rows)  3.98 us
    reshape x2, local copies, waits for them, and re-layouts, body(): m.reshape(row_count, col_count, levels, C).transpose(2, 0, 1, 3)[None]  3.12 us
  transfers between devices with their start and end apart: 30, of which 15 were waited for; matrix products, arithmetic and copies ran while one was open for 3% of the time, Pallas kernels for 9%

profile of v5, /device:TPU:1, one launch (start us, length us, event | category | flops | bytes accessed | tf_op | source)
XLA Modules:
  0.0 135.3 jit_solution(10656293485829743466)
XLA Ops:
  0.6 1.6 %reshape.38.refs_2_.refs_4_ = bf16[144,192]{1,0:T(8,128)(2,1)} reshape(bf16[6,12,2,192]{3,2,1,0:T(2,128)(2,1)} %bitcast.42) | data formatting | bytes 110592 | tf_op jit(solution)/shard_map/reshape | solution.py:593
  2.2 1.6 %reshape.39.refs_3_ = bf16[144,192]{1,0:T(8,128)(2,1)} reshape(bf16[6,12,2,192]{3,2,1,0:T(2,128)(2,1)} %bitcast.43) | data formatting | bytes 110592 | tf_op jit(solution)/shard_map/reshape | solution.py:594
  3.8 8.8 %shard_map.300 = (bf16[144,192]{1,0:T(8,128)(2,1)}, bf16[256,192]{1,0:T(8,128)(2,1)}, bf16[256,192]{1,0:T(8,128)(2,1)}, bf16[6,144,256]{2,1,0:T(8,128)(2,1)}, bf...) custom-call(s32[2,1,16]{2,1,0:T(1,128)} %refs_0_.5, ...), custom_call_target="tpu_custom_call" | custom-call | flops 1000000000 | bytes 8403968 | tf_op jit(solution)/shard_map/pallas_call | solution.py:556
  12.6 8.9 %collective-permute-start = (bf16[96,192]{1,0:T(8,128)(2,1)}, bf16[96,192]{1,0:T(8,128)(2,1)}, u32[]{:S(2)}, u32[]{:S(2)}) collective-permute-start(bf16[96,192]{1,0:T(8,128)(2,1)} %get-tuple-element.51), channel_id=1, source_target_pairs={{0,240},{16,0},{32,16},{48,32},{64,48},{80,64},{96,80},{112,96},{1... | collective-permute-start | bytes 110600 | tf_op jit(solution)/shard_map/ppermute | solution.py:576
  21.5 1.0 collective-permute-start.1
  22.5 1.4 %collective-permute-start.2 = (bf16[96,192]{1,0:T(8,128)(2,1)}, bf16[96,192]{1,0:T(8,128)(2,1)}, u32[]{:S(2)}, u32[]{:S(2)}) collective-permute-start(bf16[96,192]{1,0:T(8,128)(2,1)} %get-tuple-element.53), channel_id=1, source_target_pairs={{0,252},{4,240},{8,244},{12,248},{16,12},{20,0},{24,4},{28,8},{32,... | collective-permute-start | bytes 110600 | tf_op jit(solution)/shard_map/ppermute | solution.py:578
  23.9 5.0 %shard_map.301.refs_14_ = f32[144,1536]{1,0:T(8,128)} custom-call(s32[2,1,16]{2,1,0:T(1,128)} %refs_0_.5, s32[96]{0:T(128)} %refs_1_.3, f32[2,6,16,3312]{3,2,1,0:T(8,128)} %bitcast.34, bf16[256,1536]{1,0:T(8,128)(2,1)} %constant.17.clone.refs_17_.refs_3_.refs_16_.refs_21_, f32[144,192]{1,0:T(8,128)} %constant.15.clone.refs_18_.refs_4_.refs_17_.refs_22_, ...), custom_call_target="tpu_custom_call" | custom-call | flops 1000000000 | bytes 4473344 | tf_op jit(solution)/shard_map/pallas_call | solution.py:556
  28.9 0.0 collective-permute-done.refs_1_
  28.9 0.0 collective-permute-done.1.refs_2_
  28.9 9.2 %shard_map.302 = (bf16[8,160,384]{2,1,0:T(8,128)(2,1)}, bf16[96,192]{1,0:T(8,128)(2,1)}, bf16[96,192]{1,0:T(8,128)(2,1)}, bf16[96,192]{1,0:T(8,128)(2,1)}, bf16[96,192]{1,0:T(8,128)(2,1)}) custom-call(bf16[96,192]{1,0:T(8,128)(2,1)} %get-tuple-element.50.refs_0_, bf16[96,192]{1,0:T(8,128)(2,1)} %collective-permute-done.refs_1_, ...), custom_call_target="tpu_custom_call" | custom-call | flops 1000000000 | bytes 6876672 | tf_op jit(solution)/shard_map/pallas_call | solution.py:556
  38.1 1.6 %collective-permute-start.3 = (bf16[96,192]{1,0:T(8,128)(2,1)}, bf16[96,192]{1,0:T(8,128)(2,1)}, u32[]{:S(2)}, u32[]{:S(2)}) collective-permute-start(bf16[96,192]{1,0:T(8,128)(2,1)} %get-tuple-element.55), channel_id=1, source_target_pairs={{0,16},{16,32},{32,48},{48,64},{64,80},{80,96},{96,112},{112,128},... | collective-permute-start | bytes 110600 | tf_op jit(solution)/shard_map/ppermute | solution.py:576
  39.7 1.0 collective-permute-start.4
  40.7 0.0 collective-permute-start.5
  40.7 1.0 collective-permute-start.7
  41.7 4.0 %collective-permute-done.3.refs_1_ = bf16[96,192]{1,0:T(8,128)(2,1)} collective-permute-done((bf16[96,192]{1,0:T(8,128)(2,1)}, bf16[96,192]{1,0:T(8,128)(2,1)}, u32[]{:S(2)}, u32[]{:S(2)}) %collective-permute-start.3) | collective-permute-done | bytes 36896 | tf_op jit(solution)/shard_map/ppermute | solution.py:576
  45.7 0.0 collective-permute-done.4.refs_2_
  45.7 2.5 %collective-permute-done.5.refs_3_ = bf16[96,192]{1,0:T(8,128)(2,1)} collective-permute-done((bf16[96,192]{1,0:T(8,128)(2,1)}, bf16[96,192]{1,0:T(8,128)(2,1)}, u32[]{:S(2)}, u32[]{:S(2)}) %collective-permute-start.5) | collective-permute-done | bytes 36896 | tf_op jit(solution)/shard_map/ppermute | solution.py:578
  48.1 7.1 %shard_map.303 = (bf16[144,192]{1,0:T(8,128)(2,1)}, bf16[144,192]{1,0:T(8,128)(2,1)}, bf16[8,160,384]{2,1,0:T(8,128)(2,1)}) custom-call(bf16[96,192]{1,0:T(8,128)(2,1)} %get-tuple-element.54.refs_0_, bf16[96,192]{1,0:T(8,128)(2,1)} %collective-permute-done.3.refs_1_, bf16[96,192]{1,0:T(8,128)(2,1)} %collective-permute-done.4.refs_2_, ...), custom_call_target="tpu_custom_call" | custom-call | flops 1000000000 | bytes 6892032 | tf_op jit(solution)/shard_map/pallas_call | solution.py:556
  55.2 0.1 collective-permute-start.6
  55.4 2.9 %collective-permute-done.6.refs_2_ = bf16[8,160,384]{2,1,0:T(8,128)(2,1)} collective-permute-done((bf16[8,160,384]{2,1,0:T(8,128)(2,1)}, bf16[8,160,384]{2,1,0:T(8,128)(2,1)}, u32[]{:S(2)}, u32[]{:S(2)}) %collective-permute-start.6) | collective-permute-done | bytes 983072 | tf_op jit(solution)/shard_map/ppermute | solution.py:583
  58.2 2.5 %shard_map.304 = (bf16[1,160,384]{2,1,0:T(8,128)(2,1)}, bf16[1,160,384]{2,1,0:T(8,128)(2,1)}, bf16[1,160,384]{2,1,0:T(8,128)(2,1)}, bf16[1,160,384]{2,1,0:T(8,12...) custom-call(bf16[8,160,384]{2,1,0:T(8,128)(2,1)} %get-tuple-element., ...), custom_call_target="tpu_custom_call" | custom-call | flops 1000000000 | bytes 4915200 | tf_op jit(solution)/shard_map/pallas_call | solution.py:556
  60.7 1.4 %collective-permute-start.11 = (bf16[1,160,384]{2,1,0:T(8,128)(2,1)}, bf16[1,160,384]{2,1,0:T(8,128)(2,1)S(1)}, u32[]{:S(2)}, u32[]{:S(2)}) collective-permute-start(bf16[1,160,384]{2,1,0:T(8,128)(2,1)} %get-tuple-element.73), channel_id=1, source_target_pairs={{0,1},{1,0},{2,3},{3,2},{4,5},{5,4},{6,7},{7,6},{8,9},{9,8},{10,11... | collective-permute-start | bytes 368648 | tf_op jit(solution)/shard_map/ppermute | solution.py:583
  62.1 2.6 %collective-permute-start.12 = (bf16[1,160,384]{2,1,0:T(8,128)(2,1)}, bf16[1,160,384]{2,1,0:T(8,128)(2,1)S(1)}, u32[]{:S(2)}, u32[]{:S(2)}) collective-permute-start(bf16[1,160,384]{2,1,0:T(8,128)(2,1)} %get-tuple-element.74), channel_id=1, source_target_pairs={{0,2},{1,3},{2,0},{3,1},{4,6},{5,7},{6,4},{7,5},{8,10},{9,11},{10,... | collective-permute-start | bytes 368648 | tf_op jit(solution)/shard_map/ppermute | solution.py:583
  64.7 0.0 collective-permute-start.13
  64.7 0.0 collective-permute-start.8
  64.7 3.8 %collective-permute-start.9 = (bf16[1,160,384]{2,1,0:T(8,128)(2,1)}, bf16[1,160,384]{2,1,0:T(8,128)(2,1)S(1)}, u32[]{:S(2)}, u32[]{:S(2)}) collective-permute-start(bf16[1,160,384]{2,1,0:T(8,128)(2,1)} %get-tuple-element.70), channel_id=1, source_target_pairs={{0,2},{1,3},{2,0},{3,1},{4,6},{5,7},{6,4},{7,5},{8,10},{9,11},{10,... | collective-permute-start | bytes 368648 | tf_op jit(solution)/shard_map/ppermute | solution.py:583
  68.6 2.3 %collective-permute-done.12.refs_2_ = bf16[1,160,384]{2,1,0:T(8,128)(2,1)S(1)} collective-permute-done((bf16[1,160,384]{2,1,0:T(8,128)(2,1)}, bf16[1,160,384]{2,1,0:T(8,128)(2,1)S(1)}, u32[]{:S(2)}, u32[]{:S(2)}) %collective-permute-start.12) | collective-permute-done | bytes 122912 | tf_op jit(solution)/shard_map/ppermute | solution.py:583
  70.9 2.5 %collective-permute-done.13.refs_3_ = bf16[1,160,384]{2,1,0:T(8,128)(2,1)S(1)} collective-permute-done((bf16[1,160,384]{2,1,0:T(8,128)(2,1)}, bf16[1,160,384]{2,1,0:T(8,128)(2,1)S(1)}, u32[]{:S(2)}, u32[]{:S(2)}) %collective-permute-start.13) | collective-permute-done | bytes 122912 | tf_op jit(solution)/shard_map/ppermute | solution.py:583
  73.4 0.9 copy-done.2
  74.3 0.1 shard_map.305
  74.4 0.4 collective-permute-start.14
  74.8 1.4 %collective-permute-done.9.refs_2_ = bf16[1,160,384]{2,1,0:T(8,128)(2,1)S(1)} collective-permute-done((bf16[1,160,384]{2,1,0:T(8,128)(2,1)}, bf16[1,160,384]{2,1,0:T(8,128)(2,1)S(1)}, u32[]{:S(2)}, u32[]{:S(2)}) %collective-permute-start.9) | collective-permute-done | bytes 122912 | tf_op jit(solution)/shard_map/ppermute | solution.py:583
  76.2 2.5 %collective-permute-done.10.refs_3_ = bf16[1,160,384]{2,1,0:T(8,128)(2,1)S(1)} collective-permute-done((bf16[1,160,384]{2,1,0:T(8,128)(2,1)}, bf16[1,160,384]{2,1,0:T(8,128)(2,1)S(1)}, u32[]{:S(2)}, u32[]{:S(2)}) %collective-permute-start.10) | collective-permute-done | bytes 122912 | tf_op jit(solution)/shard_map/ppermute | solution.py:583
  78.7 0.0 collective-permute-done.14.refs_4_
  78.7 0.1 shard_map.306
  78.8 0.1 collective-permute-start.17
  78.9 0.1 collective-permute-start.16
  79.0 4.0 %collective-permute-start.15 = (bf16[160,384]{1,0:T(8,128)(2,1)S(1)}, bf16[160,384]{1,0:T(8,128)(2,1)S(1)}, u32[]{:S(2)}, u32[]{:S(2)}) collective-permute-start(bf16[160,384]{1,0:T(8,128)(2,1)S(1)} %bitcast.28), channel_id=1, source_target_pairs={{0,16},{16,0},{32,48},{48,32},{64,80},{80,64},{96,112},{112,96},{1... | collective-permute-start | bytes 368648 | tf_op jit(solution)/shard_map/ppermute | solution.py:583
  83.0 2.1 %collective-permute-done.17.refs_3_ = bf16[160,384]{1,0:T(8,128)(2,1)S(1)} collective-permute-done((bf16[160,384]{1,0:T(8,128)(2,1)S(1)}, bf16[160,384]{1,0:T(8,128)(2,1)S(1)}, u32[]{:S(2)}, u32[]{:S(2)}) %collective-permute-start.17) | collective-permute-done | bytes 122912 | tf_op jit(solution)/shard_map/ppermute | solution.py:583
  85.1 1.2 collective-permute-done.15.refs_1_
  86.3 0.1 shard_map.307.refs_0_
  86.4 0.1 collective-permute-start.20
  86.5 2.3 %collective-permute-start.19 = (bf16[192,384]{1,0:T(8,128)(2,1)S(1)}, bf16[192,384]{1,0:T(8,128)(2,1)S(1)}, u32[]{:S(2)}, u32[]{:S(2)}) collective-permute-start(bf16[192,384]{1,0:T(8,128)(2,1)S(1)} %shard_map.307.refs_0_), channel_id=1, source_target_pairs={{0,128},{16,144},{32,160},{48,176},{64,192},{80,208},{96,224},{112... | collective-permute-start | bytes 442376 | tf_op jit(solution)/shard_map/ppermute | solution.py:583
  88.8 3.3 %collective-permute-start.18 = (bf16[192,384]{1,0:T(8,128)(2,1)S(1)}, bf16[192,384]{1,0:T(8,128)(2,1)S(1)}, u32[]{:S(2)}, u32[]{:S(2)}) collective-permute-start(bf16[192,384]{1,0:T(8,128)(2,1)S(1)} %shard_map.307.refs_0_), channel_id=1, source_target_pairs={{0,64},{16,80},{32,96},{48,112},{64,0},{80,16},{96,32},{112,48},{1... | collective-permute-start | bytes 442376 | tf_op jit(solution)/shard_map/ppermute | solution.py:583
  92.1 0.5 collective-permute-done.20.refs_3_
  92.7 2.7 %collective-permute-done.19.refs_2_ = bf16[192,384]{1,0:T(8,128)(2,1)S(1)} collective-permute-done((bf16[192,384]{1,0:T(8,128)(2,1)S(1)}, bf16[192,384]{1,0:T(8,128)(2,1)S(1)}, u32[]{:S(2)}, u32[]{:S(2)}) %collective-permute-start.19) | collective-permute-done | bytes 147488 | tf_op jit(solution)/shard_map/ppermute | solution.py:583
  95.4 5.9 %collective-permute-done.18.refs_1_ = bf16[192,384]{1,0:T(8,128)(2,1)S(1)} collective-permute-done((bf16[192,384]{1,0:T(8,128)(2,1)S(1)}, bf16[192,384]{1,0:T(8,128)(2,1)S(1)}, u32[]{:S(2)}, u32[]{:S(2)}) %collective-permute-start.18) | collective-permute-done | bytes 147488 | tf_op jit(solution)/shard_map/ppermute | solution.py:583
  101.3 0.1 shard_map.308
  101.4 0.1 collective-permute-start.24
  101.5 3.4 %collective-permute-start.23 = (bf16[288,384]{1,0:T(8,128)(2,1)S(1)}, bf16[288,384]{1,0:T(8,128)(2,1)S(1)}, u32[]{:S(2)}, u32[]{:S(2)}) collective-permute-start(bf16[288,384]{1,0:T(8,128)(2,1)S(1)} %shard_map.308), channel_id=1, source_target_pairs={{0,3},{1,2},{2,1},{3,0},{4,7},{5,6},{6,5},{7,4},{8,11},{9,10},{10,... | collective-permute-start | bytes 663560 | tf_op jit(solution)/shard_map/ppermute | solution.py:583
  104.8 0.0 collective-permute-start.22
  104.8 0.7 collective-permute-start.21
  105.5 0.7 collective-permute-done.24
  106.3 3.3 %collective-permute-start.27 = (bf16[288,384]{1,0:T(8,128)(2,1)S(1)}, bf16[288,384]{1,0:T(8,128)(2,1)S(1)}, u32[]{:S(2)}, u32[]{:S(2)}) collective-permute-start(bf16[288,384]{1,0:T(8,128)(2,1)S(1)} %collective-permute-done.24), channel_id=1, source_target_pairs={{0,3},{1,2},{2,1},{3,0},{4,7},{5,6},{6,5},{7,4},{8,11},{9,10},{10,... | collective-permute-start | bytes 663560 | tf_op jit(solution)/shard_map/ppermute | solution.py:583
  109.5 7.0 %collective-permute-done.23 = bf16[288,384]{1,0:T(8,128)(2,1)S(1)} collective-permute-done((bf16[288,384]{1,0:T(8,128)(2,1)S(1)}, bf16[288,384]{1,0:T(8,128)(2,1)S(1)}, u32[]{:S(2)}, u32[]{:S(2)}) %collective-permute-start.23) | collective-permute-done | bytes 221216 | tf_op jit(solution)/shard_map/ppermute | solution.py:583
  116.5 0.1 pad_maximum_fusion.refs_1_
  116.7 0.0 copy-start
  116.7 4.9 %collective-permute-start.28 = (bf16[4,288,384]{2,1,0:T(8,128)(2,1)S(1)}, bf16[4,288,384]{2,1,0:T(8,128)(2,1)S(1)}, u32[]{:S(2)}, u32[]{:S(2)}) collective-permute-start(bf16[4,288,384]{2,1,0:T(8,128)(2,1)S(1)} %pad_maximum_fusion.refs_1_), channel_id=1, source_target_pairs={{0,4},{4,0},{8,12},{12,8},{1,5},{5,1},{9,13},{13,9},{2,6},{6,2},{1... | collective-permute-start | bytes 2654216 | tf_op jit(solution)/shard_map/ppermute | solution.py:583
  121.6 2.2 %collective-permute-done.27 = bf16[288,384]{1,0:T(8,128)(2,1)S(1)} collective-permute-done((bf16[288,384]{1,0:T(8,128)(2,1)S(1)}, bf16[288,384]{1,0:T(8,128)(2,1)S(1)}, u32[]{:S(2)}, u32[]{:S(2)}) %collective-permute-start.27) | collective-permute-done | bytes 221216 | tf_op jit(solution)/shard_map/ppermute | solution.py:583
  123.8 0.1 pad_maximum_fusion.1.refs_2_
  123.9 3.6 %collective-permute-start.29 = (bf16[4,288,384]{2,1,0:T(8,128)(2,1)S(1)}, bf16[4,288,384]{2,1,0:T(8,128)(2,1)S(1)}, u32[]{:S(2)}, u32[]{:S(2)}) collective-permute-start(bf16[4,288,384]{2,1,0:T(8,128)(2,1)S(1)} %pad_maximum_fusion.1.refs_2_), channel_id=1, source_target_pairs={{0,4},{4,0},{8,12},{12,8},{1,5},{5,1},{9,13},{13,9},{2,6},{6,2},{1... | collective-permute-start | bytes 2654216 | tf_op jit(solution)/shard_map/ppermute | solution.py:583
  127.5 1.6 %reshape.40 = bf16[6,12,2,192]{3,2,1,0:T(2,128)(2,1)} reshape(bf16[144,192]{1,0:T(8,128)(2,1)} %get-tuple-element.64) | data formatting | bytes 110592 | tf_op jit(solution)/shard_map/reshape | solution.py:682
  129.0 1.6 %reshape.41 = bf16[6,12,2,192]{3,2,1,0:T(2,128)(2,1)} reshape(bf16[144,192]{1,0:T(8,128)(2,1)} %get-tuple-element.65) | data formatting | bytes 110592 | tf_op jit(solution)/shard_map/reshape | solution.py:682
  130.6 4.5 %shard_map.309 = (f32[2,192,576]{2,1,0:T(8,128)}, f32[2,192,192]{2,1,0:T(8,128)}, f32[2,192,768]{2,1,0:T(8,128)}, f32[2,192,768]{2,1,0:T(8,128)}, f32[2,6,16,331...) custom-call(s32[2,1,16]{2,1,0:T(1,128)S(1)} %copy-done, ...), custom_call_target="tpu_custom_call" | custom-call | flops 1000000000 | bytes 9641600 | tf_op jit(solution)/shard_map/pallas_call | solution.py:556
  (18 shorter events, 0.0 us)
Async XLA Ops:
  12.6 16.3 %collective-permute-start = (bf16[96,192]{1,0:T(8,128)(2,1)}, bf16[96,192]{1,0:T(8,128)(2,1)}, u32[]{:S(2)}, u32[]{:S(2)}) collective-permute-start(bf16[96,192]{1,0:T(8,128)(2,1)} %get-tuple-element.51), channel_id=1, source_target_pairs={{0,240},{16,0},{32,16},{48,32},{64,48},{80,64},{96,80},{112,96},{1... | collective-permute-start | bytes 110600 | tf_op jit(solution)/shard_map/ppermute | solution.py:576
  21.5 7.4 %collective-permute-start.1 = (bf16[96,192]{1,0:T(8,128)(2,1)}, bf16[96,192]{1,0:T(8,128)(2,1)}, u32[]{:S(2)}, u32[]{:S(2)}) collective-permute-start(bf16[96,192]{1,0:T(8,128)(2,1)} %get-tuple-element.52), channel_id=1, source_target_pairs={{0,12},{4,0},{8,4},{12,8},{1,13},{5,1},{9,5},{13,9},{2,14},{6,2},{... | collective-permute-start | bytes 110600 | tf_op jit(solution)/shard_map/ppermute | solution.py:577
  22.5 6.4 %collective-permute-start.2 = (bf16[96,192]{1,0:T(8,128)(2,1)}, bf16[96,192]{1,0:T(8,128)(2,1)}, u32[]{:S(2)}, u32[]{:S(2)}) collective-permute-start(bf16[96,192]{1,0:T(8,128)(2,1)} %get-tuple-element.53), channel_id=1, source_target_pairs={{0,252},{4,240},{8,244},{12,248},{16,12},{20,0},{24,4},{28,8},{32,... | collective-permute-start | bytes 110600 | tf_op jit(solution)/shard_map/ppermute | solution.py:578
  38.1 7.5 %collective-permute-start.3 = (bf16[96,192]{1,0:T(8,128)(2,1)}, bf16[96,192]{1,0:T(8,128)(2,1)}, u32[]{:S(2)}, u32[]{:S(2)}) collective-permute-start(bf16[96,192]{1,0:T(8,128)(2,1)} %get-tuple-element.55), channel_id=1, source_target_pairs={{0,16},{16,32},{32,48},{48,64},{64,80},{80,96},{96,112},{112,128},... | collective-permute-start | bytes 110600 | tf_op jit(solution)/shard_map/ppermute | solution.py:576
  39.7 5.9 %collective-permute-start.4 = (bf16[96,192]{1,0:T(8,128)(2,1)}, bf16[96,192]{1,0:T(8,128)(2,1)}, u32[]{:S(2)}, u32[]{:S(2)}) collective-permute-start(bf16[96,192]{1,0:T(8,128)(2,1)} %get-tuple-element.56), channel_id=1, source_target_pairs={{0,4},{4,8},{8,12},{12,0},{1,5},{5,9},{9,13},{13,1},{2,6},{6,10},{... | collective-permute-start | bytes 110600 | tf_op jit(solution)/shard_map/ppermute | solution.py:577
  40.7 7.4 %collective-permute-start.5 = (bf16[96,192]{1,0:T(8,128)(2,1)}, bf16[96,192]{1,0:T(8,128)(2,1)}, u32[]{:S(2)}, u32[]{:S(2)}) collective-permute-start(bf16[96,192]{1,0:T(8,128)(2,1)} %get-tuple-element.57), channel_id=1, source_target_pairs={{0,20},{4,24},{8,28},{12,16},{16,36},{20,40},{24,44},{28,32},{32,5... | collective-permute-start | bytes 110600 | tf_op jit(solution)/shard_map/ppermute | solution.py:578
  40.7 14.6 %collective-permute-start.7 = (bf16[8,160,384]{2,1,0:T(8,128)(2,1)}, bf16[8,160,384]{2,1,0:T(8,128)(2,1)}, u32[]{:S(2)}, u32[]{:S(2)}) collective-permute-start(bf16[8,160,384]{2,1,0:T(8,128)(2,1)} %get-tuple-element.67.refs_1_), channel_id=1, source_target_pairs={{0,4},{4,0},{8,12},{12,8},{1,5},{5,1},{9,13},{13,9},{2,6},{6,2},{1... | collective-permute-start | bytes 2949128 | tf_op jit(solution)/shard_map/ppermute | solution.py:583
  55.2 3.0 %collective-permute-start.6 = (bf16[8,160,384]{2,1,0:T(8,128)(2,1)}, bf16[8,160,384]{2,1,0:T(8,128)(2,1)}, u32[]{:S(2)}, u32[]{:S(2)}) collective-permute-start(bf16[8,160,384]{2,1,0:T(8,128)(2,1)} %get-tuple-element.66.refs_0_), channel_id=1, source_target_pairs={{0,4},{4,0},{8,12},{12,8},{1,5},{5,1},{9,13},{13,9},{2,6},{6,2},{1... | collective-permute-start | bytes 2949128 | tf_op jit(solution)/shard_map/ppermute | solution.py:583
  60.7 7.9 %collective-permute-start.11 = (bf16[1,160,384]{2,1,0:T(8,128)(2,1)}, bf16[1,160,384]{2,1,0:T(8,128)(2,1)S(1)}, u32[]{:S(2)}, u32[]{:S(2)}) collective-permute-start(bf16[1,160,384]{2,1,0:T(8,128)(2,1)} %get-tuple-element.73), channel_id=1, source_target_pairs={{0,1},{1,0},{2,3},{3,2},{4,5},{5,4},{6,7},{7,6},{8,9},{9,8},{10,11... | collective-permute-start | bytes 368648 | tf_op jit(solution)/shard_map/ppermute | solution.py:583
  62.1 8.8 %collective-permute-start.12 = (bf16[1,160,384]{2,1,0:T(8,128)(2,1)}, bf16[1,160,384]{2,1,0:T(8,128)(2,1)S(1)}, u32[]{:S(2)}, u32[]{:S(2)}) collective-permute-start(bf16[1,160,384]{2,1,0:T(8,128)(2,1)} %get-tuple-element.74), channel_id=1, source_target_pairs={{0,2},{1,3},{2,0},{3,1},{4,6},{5,7},{6,4},{7,5},{8,10},{9,11},{10,... | collective-permute-start | bytes 368648 | tf_op jit(solution)/shard_map/ppermute | solution.py:583
  64.7 8.7 %collective-permute-start.13 = (bf16[1,160,384]{2,1,0:T(8,128)(2,1)}, bf16[1,160,384]{2,1,0:T(8,128)(2,1)S(1)}, u32[]{:S(2)}, u32[]{:S(2)}) collective-permute-start(bf16[1,160,384]{2,1,0:T(8,128)(2,1)} %get-tuple-element.75), channel_id=1, source_target_pairs={{0,3},{1,2},{2,1},{3,0},{4,7},{5,6},{6,5},{7,4},{8,11},{9,10},{10,... | collective-permute-start | bytes 368648 | tf_op jit(solution)/shard_map/ppermute | solution.py:583
  64.7 10.1 %collective-permute-start.8 = (bf16[1,160,384]{2,1,0:T(8,128)(2,1)}, bf16[1,160,384]{2,1,0:T(8,128)(2,1)S(1)}, u32[]{:S(2)}, u32[]{:S(2)}) collective-permute-start(bf16[1,160,384]{2,1,0:T(8,128)(2,1)} %get-tuple-element.69), channel_id=1, source_target_pairs={{0,1},{1,0},{2,3},{3,2},{4,5},{5,4},{6,7},{7,6},{8,9},{9,8},{10,11... | collective-permute-start | bytes 368648 | tf_op jit(solution)/shard_map/ppermute | solution.py:583
  64.7 11.5 %collective-permute-start.9 = (bf16[1,160,384]{2,1,0:T(8,128)(2,1)}, bf16[1,160,384]{2,1,0:T(8,128)(2,1)S(1)}, u32[]{:S(2)}, u32[]{:S(2)}) collective-permute-start(bf16[1,160,384]{2,1,0:T(8,128)(2,1)} %get-tuple-element.70), channel_id=1, source_target_pairs={{0,2},{1,3},{2,0},{3,1},{4,6},{5,7},{6,4},{7,5},{8,10},{9,11},{10,... | collective-permute-start | bytes 368648 | tf_op jit(solution)/shard_map/ppermute | solution.py:583
  68.6 10.1 %collective-permute-start.10 = (bf16[1,160,384]{2,1,0:T(8,128)(2,1)}, bf16[1,160,384]{2,1,0:T(8,128)(2,1)S(1)}, u32[]{:S(2)}, u32[]{:S(2)}) collective-permute-start(bf16[1,160,384]{2,1,0:T(8,128)(2,1)} %get-tuple-element.71), channel_id=1, source_target_pairs={{0,3},{1,2},{2,1},{3,0},{4,7},{5,6},{6,5},{7,4},{8,11},{9,10},{10,... | collective-permute-start | bytes 368648 | tf_op jit(solution)/shard_map/ppermute | solution.py:583
  73.4 0.9 copy-start.2
  74.3 4.4 %copy-start.1 = (bf16[1,160,384]{2,1,0:T(8,128)(2,1)S(1)}, bf16[1,160,384]{2,1,0:T(8,128)(2,1)}, u32[]{:S(2)}) copy-start(bf16[1,160,384]{2,1,0:T(8,128)(2,1)} %get-tuple-element.68.refs_0_) | copy-start | bytes 368644
  74.4 4.3 %collective-permute-start.14 = (bf16[1,160,384]{2,1,0:T(8,128)(2,1)S(1)}, bf16[1,160,384]{2,1,0:T(8,128)(2,1)S(1)}, u32[]{:S(2)}, u32[]{:S(2)}) collective-permute-start(bf16[1,160,384]{2,1,0:T(8,128)(2,1)S(1)} %shard_map.305), channel_id=1, source_target_pairs={{0,8},{4,12},{8,0},{12,4},{1,9},{5,13},{9,1},{13,5},{2,10},{6,14},... | collective-permute-start | bytes 368648 | tf_op jit(solution)/shard_map/ppermute | solution.py:583
  78.8 6.3 %collective-permute-start.17 = (bf16[160,384]{1,0:T(8,128)(2,1)S(1)}, bf16[160,384]{1,0:T(8,128)(2,1)S(1)}, u32[]{:S(2)}, u32[]{:S(2)}) collective-permute-start(bf16[160,384]{1,0:T(8,128)(2,1)S(1)} %bitcast.26), channel_id=1, source_target_pairs={{0,48},{16,32},{32,16},{48,0},{64,112},{80,96},{96,80},{112,64},{1... | collective-permute-start | bytes 368648 | tf_op jit(solution)/shard_map/ppermute | solution.py:583
  78.9 6.2 %collective-permute-start.16 = (bf16[160,384]{1,0:T(8,128)(2,1)S(1)}, bf16[160,384]{1,0:T(8,128)(2,1)S(1)}, u32[]{:S(2)}, u32[]{:S(2)}) collective-permute-start(bf16[160,384]{1,0:T(8,128)(2,1)S(1)} %bitcast.27), channel_id=1, source_target_pairs={{0,32},{16,48},{32,0},{48,16},{64,96},{80,112},{96,64},{112,80},{1... | collective-permute-start | bytes 368648 | tf_op jit(solution)/shard_map/ppermute | solution.py:583
  79.0 7.3 %collective-permute-start.15 = (bf16[160,384]{1,0:T(8,128)(2,1)S(1)}, bf16[160,384]{1,0:T(8,128)(2,1)S(1)}, u32[]{:S(2)}, u32[]{:S(2)}) collective-permute-start(bf16[160,384]{1,0:T(8,128)(2,1)S(1)} %bitcast.28), channel_id=1, source_target_pairs={{0,16},{16,0},{32,48},{48,32},{64,80},{80,64},{96,112},{112,96},{1... | collective-permute-start | bytes 368648 | tf_op jit(solution)/shard_map/ppermute | solution.py:583
  86.4 6.3 %collective-permute-start.20 = (bf16[192,384]{1,0:T(8,128)(2,1)S(1)}, bf16[192,384]{1,0:T(8,128)(2,1)S(1)}, u32[]{:S(2)}, u32[]{:S(2)}) collective-permute-start(bf16[192,384]{1,0:T(8,128)(2,1)S(1)} %shard_map.307.refs_0_), channel_id=1, source_target_pairs={{0,192},{16,208},{32,224},{48,240},{64,128},{80,144},{96,160},{112... | collective-permute-start | bytes 442376 | tf_op jit(solution)/shard_map/ppermute | solution.py:583
  86.5 8.9 %collective-permute-start.19 = (bf16[192,384]{1,0:T(8,128)(2,1)S(1)}, bf16[192,384]{1,0:T(8,128)(2,1)S(1)}, u32[]{:S(2)}, u32[]{:S(2)}) collective-permute-start(bf16[192,384]{1,0:T(8,128)(2,1)S(1)} %shard_map.307.refs_0_), channel_id=1, source_target_pairs={{0,128},{16,144},{32,160},{48,176},{64,192},{80,208},{96,224},{112... | collective-permute-start | bytes 442376 | tf_op jit(solution)/shard_map/ppermute | solution.py:583
  88.8 12.5 %collective-permute-start.18 = (bf16[192,384]{1,0:T(8,128)(2,1)S(1)}, bf16[192,384]{1,0:T(8,128)(2,1)S(1)}, u32[]{:S(2)}, u32[]{:S(2)}) collective-permute-start(bf16[192,384]{1,0:T(8,128)(2,1)S(1)} %shard_map.307.refs_0_), channel_id=1, source_target_pairs={{0,64},{16,80},{32,96},{48,112},{64,0},{80,16},{96,32},{112,48},{1... | collective-permute-start | bytes 442376 | tf_op jit(solution)/shard_map/ppermute | solution.py:583
  101.4 4.9 %collective-permute-start.24 = (bf16[288,384]{1,0:T(8,128)(2,1)S(1)}, bf16[288,384]{1,0:T(8,128)(2,1)S(1)}, u32[]{:S(2)}, u32[]{:S(2)}) collective-permute-start(bf16[288,384]{1,0:T(8,128)(2,1)S(1)} %shard_map.308), channel_id=1, source_target_pairs={{0,8},{4,12},{8,0},{12,4},{1,9},{5,13},{9,1},{13,5},{2,10},{6,14},... | collective-permute-start | bytes 663560 | tf_op jit(solution)/shard_map/ppermute | solution.py:583
  101.5 15.0 %collective-permute-start.23 = (bf16[288,384]{1,0:T(8,128)(2,1)S(1)}, bf16[288,384]{1,0:T(8,128)(2,1)S(1)}, u32[]{:S(2)}, u32[]{:S(2)}) collective-permute-start(bf16[288,384]{1,0:T(8,128)(2,1)S(1)} %shard_map.308), channel_id=1, source_target_pairs={{0,3},{1,2},{2,1},{3,0},{4,7},{5,6},{6,5},{7,4},{8,11},{9,10},{10,... | collective-permute-start | bytes 663560 | tf_op jit(solution)/shard_map/ppermute | solution.py:583
  104.8 11.7 %collective-permute-start.22 = (bf16[288,384]{1,0:T(8,128)(2,1)S(1)}, bf16[288,384]{1,0:T(8,128)(2,1)S(1)}, u32[]{:S(2)}, u32[]{:S(2)}) collective-permute-start(bf16[288,384]{1,0:T(8,128)(2,1)S(1)} %shard_map.308), channel_id=1, source_target_pairs={{0,2},{1,3},{2,0},{3,1},{4,6},{5,7},{6,4},{7,5},{8,10},{9,11},{10,... | collective-permute-start | bytes 663560 | tf_op jit(solution)/shard_map/ppermute | solution.py:583
  104.8 11.7 %collective-permute-start.21 = (bf16[288,384]{1,0:T(8,128)(2,1)S(1)}, bf16[288,384]{1,0:T(8,128)(2,1)S(1)}, u32[]{:S(2)}, u32[]{:S(2)}) collective-permute-start(bf16[288,384]{1,0:T(8,128)(2,1)S(1)} %shard_map.308), channel_id=1, source_target_pairs={{0,1},{1,0},{2,3},{3,2},{4,5},{5,4},{6,7},{7,6},{8,9},{9,8},{10,11... | collective-permute-start | bytes 663560 | tf_op jit(solution)/shard_map/ppermute | solution.py:583
  106.3 17.5 %collective-permute-start.27 = (bf16[288,384]{1,0:T(8,128)(2,1)S(1)}, bf16[288,384]{1,0:T(8,128)(2,1)S(1)}, u32[]{:S(2)}, u32[]{:S(2)}) collective-permute-start(bf16[288,384]{1,0:T(8,128)(2,1)S(1)} %collective-permute-done.24), channel_id=1, source_target_pairs={{0,3},{1,2},{2,1},{3,0},{4,7},{5,6},{6,5},{7,4},{8,11},{9,10},{10,... | collective-permute-start | bytes 663560 | tf_op jit(solution)/shard_map/ppermute | solution.py:583
  109.5 14.2 %collective-permute-start.26 = (bf16[288,384]{1,0:T(8,128)(2,1)S(1)}, bf16[288,384]{1,0:T(8,128)(2,1)S(1)}, u32[]{:S(2)}, u32[]{:S(2)}) collective-permute-start(bf16[288,384]{1,0:T(8,128)(2,1)S(1)} %collective-permute-done.24), channel_id=1, source_target_pairs={{0,2},{1,3},{2,0},{3,1},{4,6},{5,7},{6,4},{7,5},{8,10},{9,11},{10,... | collective-permute-start | bytes 663560 | tf_op jit(solution)/shard_map/ppermute | solution.py:583
  116.5 7.3 %collective-permute-start.25 = (bf16[288,384]{1,0:T(8,128)(2,1)S(1)}, bf16[288,384]{1,0:T(8,128)(2,1)S(1)}, u32[]{:S(2)}, u32[]{:S(2)}) collective-permute-start(bf16[288,384]{1,0:T(8,128)(2,1)S(1)} %collective-permute-done.24), channel_id=1, source_target_pairs={{0,1},{1,0},{2,3},{3,2},{4,5},{5,4},{6,7},{7,6},{8,9},{9,8},{10,11... | collective-permute-start | bytes 663560 | tf_op jit(solution)/shard_map/ppermute | solution.py:583
  116.7 13.9 %copy-start = (s32[2,1,16]{2,1,0:T(1,128)S(1)}, s32[2,1,16]{2,1,0:T(1,128)}, u32[]{:S(2)}) copy-start(s32[2,1,16]{2,1,0:T(1,128)} %refs_0_.5) | copy-start | bytes 388
  116.7 13.9 %collective-permute-start.28 = (bf16[4,288,384]{2,1,0:T(8,128)(2,1)S(1)}, bf16[4,288,384]{2,1,0:T(8,128)(2,1)S(1)}, u32[]{:S(2)}, u32[]{:S(2)}) collective-permute-start(bf16[4,288,384]{2,1,0:T(8,128)(2,1)S(1)} %pad_maximum_fusion.refs_1_), channel_id=1, source_target_pairs={{0,4},{4,0},{8,12},{12,8},{1,5},{5,1},{9,13},{13,9},{2,6},{6,2},{1... | collective-permute-start | bytes 2654216 | tf_op jit(solution)/shard_map/ppermute | solution.py:583
  123.9 6.7 %collective-permute-start.29 = (bf16[4,288,384]{2,1,0:T(8,128)(2,1)S(1)}, bf16[4,288,384]{2,1,0:T(8,128)(2,1)S(1)}, u32[]{:S(2)}, u32[]{:S(2)}) collective-permute-start(bf16[4,288,384]{2,1,0:T(8,128)(2,1)S(1)} %pad_maximum_fusion.1.refs_2_), channel_id=1, source_target_pairs={{0,4},{4,0},{8,12},{12,8},{1,5},{5,1},{9,13},{13,9},{2,6},{6,2},{1... | collective-permute-start | bytes 2654216 | tf_op jit(solution)/shard_map/ppermute | solution.py:583
